TPU v7x, 256 devices: a whole 4x4x8 slice. The times are simulated.
256 devices in a mesh: slab: 16 (over z, y_hi), pencil: 16 (over x, y_lo, core).
Axes of the slice: x: 4, y: 4 (y_hi: 2, y_lo: 2; y = y_hi * 2 + y_lo), z: 8, core: 2. Of those that a mesh axis runs over, the one named last changes fastest.
Arguments:
- layer_input: bfloat16 [32, 64, 256, 256], P(None, 'slab', 'pencil'), may hold values from -6 to 6
- pre_activation: bfloat16 [32, 64, 256, 256], P(None, 'slab', 'pencil'), may hold values from -6 to 6
- coefficient: bfloat16 [64, 256, 256], P('slab', 'pencil'), may hold values from 0.5 to 2.5
- source: bfloat16 [64, 256, 256], P('slab', 'pencil'), may hold values from -6 to 6
- projection: float32 [32], replicated, may hold values from -1 to 1
- pointwise: bfloat16 [32, 32], replicated, may hold values from -1 to 1
- spectral_weight: bfloat16 [2, 32, 32, 32, 512], P(None, 'slab', 'pencil'), may hold values from -12 to 12
Outputs:
- input_grad: bfloat16 [32, 64, 256, 256], P(None, 'slab', 'pencil')
- weight_grad: bfloat16 [2, 32, 32, 32, 512], P(None, 'slab', 'pencil')
All inputs are finite; a program needn't handle non-finite values.
Results may differ from a plain program's by a relative error of at most 0.0013.
Values sent between devices are 32-bit elements; how exact they have to be, the bound alone decides.
No kernel may reach another device: no remote copies, remote signals or barrier semaphores. Data moves between devices by JAX's collectives and lax.ppermute only.
A program may use at most 128 MiB of HBM per device.

v0:
```python
import math

import jax
import jax.numpy as jnp
from jax import lax
from jax.sharding import PartitionSpec as P

highest = lax.Precision.HIGHEST


def padded_2(array, sides, width):
    for axis, dim in sides:
        size, length = (lax.axis_size(axis), array.shape[dim])
        up = [(i, (i + 1) % size) for i in range(size)]
        down = [(j, i) for i, j in up]
        last = lax.slice_in_dim(array, length - width, length, axis=dim)
        initial = lax.slice_in_dim(array, 0, width, axis=dim)
        before = lax.ppermute(last, axis, up)
        after = lax.ppermute(initial, axis, down)
        array = jnp.concatenate([before, array, after], axis=dim)
    return array


def exact_gelu(inputs):
    return jax.nn.gelu(inputs, approximate=False)


def mode_values(row_count, modes_half):
    positions = jnp.arange(row_count, dtype=jnp.int32)
    return jnp.where(positions < modes_half, positions, positions - 2 * modes_half)


def phase_tables(wave_numbers, cell_index, length):
    phase_steps = jnp.mod(wave_numbers[:, None] * cell_index[None, :], length)
    angles = phase_steps.astype(jnp.float32) * (2.0 * math.pi / length)
    return (jnp.cos(angles), jnp.sin(angles))


def rotate(cosine_table, sine_table, values, pattern, modes_half, forward):
    cos_part = jnp.einsum(pattern, cosine_table, values, precision=highest)
    sin_part = jnp.einsum(pattern, sine_table, values, precision=highest)
    if forward:
        real_part = cos_part[..., :modes_half] + sin_part[..., modes_half:]
        imag_part = cos_part[..., modes_half:] - sin_part[..., :modes_half]
    else:
        real_part = cos_part[..., :modes_half] - sin_part[..., modes_half:]
        imag_part = cos_part[..., modes_half:] + sin_part[..., :modes_half]
    return jnp.concatenate([real_part, imag_part], axis=-1)


def smooth_plane(padded):
    along_x = 0.5 * padded[:-2] + padded[1:-1] + 0.5 * padded[2:]
    along_y = 0.5 * along_x[:, :-2] + along_x[:, 1:-1] + 0.5 * along_x[:, 2:]
    return 0.5 * jnp.roll(along_y, 1, axis=2) + along_y + 0.5 * jnp.roll(along_y, -1, axis=2)


def operate(center, smoothed, coef_values):
    return 16.0 / 3.0 * center - 2.0 / 3.0 * smoothed - coef_values * center


def shards(
    layer_input, pre_activation, coefficient, source, projection, pointwise, spectral_weight
):
    channels = layer_input.shape[0]
    slab_cells = layer_input.shape[1]
    pencil_cells = layer_input.shape[2]
    depth_cells = layer_input.shape[3]
    slab_count = lax.axis_size("slab")
    pencil_count = lax.axis_size("pencil")
    full_x = slab_cells * slab_count
    full_y = pencil_cells * pencil_count
    local_kx = spectral_weight.shape[1]
    local_ky = spectral_weight.shape[2]
    modes_x = local_kx * slab_count // 2
    modes_y = local_ky * pencil_count // 2
    modes_z = spectral_weight.shape[4] // channels
    pre_values = pre_activation.astype(jnp.float32)
    activated, pullback = jax.vjp(exact_gelu, pre_values)
    field = jnp.einsum("c,cxyz->xyz", projection, activated, precision=highest)
    coef_values = coefficient.astype(jnp.float32)
    source_values = source.astype(jnp.float32)
    padded_field = padded_2(field, (("slab", 0), ("pencil", 1)), 1)
    residual = operate(field, smooth_plane(padded_field), coef_values) - source_values
    padded_residual = padded_2(residual, (("slab", 0), ("pencil", 1)), 1)
    field_grad = operate(residual, smooth_plane(padded_residual), coef_values)
    act_grad = pullback(projection[:, None, None, None] * field_grad[None])[0]
    depth_index = jnp.arange(depth_cells, dtype=jnp.int32)
    cos_z, sin_z = phase_tables(jnp.arange(modes_z, dtype=jnp.int32), depth_index, depth_cells)
    depth_table = jnp.concatenate([cos_z, -sin_z], axis=0)

    def to_modes_z(values):
        flat = jnp.dot(values.reshape(-1, depth_cells), depth_table.T, precision=highest)
        return flat.reshape(channels, slab_cells, pencil_cells, 2 * modes_z)

    spectra_z = jnp.concatenate(
        [to_modes_z(layer_input.astype(jnp.float32)), to_modes_z(act_grad)], axis=0
    )
    x_cells = lax.axis_index("slab") * slab_cells + jnp.arange(slab_cells, dtype=jnp.int32)
    y_cells = lax.axis_index("pencil") * pencil_cells + jnp.arange(pencil_cells, dtype=jnp.int32)
    cosine_table, sine_table = phase_tables(
        mode_values(lax.axis_size("slab") * local_kx, modes_x), x_cells, full_x
    )
    partial_x = lax.psum_scatter(
        rotate(cosine_table, sine_table, spectra_z, "kx,cxym->kcym", modes_z, True),
        "slab",
        scatter_dimension=0,
        tiled=True,
    )
    cosine_table, sine_table = phase_tables(
        mode_values(lax.axis_size("pencil") * local_ky, modes_y), y_cells, full_y
    )
    spectra = jnp.transpose(
        lax.psum_scatter(
            rotate(cosine_table, sine_table, partial_x, "ky,acym->kacm", modes_z, True),
            "pencil",
            scatter_dimension=0,
            tiled=True,
        ),
        (1, 0, 2, 3),
    )
    total_cells = float(full_x * full_y * depth_cells)
    scale = jnp.where(jnp.arange(modes_z) == 0, 1.0, 2.0).astype(jnp.float32) / total_cells
    input_real = spectra[:, :, :channels, :modes_z]
    input_imag = spectra[:, :, :channels, modes_z:]
    grad_real = jnp.swapaxes(spectra[:, :, channels:, :modes_z], 2, 3)
    grad_imag = jnp.swapaxes(spectra[:, :, channels:, modes_z:], 2, 3)
    scale_column = scale[:, None]
    outer_real = scale_column * (
        input_real[..., None] * grad_real[:, :, None]
        + input_imag[..., None] * grad_imag[:, :, None]
    )
    outer_imag = scale_column * (
        input_real[..., None] * grad_imag[:, :, None]
        - input_imag[..., None] * grad_real[:, :, None]
    )
    weight_grad = (
        jnp.stack([outer_real, outer_imag])
        .reshape(2, local_kx, local_ky, channels, modes_z * channels)
        .astype(jnp.bfloat16)
    )
    weights = spectral_weight.astype(jnp.float32).reshape(
        2, local_kx, local_ky, channels, modes_z, channels
    )
    back_real = jnp.sum(
        weights[0] * grad_real[:, :, None] + weights[1] * grad_imag[:, :, None], axis=-1
    )
    back_imag = jnp.sum(
        weights[0] * grad_imag[:, :, None] - weights[1] * grad_real[:, :, None], axis=-1
    )
    scaled = jnp.concatenate([back_real * scale, back_imag * scale], axis=-1)
    shard_part = lax.all_gather(scaled, "pencil", axis=1, tiled=True)
    cosine_table, sine_table = phase_tables(
        mode_values(shard_part.shape[1], modes_y), y_cells, full_y
    )
    spread_first = rotate(cosine_table, sine_table, shard_part, "ky,akcm->aycm", modes_z, False)
    shard_part = lax.all_gather(spread_first, "slab", axis=0, tiled=True)
    cosine_table, sine_table = phase_tables(
        mode_values(shard_part.shape[0], modes_x), x_cells, full_x
    )
    spatial = rotate(cosine_table, sine_table, shard_part, "kx,kycm->xycm", modes_z, False)
    ordered = jnp.transpose(spatial, (2, 0, 1, 3)).reshape(-1, 2 * modes_z)
    spectral_part = jnp.dot(ordered, depth_table, precision=highest).reshape(
        channels, slab_cells, pencil_cells, depth_cells
    )
    local_part = jnp.dot(
        pointwise.astype(jnp.float32), act_grad.reshape(channels, -1), precision=highest
    )
    local_part = local_part.reshape(channels, slab_cells, pencil_cells, depth_cells)
    input_grad = (spectral_part + local_part).astype(jnp.bfloat16)
    return (input_grad, weight_grad)


def solution(mesh):
    return jax.shard_map(
        shards,
        mesh=mesh,
        in_specs=(
            P(None, "slab", "pencil", None),
            P(None, "slab", "pencil", None),
            P("slab", "pencil", None),
            P("slab", "pencil", None),
            P(),
            P(),
            P(None, "slab", "pencil", None, None),
        ),
        out_specs=(P(None, "slab", "pencil", None), P(None, "slab", "pencil", None, None)),
        check_vma=False,
    )
```

profile of v0, /device:TPU:1, one launch (start us, length us, event | category | flops | bytes accessed | tf_op | source)
XLA Modules:
  0.0 587.9 jit_solution(5316565974104994735)
XLA Ops:
  7.2 6.6 %fusion.4 = (f32[32,4,16,256]{3,2,1,0:T(8,128)S(1)}, f32[32,4,16,256]{3,2,1,0:T(8,128)}) fusion(bf16[32,4,16,256]{3,2,1,0:T(8,128)(2,1)} %param.8), kind=kLoop, calls=%fused_computation.12 | loop fusion | flops 34078720 | bytes 5242880 | tf_op jit(solution)/shard_map/jvp()/mul | solution.py:25
  13.8 2.4 fusion.40
  16.2 3.8 collective-permute-start
  20.0 5.4 collective-permute-start.1
  31.8 2.1 collective-permute-start.4
  33.9 4.4 collective-permute-start.5
  39.5 2.1 collective-permute-start.7
  43.3 2.6 fusion.38
  49.4 2.4 copy.36
  51.8 9.2 %fusion.91 = f32[32,64,16,32]{1,0,3,2:T(8,128)} fusion(f32[64,4,16,32]{0,1,3,2:T(4,128)S(1)} %copy.36, s32[4]{0:T(128)S(1)} %iota_add_fusion.1, s32[32]{0:T(128)S(1)} %compare_select_fusion), kind=kOutput, calls=%fused_computation.162 | convolution fusion | flops 50333440 | bytes 4718736 | tf_op jit(solution)/shard_map/kx,cxym->kcym/dot_general | solution.py:41
  61.1 9.3 %fusion.94 = f32[32,64,16,32]{1,0,3,2:T(8,128)} fusion(f32[64,4,16,32]{0,1,3,2:T(4,128)S(1)} %copy.36, s32[4]{0:T(128)S(1)} %iota_add_fusion.1, s32[32]{0:T(128)S(1)} %compare_select_fusion), kind=kOutput, calls=%fused_computation.165 | convolution fusion | flops 50333440 | bytes 4718736 | tf_op jit(solution)/shard_map/kx,cxym->kcym/dot_general | solution.py:40
  70.4 11.9 %slice_add_fusion = (f32[32,64,16,16]{1,0,3,2:T(8,128)}, f32[32,64,16,16]{1,0,3,2:T(8,128)}) fusion(f32[32,64,16,32]{1,0,3,2:T(8,128)} %fusion.91, f32[32,64,16,32]{1,0,3,2:T(8,128)} %fusion.94), kind=kLoop, calls=%fused_computation.6 | loop fusion | flops 1048576 | bytes 12582912 | tf_op jit(solution)/shard_map/add | solution.py:43
  82.3 5.2 pad_maximum_fusion
  87.5 8.1 %copy.38 = f32[32,64,16,32]{1,3,2,0:T(8,128)} copy(f32[32,64,16,32]{1,0,3,2:T(8,128)S(1)} %pad_maximum_fusion) | data formatting | bytes 8388608 | tf_op jit(solution)/shard_map/concatenate | solution.py:48
  95.7 223.7 %reduce-scatter.3.cloned.1.call-done = f32[2,64,16,32]{1,3,2,0:T(8,128)} async-done(((f32[32,64,16,32]{1,3,2,0:T(8,128)}), f32[2,64,16,32]{1,3,2,0:T(8,128)}) %reduce-scatter.3.cloned.1.call-update) | async-done | bytes 262160 | tf_op jit(solution)/shard_map/reduce_scatter | solution.py:103
  319.4 2.3 fusion.47
  321.7 2.3 fusion.45
  328.1 2.2 squeeze.9
  330.3 59.0 %reduce-scatter.5.cloned.1.call-done = f32[2,2,64,32]{2,3,1,0:T(8,128)} async-done(((f32[32,2,64,32]{2,3,1,0:T(8,128)}), f32[2,2,64,32]{2,3,1,0:T(8,128)}) %reduce-scatter.5.cloned.1.call-update) | async-done | bytes 32784 | tf_op jit(solution)/shard_map/reduce_scatter | solution.py:113
  392.2 24.7 %all_gather.6 = f32[2,32,32,32]{3,2,0,1:T(8,128)S(1)} all-gather(f32[2,2,32,32]{3,2,0,1:T(8,128)S(1)} %copy.44), channel_id=1, replica_groups=mesh['slab'=16,'pencil'=16] {'pencil'}, dimensions={1}, use_global_device_ids=true | all-gather | bytes 278528 | tf_op jit(solution)/shard_map/all_gather | solution.py:151
  430.5 124.2 %all-gather.2.cloned.1.call-done = f32[32,16,32,32]{3,2,1,0:T(8,128)} async-done(((f32[2,16,32,32]{3,2,1,0:T(8,128)}), f32[32,16,32,32]{3,2,1,0:T(8,128)}) %all-gather.2.cloned.1.call-update) | async-done | bytes 2097168 | tf_op jit(solution)/shard_map/all_gather | solution.py:156
  554.7 13.0 %fusion.2 = f32[4,16,32,32]{3,0,2,1:T(4,128)S(1)} fusion(f32[32,16,32,32]{3,2,1,0:T(8,128)} %all-gather.2.cloned.1.call-done, s32[4]{0:T(128)S(1)} %iota_add_fusion.1, s32[32]{0:T(128)S(1)} %compare_select_fusion), kind=kOutput, calls=%fused_computation.3 | convolution fusion | flops 25167616 | bytes 2359440 | tf_op jit(solution)/shard_map/kx,kycm->xycm/dot_general | solution.py:40
  567.7 8.6 %fusion = f32[4,16,32,32]{3,0,2,1:T(4,128)S(1)} fusion(f32[32,16,32,32]{3,2,1,0:T(8,128)S(1)} %copy-done.2, s32[4]{0:T(128)S(1)} %iota_add_fusion.1, s32[32]{0:T(128)S(1)} %compare_select_fusion), kind=kOutput, calls=%fused_computation.1 | convolution fusion | flops 25167616 | bytes 2359440 | tf_op jit(solution)/shard_map/kx,kycm->xycm/dot_general | solution.py:41
  578.1 3.0 add_convert_fusion
  (97 shorter events, 35.0 us)
Async XLA Ops:
  7.2 21.2 %copy-start = (bf16[32,4,16,256]{3,2,1,0:T(8,128)(2,1)S(1)}, bf16[32,4,16,256]{3,2,1,0:T(8,128)(2,1)}, u32[]{:S(2)}) copy-start(bf16[32,4,16,256]{3,2,1,0:T(8,128)(2,1)} %param.7) | copy-start | bytes 3145732
  7.2 6.6 %copy-start.9 = (f32[32]{0:T(128)S(1)}, f32[32]{0:T(128)}, u32[]{:S(2)}) copy-start(f32[32]{0:T(128)} %param.11) | copy-start | bytes 388
  7.2 312.2 %reduce-scatter.3.cloned.1.call-start = ((), (), s32[]{:S(2)}) async-start(), calls=%async_computation.2 | async-start | bytes 8912896 | tf_op jit(solution)/shard_map/reduce_scatter | solution.py:103
  13.8 17.9 %copy-start.6 = (bf16[4,16,256]{2,1,0:T(8,128)(2,1)S(1)}, bf16[4,16,256]{2,1,0:T(8,128)(2,1)}, u32[]{:S(2)}) copy-start(bf16[4,16,256]{2,1,0:T(8,128)(2,1)} %param.9) | copy-start | bytes 98308
  13.8 17.9 %copy-start.7 = (bf16[4,16,256]{2,1,0:T(8,128)(2,1)S(1)}, bf16[4,16,256]{2,1,0:T(8,128)(2,1)}, u32[]{:S(2)}) copy-start(bf16[4,16,256]{2,1,0:T(8,128)(2,1)} %param.10) | copy-start | bytes 98308
  16.2 10.2 %collective-permute-start = (f32[1,16,256]{2,1,0:T(8,128)S(1)}, f32[1,16,256]{2,1,0:T(8,128)S(1)}, u32[]{:S(2)}, u32[]{:S(2)}) collective-permute-start(f32[1,16,256]{2,1,0:T(8,128)S(1)} %get-tuple-element.36), channel_id=1, source_target_pairs={{0,16},{16,32},{32,48},{48,64},{64,80},{80,96},{96,112},{112,128},... | collective-permute-start | bytes 49160 | tf_op jit(solution)/shard_map/ppermute | solution.py:18
  20.0 6.4 %collective-permute-start.1 = (f32[1,16,256]{2,1,0:T(8,128)S(1)}, f32[1,16,256]{2,1,0:T(8,128)S(1)}, u32[]{:S(2)}, u32[]{:S(2)}) collective-permute-start(f32[1,16,256]{2,1,0:T(8,128)S(1)} %get-tuple-element.37), channel_id=1, source_target_pairs={{16,0},{32,16},{48,32},{64,48},{80,64},{96,80},{112,96},{128,112},... | collective-permute-start | bytes 49160 | tf_op jit(solution)/shard_map/ppermute | solution.py:19
  26.5 2.9 collective-permute-start.2
  28.4 3.1 collective-permute-start.3
  31.6 11.7 %copy-start.3 = (bf16[32,4,16,256]{3,2,1,0:T(8,128)(2,1)S(1)}, bf16[32,4,16,256]{3,2,1,0:T(8,128)(2,1)}, u32[]{:S(2)}) copy-start(bf16[32,4,16,256]{3,2,1,0:T(8,128)(2,1)} %param.8) | copy-start | bytes 3145732
  31.8 7.5 %collective-permute-start.4 = (f32[1,16,256]{2,1,0:T(8,128)S(1)}, f32[1,16,256]{2,1,0:T(8,128)S(1)}, u32[]{:S(2)}, u32[]{:S(2)}) collective-permute-start(f32[1,16,256]{2,1,0:T(8,128)S(1)} %get-tuple-element.30), channel_id=1, source_target_pairs={{0,16},{16,32},{32,48},{48,64},{64,80},{80,96},{96,112},{112,128},... | collective-permute-start | bytes 49160 | tf_op jit(solution)/shard_map/ppermute | solution.py:18
  33.9 5.4 collective-permute-start.5
  39.4 3.5 collective-permute-start.6
  39.5 3.5 collective-permute-start.7
  45.9 1.8 copy-start.4
  95.7 293.6 %reduce-scatter.5.cloned.1.call-start = ((), (), s32[]{:S(2)}) async-start(), calls=%async_computation.3 | async-start | bytes 1114112 | tf_op jit(solution)/shard_map/reduce_scatter | solution.py:113
  324.4 1.7 copy-start.5
  326.0 228.7 %all-gather.2.cloned.1.call-start = ((), (), s32[]{:S(2)}) async-start(), calls=%async_computation.4 | async-start | bytes 8912896 | tf_op jit(solution)/shard_map/all_gather | solution.py:156
  421.8 1.2 copy-start.8
  554.7 13.0 %copy-start.2 = (f32[32,16,32,32]{3,2,1,0:T(8,128)S(1)}, f32[32,16,32,32]{3,2,1,0:T(8,128)}, u32[]{:S(2)}) copy-start(f32[32,16,32,32]{3,2,1,0:T(8,128)} %all-gather.2.cloned.1.call-done) | copy-start | bytes 6291460
  578.1 3.1 copy-start.1
Sparse Core Ops, SparseCore 0:
  95.8 223.5 reduce-scatter.2
  326.1 63.1 reduce-scatter.4
  421.2 133.4 all-gather.1
where the time goes:
time: 597 us; the launch traced here: 588 us
  waiting for transfers between devices  411 us (69%)
  matrix products  56.8 us (10%)
  other arithmetic  34.7 us (6%)
  local copies, waits for them, and re-layouts  26.4 us (4%)
  blocking collectives  24.7 us (4%)
  starting transfers between devices  19.9 us (3%)
  between operations  14.4 us (2%)
    reduce_scatter x1, waiting for transfers between devices, shards(): lax.psum_scatter(rotate(cosine_table, sine_table, spectra_z, 'kx,cxym->kc...  224 us
    all_gather x1, waiting for transfers between devices, shards(): shard_part = lax.all_gather(spread_first, 'slab', axis=0, tiled=True)  124 us
    reduce_scatter x1, waiting for transfers between devices, shards(): lax.psum_scatter(rotate(cosine_table, sine_table, partial_x, 'ky,acym->ka...  59 us
    dot_general x4, matrix products, rotate(): cos_part = jnp.einsum(pattern, cosine_table, values, precision=highest)  25.9 us
    all_gather x1, blocking collectives, shards(): shard_part = lax.all_gather(scaled, 'pencil', axis=1, tiled=True)  24.7 us
    dot_general x4, matrix products, rotate(): sin_part = jnp.einsum(pattern, sine_table, values, precision=highest)  21.5 us
    add x2, other arithmetic, rotate(): real_part = cos_part[..., :modes_half] + sin_part[..., modes_half:]  12.1 us
  transfers between devices with their start and end apart: 11, of which 7 were waited for; matrix products, arithmetic and copies ran while one was open for 3% of the time, Pallas kernels for 0%

commit v1 on v0

v1 whole, which is shorter than its diff:
```python
import functools
import math

import jax
import jax.numpy as jnp
import ml_dtypes
import numpy as np
from jax import lax
from jax.experimental import pallas as pl
from jax.experimental.pallas import tpu as pltpu
from jax.sharding import PartitionSpec as P

F32 = jnp.float32
BF16 = jnp.bfloat16
C, CX, CY, NZ = 32, 4, 16, 256
NX, NY = 64, 256
N = 16
KZ = 16
LANES = CX * C
CELLS = float(NX * NY * NZ)
VMEM_LIMIT = 40 * 1024 * 1024


def split_2(table):
    high = table.astype(ml_dtypes.bfloat16)
    low = (table - high.astype(np.float64)).astype(ml_dtypes.bfloat16)
    return high, low


def depth_tables():
    angles = 2.0 * math.pi * ((np.arange(KZ)[:, None] * np.arange(NZ)[None, :]) % NZ) / NZ
    table = np.concatenate([np.cos(angles), -np.sin(angles)], axis=0)
    high, low = split_2(table)
    return np.concatenate([high, low], axis=0), np.concatenate([high, high, low], axis=0)


def wave(index):
    return index if index < 16 else index - 32


def pencil_phases():
    position = 16.0 * np.arange(N)[:, None] + 7.5
    angles = 2.0 * math.pi * np.arange(17)[None, :] * position / NY
    return np.concatenate([np.cos(angles), np.sin(angles)], axis=1).astype(np.float32).reshape(-1)


def slab_tables():
    forward = np.zeros((N, N, 4, 2, LANES))
    backward = np.zeros((N, N, 4, 2, LANES))
    for position in range(N):
        for other in range(N):
            for shift in range(4):
                for group in range(4):
                    k = wave(2 * other + group // 2)
                    lanes = slice(group * C, (group + 1) * C)
                    x = 4 * position + (group - shift) % 4
                    angle = 2.0 * math.pi * ((k * x) % NX) / NX
                    cos, sin = math.cos(angle), math.sin(angle)
                    forward[position, other, shift, 0, lanes] = cos if group % 2 == 0 else -sin
                    forward[position, other, shift, 1, lanes] = sin if group % 2 == 0 else cos
                    x = 4 * position + (group + shift) % 4
                    angle = 2.0 * math.pi * ((k * x) % NX) / NX
                    cos, sin = math.cos(angle), math.sin(angle)
                    backward[position, other, shift, 0, lanes] = cos if group % 2 == 0 else -sin
                    backward[position, other, shift, 1, lanes] = sin if group % 2 == 0 else cos
    shape = (N, N * 8, LANES)
    return forward.astype(np.float32).reshape(shape), backward.astype(np.float32).reshape(shape)


DEPTH_FORWARD, DEPTH_BACKWARD = depth_tables()
PENCIL_PHASES = pencil_phases()
SLAB_FORWARD, SLAB_BACKWARD = slab_tables()


def normal_tail(values):
    size = jnp.abs(values)
    bell = jnp.exp(-0.5 * values * values)
    denominator = 1.0 + (0.3275911 / math.sqrt(2.0)) * size
    t = pl.reciprocal(denominator, approx=True)
    t = t * (2.0 - denominator * t)
    poly = 0.5 * 1.061405429 * t - 0.5 * 1.453152027
    poly = poly * t + 0.5 * 1.421413741
    poly = poly * t - 0.5 * 0.284496736
    poly = poly * t + 0.5 * 0.254829592
    return bell, poly * t * bell


def field_kernel(pre_ref, coef_ref, source_ref, proj_ref, field_ref, up_ref, down_ref):
    def add_channel(c, total):
        values = pre_ref[c].astype(F32)
        _, tail = normal_tail(values)
        return total + proj_ref[c] * (jnp.maximum(values, 0.0) - jnp.abs(values) * tail)

    total = lax.fori_loop(0, C, add_channel, jnp.zeros((CX, CY, NZ), F32), unroll=2)
    field_ref[...] = total
    up_ref[0:2] = total[2:4]
    down_ref[0:2] = total[0:2]
    up_ref[2] = coef_ref[3].astype(F32)
    up_ref[3] = source_ref[3].astype(F32)
    down_ref[2] = coef_ref[0].astype(F32)
    down_ref[3] = source_ref[0].astype(F32)


def slope_kernel(pre_ref, proj_ref, slope_ref):
    def one_channel(c, carry):
        values = pre_ref[c].astype(F32)
        bell, tail = normal_tail(values)
        below = jnp.where(values >= 0.0, 1.0 - tail, tail)
        slope = proj_ref[c] * (below + values * (bell * (1.0 / math.sqrt(2.0 * math.pi))))
        for x in range(CX):
            for side in range(2):
                piece = slope[x, :, side * 128 : (side + 1) * 128]
                slope_ref[side, pl.ds(x * C + c, CY, stride=LANES), :] = piece
        return carry

    lax.fori_loop(0, C, one_channel, 0, unroll=2)


def nt_dot(left, right):
    return lax.dot_general(left, right, (((1,), (1,)), ((), ())), preferred_element_type=F32)


def tn_dot(left, right):
    return lax.dot_general(left, right, (((0,), (0,)), ((), ())), preferred_element_type=F32)


def pencil_forward(modes_ref, phase_ref, position, out_ref, base):
    for half in range(2):
        sums, diffs = [], []
        for part in range(2):
            rows = pl.ds(part * KZ + 8 * half, 8)
            first = [modes_ref[j, rows, :] for j in range(8)]
            second = [modes_ref[15 - j, rows, :] for j in range(8)]
            sums.append([a + b for a, b in zip(first, second)])
            diffs.append([a - b for a, b in zip(first, second)])
        for k in range(17):
            cosines = [math.cos(2.0 * math.pi * k * (7.5 - j) / NY) for j in range(8)]
            sines = [math.sin(2.0 * math.pi * k * (7.5 - j) / NY) for j in range(8)]
            even = [sum(w * v for w, v in zip(cosines, part)) for part in sums]
            w_cos = phase_ref[position * 34 + k]
            w_sin = phase_ref[position * 34 + 17 + k]
            if k == 0:
                results = [(0, even[0], even[1], w_sin)]
            else:
                odd = [sum(w * v for w, v in zip(sines, part)) for part in diffs]
                results = [(32 - k, even[0] + odd[1], even[1] - odd[0], -w_sin)]
                if k < 16:
                    results.append((k, even[0] - odd[1], even[1] + odd[0], w_sin))
            for index, real, imag, sin in results:
                row = base + (index % 2) * 32 + 8 * half
                out_ref[index // 2, pl.ds(row, 8), :] = w_cos * real + sin * imag
                out_ref[index // 2, pl.ds(row + KZ, 8), :] = w_cos * imag - sin * real


def input_kernel(position_ref, phase_ref, input_ref, table_ref, out_ref, rows_ref, modes_ref):
    for side in range(2):
        piece = input_ref[:, :, :, side * 128 : (side + 1) * 128]
        rows_ref[side] = piece.astype(F32).reshape(C * CX * CY, 128)
    for y in range(CY):
        sides = [
            jnp.concatenate(
                [rows_ref[side, pl.ds(x * CY + y, C, stride=CX * CY), :] for x in range(CX)],
                axis=0,
            )
            for side in range(2)
        ]
        values = jnp.concatenate(sides, axis=1).astype(BF16)
        both = nt_dot(table_ref[...], values)
        modes_ref[y] = both[:32] + both[32:]
    pencil_forward(modes_ref, phase_ref, position_ref[0], out_ref, 0)


def pack_kernel(field_ref, coef_ref, source_ref, before_ref, after_ref, up_ref, down_ref):
    for out_ref, cells, cell in ((up_ref, slice(14, 16), slice(15, 16)), (down_ref, slice(0, 2), slice(0, 1))):
        for x in range(8):
            if x < 2:
                rows = before_ref[x, cells, :]
            elif x < 6:
                rows = field_ref[x - 2, cells, :]
            else:
                rows = after_ref[x - 6, cells, :]
            out_ref[2 * x : 2 * x + 2, :] = rows
        for base, part, own_ref in ((16, 2, coef_ref), (22, 3, source_ref)):
            for x in range(6):
                if x == 0:
                    row = before_ref[part, cell, :]
                elif x == 5:
                    row = after_ref[part, cell, :]
                else:
                    row = own_ref[x - 1].astype(F32)[cell, :]
                out_ref[base + x : base + x + 1, :] = row
        out_ref[28:32, :] = jnp.zeros((4, NZ), F32)


def smooth(values):
    values = values + 0.5 * (pltpu.roll(values, 1, 2) + pltpu.roll(values, NZ - 1, 2))
    values = values + 0.5 * (pltpu.roll(values, 1, 1) + pltpu.roll(values, 31, 1))
    return 0.5 * (values[:-2] + values[2:]) + values[1:-1]


def grad_kernel(
    position_ref,
    phase_ref,
    field_ref,
    coef_ref,
    source_ref,
    before_ref,
    after_ref,
    low_ref,
    high_ref,
    slope_ref,
    table_ref,
    input_part_ref,
    out_ref,
    act_ref,
    wide_field,
    wide_coef,
    wide_source,
    grad_ref,
    modes_ref,
):
    own = slice(8, 24)
    wide_field[...] = jnp.zeros_like(wide_field)
    wide_coef[...] = jnp.zeros_like(wide_coef)
    wide_source[...] = jnp.zeros_like(wide_source)
    wide_field[0:2, own, :] = before_ref[0:2]
    wide_field[2:6, own, :] = field_ref[...]
    wide_field[6:8, own, :] = after_ref[0:2]
    for x in range(8):
        wide_field[x, 6:8, :] = low_ref[2 * x : 2 * x + 2, :]
        wide_field[x, 24:26, :] = high_ref[2 * x : 2 * x + 2, :]
    for wide, own_ref, part, base in ((wide_coef, coef_ref, 2, 16), (wide_source, source_ref, 3, 22)):
        wide[0, own, :] = before_ref[part]
        wide[1:5, own, :] = own_ref[...].astype(F32)
        wide[5, own, :] = after_ref[part]
        for x in range(6):
            wide[x, 7:8, :] = low_ref[base + x : base + x + 1, :]
            wide[x, 24:25, :] = high_ref[base + x : base + x + 1, :]
    field = wide_field[...]
    center = field[1:7]
    residual = (16.0 / 3.0 - wide_coef[...]) * center - (2.0 / 3.0) * smooth(field) - wide_source[...]
    grad_ref[...] = (16.0 / 3.0 - wide_coef[1:5]) * residual[1:5] - (2.0 / 3.0) * smooth(residual)
    for y in range(CY):
        grads = []
        for x in range(CX):
            rows = slice(y * LANES + x * C, y * LANES + (x + 1) * C)
            slope = jnp.concatenate([slope_ref[0, rows, :], slope_ref[1, rows, :]], axis=1)
            grads.append(slope * grad_ref[x, 8 + y : 9 + y, :])
        act = jnp.concatenate(grads, axis=0)
        high = act.astype(BF16)
        low = (act - high.astype(F32)).astype(BF16)
        act_ref[y, 0:LANES, :] = high
        act_ref[y, LANES : 2 * LANES, :] = low
        both = nt_dot(table_ref[...], high)
        modes_ref[y] = both[:32] + both[32:] + nt_dot(table_ref[0:32, :], low)
    out_ref[:, 0:64, :] = input_part_ref[...]
    pencil_forward(modes_ref, phase_ref, position_ref[0], out_ref, 64)


def local_kernel(pointwise_ref, act_ref, out_ref):
    for y in range(CY):
        out_ref[y] = jnp.dot(pointwise_ref[...], act_ref[y], preferred_element_type=F32)


def slab_forward_kernel(parts_ref, table_ref, out_ref):
    for block in range(4):
        for half in range(2):
            pieces = []
            for part in range(2):
                rows = pl.ds(block * 32 + part * KZ + 8 * half, 8)
                total = parts_ref[0, rows, :]
                for source in range(1, N):
                    total = total + parts_ref[source, rows, :]
                pieces.append([total] + [pltpu.roll(total, 32 * d, 1) for d in range(1, 4)])
            for owner in range(N):
                result = None
                for d in range(4):
                    for part in range(2):
                        row = owner * 8 + d * 2 + part
                        term = pieces[part][d] * table_ref[row : row + 1, :]
                        result = term if result is None else result + term
                out_ref[owner, pl.ds(block * KZ + 8 * half, 8), :] = result


def flat_modes(block, group):
    lane_group = lax.broadcasted_iota(jnp.int32, (KZ, LANES), 1) // C
    row = lax.broadcasted_iota(jnp.int32, (KZ, LANES), 0)
    picked = jnp.where(lane_group == group, block, 0.0)
    picked = picked + pltpu.roll(picked, 64, 1)
    picked = picked + pltpu.roll(picked, 32, 1)
    tiles = [
        jnp.sum(jnp.where(row == 4 * tile + lane_group, picked, 0.0), axis=0, keepdims=True)
        for tile in range(4)
    ]
    return jnp.concatenate(tiles, axis=1)


def split_3(values):
    high = values.astype(BF16)
    rest = values - high.astype(F32)
    middle = rest.astype(BF16)
    low = (rest - middle.astype(F32)).astype(BF16)
    return high, middle, low


def back_kernel(parts_ref, weight_ref, modes_ref, out_ref):
    total = parts_ref[0]
    for source in range(1, N):
        total = total + parts_ref[source]
    modes_ref[...] = total
    rows = lax.broadcasted_iota(jnp.int32, (KZ, KZ * C), 0)
    lanes = lax.broadcasted_iota(jnp.int32, (KZ, KZ * C), 1)
    mask = jnp.where(lanes // C == rows, 1.0, 0.0).astype(BF16)
    kz = lax.broadcasted_iota(jnp.int32, (KZ, LANES), 0)
    scale = jnp.where(kz == 0, 1.0 / CELLS, 2.0 / CELLS)
    for ky in range(2):
        block = total[32 + ky * KZ : 32 + (ky + 1) * KZ]
        products = []
        for kx in range(2):
            real, imag = flat_modes(block, 2 * kx), flat_modes(block, 2 * kx + 1)
            w_real = weight_ref[0, kx, ky].astype(F32)
            w_imag = weight_ref[1, kx, ky].astype(F32)
            products.append(w_real * real + w_imag * imag)
            products.append(w_real * imag - w_imag * real)
        high, middle, low = split_3(jnp.concatenate(products, axis=0))
        back = scale * (nt_dot(mask, high) + nt_dot(mask, middle) + nt_dot(mask, low))
        for device in range(N):
            out_ref[device, ky * KZ : (ky + 1) * KZ, :] = back


def weight_grad_kernel(modes_ref, out_ref):
    rows = lax.broadcasted_iota(jnp.int32, (KZ, KZ * C), 0)
    lanes = lax.broadcasted_iota(jnp.int32, (KZ, KZ * C), 1)
    mask = jnp.where(lanes // C == rows, 1.0, 0.0).astype(BF16)
    first = lax.broadcasted_iota(jnp.int32, (1, KZ * C), 1) < C
    scale = jnp.where(first, 1.0 / CELLS, 2.0 / CELLS)
    for ky in range(2):
        inputs = modes_ref[ky * KZ : (ky + 1) * KZ, :]
        grads = modes_ref[32 + ky * KZ : 32 + (ky + 1) * KZ, :]
        high, middle, low = split_3(inputs)
        spread = tn_dot(high, mask) + tn_dot(middle, mask) + tn_dot(low, mask)
        for kx in range(2):
            real = scale * flat_modes(grads, 2 * kx)
            imag = scale * flat_modes(grads, 2 * kx + 1)
            in_real = spread[(2 * kx) * C : (2 * kx + 1) * C]
            in_imag = spread[(2 * kx + 1) * C : (2 * kx + 2) * C]
            out_ref[0, kx, ky] = (in_real * real + in_imag * imag).astype(BF16)
            out_ref[1, kx, ky] = (in_real * imag - in_imag * real).astype(BF16)


def slab_backward_kernel(parts_ref, table_ref, out_ref):
    for ky in range(2):
        for half in range(2):
            totals = [[None] * 4, [None] * 4]
            for source in range(N):
                values = parts_ref[source, pl.ds(ky * KZ + 8 * half, 8), :]
                for d in range(4):
                    for part in range(2):
                        row = source * 8 + d * 2 + part
                        term = values * table_ref[row : row + 1, :]
                        last = totals[part][d]
                        totals[part][d] = term if last is None else last + term
            for part in range(2):
                result = totals[part][0]
                for d in range(1, 4):
                    result = result + pltpu.roll(totals[part][d], 32 * d, 1)
                for device in range(N):
                    out_ref[device, pl.ds(ky * 32 + part * KZ + 8 * half, 8), :] = result


def output_kernel(
    position_ref, phase_ref, parts_ref, local_ref, table_ref, out_ref, modes_ref, rows_ref
):
    position = position_ref[0]
    for half in range(2):
        evens, odds = [], []
        for k in range(17):
            w_cos = phase_ref[position * 34 + k]
            w_sin = phase_ref[position * 34 + 17 + k]

            def turned(index, sin):
                row = (index % 2) * 32 + 8 * half
                real = parts_ref[index // 2, pl.ds(row, 8), :]
                imag = parts_ref[index // 2, pl.ds(row + KZ, 8), :]
                return w_cos * real - sin * imag, w_cos * imag + sin * real

            if k == 0:
                evens.append(turned(0, w_sin))
                odds.append(None)
            elif k == 16:
                real, imag = turned(16, -w_sin)
                evens.append((real, imag))
                odds.append((-real, -imag))
            else:
                plus, minus = turned(k, w_sin), turned(32 - k, -w_sin)
                evens.append((plus[0] + minus[0], plus[1] + minus[1]))
                odds.append((plus[0] - minus[0], plus[1] - minus[1]))
            modes_ref[0, k, 0] = evens[-1][0]
            modes_ref[0, k, 1] = evens[-1][1]
            if k:
                modes_ref[1, k, 0] = odds[-1][0]
                modes_ref[1, k, 1] = odds[-1][1]
        for y in range(8):
            even = [modes_ref[0, 0, 0], modes_ref[0, 0, 1]]
            odd = [None, None]
            for k in range(1, 17):
                angle = 2.0 * math.pi * k * (y - 7.5) / NY
                cos, sin = math.cos(angle), math.sin(angle)
                for part in range(2):
                    even[part] = even[part] + cos * modes_ref[0, k, part]
                    term = sin * modes_ref[1, k, part]
                    odd[part] = term if odd[part] is None else odd[part] + term
            rows = pl.ds(8 * half, 8)
            more = pl.ds(KZ + 8 * half, 8)
            rows_ref[y, rows, :] = even[0] - odd[1]
            rows_ref[y, more, :] = even[1] + odd[0]
            rows_ref[15 - y, rows, :] = even[0] + odd[1]
            rows_ref[15 - y, more, :] = even[1] - odd[0]


def finish_kernel(rows_ref, local_ref, table_ref, out_ref, flat_ref):
    for y in range(CY):
        values = rows_ref[y]
        high = values.astype(BF16)
        low = (values - high.astype(F32)).astype(BF16)
        stacked = jnp.concatenate([high, low, high], axis=0)
        result = tn_dot(stacked, table_ref[...]) + local_ref[y]
        for x in range(CX):
            for side in range(2):
                piece = result[x * C : (x + 1) * C, side * 128 : (side + 1) * 128]
                flat_ref[side, pl.ds(x * CY + y, C, stride=CX * CY), :] = piece
    for side in range(2):
        piece = flat_ref[side].astype(BF16).reshape(C, CX, CY, 128)
        out_ref[:, :, :, side * 128 : (side + 1) * 128] = piece


def last_kernel(
    position_ref, phase_ref, parts_ref, local_ref, table_ref, out_ref, modes_ref, rows_ref, flat_ref
):
    output_kernel(
        position_ref, phase_ref, parts_ref, local_ref, table_ref, out_ref, modes_ref, rows_ref
    )
    finish_kernel(rows_ref, local_ref, table_ref, out_ref, flat_ref)


def call(kernel, name, out, scratch=(), scalars=()):
    def run(*args):
        single = not isinstance(out, list)
        specs = [
            pl.BlockSpec(memory_space=pltpu.SMEM if i in scalars else pltpu.VMEM)
            for i in range(len(args))
        ]
        shapes = [jax.ShapeDtypeStruct(*o) for o in ([out] if single else out)]
        result = pl.pallas_call(
            kernel,
            out_shape=shapes,
            in_specs=specs,
            out_specs=[pl.BlockSpec(memory_space=pltpu.VMEM)] * len(shapes),
            scratch_shapes=[pltpu.VMEM(*s) for s in scratch],
            compiler_params=pltpu.CompilerParams(vmem_limit_bytes=VMEM_LIMIT),
            name=name,
        )(*args)
        return result[0] if single else result

    return run


def shards(
    layer_input, pre_activation, coefficient, source, projection, pointwise, spectral_weight
):
    up = [(i, (i + 1) % N) for i in range(N)]
    down = [(j, i) for i, j in up]
    slab = lax.axis_index("slab")
    pencil = lax.axis_index("pencil").reshape(1)
    phases = jnp.asarray(PENCIL_PHASES)
    depth_forward = jnp.asarray(DEPTH_FORWARD)
    depth_backward = jnp.asarray(DEPTH_BACKWARD)
    slab_forward = lax.dynamic_index_in_dim(jnp.asarray(SLAB_FORWARD), slab, 0, False)
    slab_backward = lax.dynamic_index_in_dim(jnp.asarray(SLAB_BACKWARD), slab, 0, False)
    pointwise_4 = jnp.kron(jnp.eye(CX, dtype=BF16), pointwise)
    pointwise_8 = jnp.concatenate([pointwise_4, pointwise_4], axis=1)

    field, edge_up, edge_down = call(
        field_kernel,
        "field",
        [((CX, CY, NZ), F32), ((4, CY, NZ), F32), ((4, CY, NZ), F32)],
        scalars=(3,),
    )(pre_activation, coefficient, source, projection)
    before = lax.ppermute(edge_up, "slab", up)
    after = lax.ppermute(edge_down, "slab", down)
    side_up, side_down = call(pack_kernel, "pack", [((32, NZ), F32), ((32, NZ), F32)])(
        field, coefficient, source, before, after
    )
    low = lax.ppermute(side_up, "pencil", up)
    high = lax.ppermute(side_down, "pencil", down)
    slope = call(slope_kernel, "slope", ((2, CY * LANES, 128), F32), scalars=(1,))(
        pre_activation, projection
    )
    input_part = call(
        input_kernel,
        "input_modes",
        ((N, 64, LANES), F32),
        scratch=[((2, C * CX * CY, 128), F32), ((CY, 32, LANES), F32)],
        scalars=(0, 1),
    )(pencil, phases, layer_input, depth_forward)
    to_pencil, act = call(
        grad_kernel,
        "grad_modes",
        [((N, 128, LANES), F32), ((CY, 2 * LANES, NZ), BF16)],
        scratch=[
            ((8, 32, NZ), F32),
            ((6, 32, NZ), F32),
            ((6, 32, NZ), F32),
            ((4, 32, NZ), F32),
            ((CY, 32, LANES), F32),
        ],
        scalars=(0, 1),
    )(
        pencil,
        phases,
        field,
        coefficient,
        source,
        before,
        after,
        low,
        high,
        slope,
        depth_forward,
        input_part,
    )
    from_pencil = lax.all_to_all(to_pencil, "pencil", 0, 0, tiled=True)
    local = call(local_kernel, "local", ((CY, LANES, NZ), F32))(pointwise_8, act)
    to_slab = call(slab_forward_kernel, "slab_forward", ((N, 64, LANES), F32))(
        from_pencil, slab_forward
    )
    from_slab = lax.all_to_all(to_slab, "slab", 0, 0, tiled=True)
    modes, to_slab = call(back_kernel, "back", [((64, LANES), F32), ((N, 32, LANES), F32)])(
        from_slab, spectral_weight
    )
    from_slab = lax.all_to_all(to_slab, "slab", 0, 0, tiled=True)
    weight_grad = call(weight_grad_kernel, "weight_grad", (spectral_weight.shape, BF16))(modes)
    to_pencil = call(slab_backward_kernel, "slab_backward", ((N, 64, LANES), F32))(
        from_slab, slab_backward
    )
    from_pencil = lax.all_to_all(to_pencil, "pencil", 0, 0, tiled=True)
    input_grad = call(
        last_kernel,
        "output",
        ((C, CX, CY, NZ), BF16),
        scratch=[
            ((2, 17, 2, 8, LANES), F32),
            ((CY, 32, LANES), F32),
            ((2, C * CX * CY, 128), F32),
        ],
        scalars=(0, 1),
    )(pencil, phases, from_pencil, local, depth_backward)
    return (input_grad, weight_grad)


def solution(mesh):
    return jax.shard_map(
        shards,
        mesh=mesh,
        in_specs=(
            P(None, "slab", "pencil", None),
            P(None, "slab", "pencil", None),
            P("slab", "pencil", None),
            P("slab", "pencil", None),
            P(),
            P(),
            P(None, "slab", "pencil", None, None),
        ),
        out_specs=(P(None, "slab", "pencil", None), P(None, "slab", "pencil", None, None)),
        check_vma=False,
    )
```

time: 597 us -> 120 us (0.20); the launches traced: 588 us -> 119 us
  waiting for transfers between devices: 411 us -> 33.5 us
  matrix products: 56.8 us -> 0 us
  other arithmetic: 34.7 us -> 0.13 us
  Pallas kernels: 0 us -> 21.2 us
  local copies, waits for them, and re-layouts: 26.4 us -> 8.83 us
  between operations: 14.4 us -> 0.81 us
  starting transfers between devices: 19.9 us -> 29.3 us
    reduce_scatter x2 -> x0, waiting for transfers between devices: 283 us -> none  [the longest x1 224 us: shards(): lax.psum_scatter(rotate(cosine_table, sine_table, spectra_z, 'kx,cxym->kc...]
    all_gather x1 -> x0, waiting for transfers between devices: 124 us -> none  [shards(): shard_part = lax.all_gather(spread_first, 'slab', axis=0, tiled=True)]
    dot_general x13 -> x0, matrix products: 56.8 us -> none  [the longest x4 25.9 us: rotate(): cos_part = jnp.einsum(pattern, cosine_table, values, precision=highest)]
    all_to_all x0 -> x3, waiting for transfers between devices: none -> 31.9 us  [the longest x2 21.2 us: shards(): from_pencil = lax.all_to_all(to_pencil, 'pencil', 0, 0, tiled=True)]
    all_to_all x0 -> x1, blocking collectives: none -> 25.7 us  [shards(): from_slab = lax.all_to_all(to_slab, 'slab', 0, 0, tiled=True)]
    all_gather x1 -> x0, blocking collectives: 24.7 us -> none  [shards(): shard_part = lax.all_gather(scaled, 'pencil', axis=1, tiled=True)]
    pallas_call x0 -> x11, Pallas kernels: none -> 21.2 us  [run(): pl.pallas_call(kernel, out_shape=shapes, in_specs=specs, out_specs=[pl.Bl...]
    all_to_all x0 -> x3, starting transfers between devices: none -> 18.2 us  [the longest x2 13.6 us: shards(): from_pencil = lax.all_to_all(to_pencil, 'pencil', 0, 0, tiled=True)]
  transfers between devices with their start and end apart: 11 -> 7, of which waited for: 7 -> 4; matrix products, arithmetic and copies ran while one was open for 3% -> 2% of each run, Pallas kernels for 0% -> 7%
where the time goes in v1:
time: 120 us; the launch traced here: 119 us
  waiting for transfers between devices  33.5 us (28%)
  starting transfers between devices  29.3 us (24%)
  blocking collectives  25.7 us (21%)
  Pallas kernels  21.2 us (18%)
  local copies, waits for them, and re-layouts  8.83 us (7%)
    all_to_all x1, blocking collectives, shards(): from_slab = lax.all_to_all(to_slab, 'slab', 0, 0, tiled=True)  25.7 us
    all_to_all x2, waiting for transfers between devices, shards(): from_pencil = lax.all_to_all(to_pencil, 'pencil', 0, 0, tiled=True)  21.2 us
    pallas_call x11, Pallas kernels, run(): pl.pallas_call(kernel, out_shape=shapes, in_specs=specs, out_specs=[pl.Bl...  21.2 us
    all_to_all x2, starting transfers between devices, shards(): from_pencil = lax.all_to_all(to_pencil, 'pencil', 0, 0, tiled=True)  13.6 us
    all_to_all x1, waiting for transfers between devices, shards(): from_slab = lax.all_to_all(to_slab, 'slab', 0, 0, tiled=True)  10.7 us
    unnamed x32, local copies, waits for them, and re-layouts  7.01 us
    ppermute x1, starting transfers between devices, shards(): after = lax.ppermute(edge_down, 'slab', down)  5.38 us
    all_to_all x1, starting transfers between devices, shards(): from_slab = lax.all_to_all(to_slab, 'slab', 0, 0, tiled=True)  4.68 us
  transfers between devices with their start and end apart: 7, of which 4 were waited for; matrix products, arithmetic and copies ran while one was open for 2% of the time, Pallas kernels for 7%

profile of v1, /device:TPU:1, one launch (start us, length us, event | category | flops | bytes accessed | tf_op | source)
XLA Modules:
  0.0 119.4 jit_solution(12225154400277769305)
XLA Ops:
  0.7 1.2 %copy-done = bf16[32,4,16,256]{3,2,1,0:T(8,128)(2,1)S(1)} copy-done((bf16[32,4,16,256]{3,2,1,0:T(8,128)(2,1)S(1)}, bf16[32,4,16,256]{3,2,1,0:T(8,128)(2,1)}, u32[]{:S(2)}) %copy-start) | copy-done | bytes 1048600
  4.1 2.6 %field.1 = (f32[4,16,256]{2,1,0:T(8,128)S(1)}, f32[4,16,256]{2,1,0:T(8,128)S(1)}, f32[4,16,256]{2,1,0:T(8,128)S(1)}) custom-call(bf16[32,4,16,256]{3,2,1,0:T(8,128)(2,1)S(1)} %copy-done, bf16[4,16,256]{2,1,0:T(8,128)(2,1)S(1)} %copy-done.5, bf16[4,16,256]{2,1,0:T(8,128)(2,1)S(1)} %copy-done.7, f32[32]{0:T(128)S(1)} %copy-done.13), custom_call_target="tpu_custom_call" | custom-call | tf_op jit(solution)/shard_map/field/pallas_call | solution.py:454
  6.7 3.8 %collective-permute-start = (f32[4,16,256]{2,1,0:T(8,128)S(1)}, f32[4,16,256]{2,1,0:T(8,128)S(1)}, u32[]{:S(2)}, u32[]{:S(2)}) collective-permute-start(f32[4,16,256]{2,1,0:T(8,128)S(1)} %get-tuple-element.12), channel_id=1, source_target_pairs={{0,16},{16,32},{32,48},{48,64},{64,80},{80,96},{96,112},{112,128},... | collective-permute-start | bytes 196616 | tf_op jit(solution)/shard_map/ppermute | solution.py:489
  10.5 5.4 %collective-permute-start.1 = (f32[4,16,256]{2,1,0:T(8,128)S(1)}, f32[4,16,256]{2,1,0:T(8,128)S(1)}, u32[]{:S(2)}, u32[]{:S(2)}) collective-permute-start(f32[4,16,256]{2,1,0:T(8,128)S(1)} %get-tuple-element.13), channel_id=1, source_target_pairs={{16,0},{32,16},{48,32},{64,48},{80,64},{96,80},{112,96},{128,112},... | collective-permute-start | bytes 196616 | tf_op jit(solution)/shard_map/ppermute | solution.py:490
  15.9 1.6 %collective-permute-done.before_ref = f32[4,16,256]{2,1,0:T(8,128)S(1)} collective-permute-done((f32[4,16,256]{2,1,0:T(8,128)S(1)}, f32[4,16,256]{2,1,0:T(8,128)S(1)}, u32[]{:S(2)}, u32[]{:S(2)}) %collective-permute-start) | collective-permute-done | bytes 65568 | tf_op jit(solution)/shard_map/ppermute | solution.py:489
  18.1 1.8 %collective-permute-start.2 = (f32[32,256]{1,0:T(8,128)}, f32[32,256]{1,0:T(8,128)S(1)}, u32[]{:S(2)}, u32[]{:S(2)}) collective-permute-start(f32[32,256]{1,0:T(8,128)} %get-tuple-element.14), channel_id=1, source_target_pairs={{0,1},{1,2},{2,3},{3,4},{4,5},{5,6},{6,7},{7,8},{8,9},{9,10},{10,1... | collective-permute-start | bytes 98312 | tf_op jit(solution)/shard_map/ppermute | solution.py:494
  20.6 3.9 %slope.1.slope_ref = f32[2,2048,128]{2,1,0:T(8,128)S(1)} custom-call(bf16[32,4,16,256]{3,2,1,0:T(8,128)(2,1)S(1)} %copy-done.1, f32[32]{0:T(128)S(1)} %copy-done.14), custom_call_target="tpu_custom_call" | custom-call | tf_op jit(solution)/shard_map/slope/pallas_call | solution.py:454
  24.6 2.5 %input_modes.1.input_part_ref = f32[16,64,128]{2,1,0:T(8,128)S(1)} custom-call(s32[1]{0:T(128)} %bitcast.position_ref, f32[544]{0:T(1024)S(1)} %copy-done.12, bf16[32,4,16,256]{3,2,1,0:T(8,128)(2,1)S(1)} %copy-done.4, bf16[64,256]{1,0:T(8,128)(2,1)S(1)} %copy-done.10), custom_call_target="tpu_custom_call" | custom-call | tf_op jit(solution)/shard_map/input_modes/pallas_call | solution.py:454
  27.1 3.2 %grad_modes.1 = (f32[16,128,128]{2,1,0:T(8,128)}, bf16[16,256,256]{2,1,0:T(8,128)(2,1)S(1)}) custom-call(s32[1]{0:T(128)} %bitcast.position_ref, f32[544]{0:T(1024)S(1)} %copy-done.12, f32[4,16,256]{2,1,0:T(8,128)S(1)} %get-tuple-element.11.field_ref, bf16[4,16,256]{2,1,0:T(8,128)(2,1)S(1)} %copy-done.6, bf16[4,16,256]{2,1,0:T(8,128)(2,1)S(1)} %copy-done.8, ...), custom_call_target="tpu_custom_call" | custom-call | tf_op jit(solution)/shard_map/grad_modes/pallas_call | solution.py:454
  30.3 1.3 %copy-done.2 = bf16[16,256,256]{2,1,0:T(8,128)(2,1)} copy-done((bf16[16,256,256]{2,1,0:T(8,128)(2,1)}, bf16[16,256,256]{2,1,0:T(8,128)(2,1)S(1)}, u32[]{:S(2)}) %copy-start.2) | copy-done | bytes 2097176
  31.7 7.1 %all-to-all-start = ((f32[16,128,128]{2,1,0:T(8,128)}), f32[16,128,128]{2,1,0:T(8,128)S(1)}, u32[]{:S(2)}, u32[]{:S(2)}) async-start(f32[16,128,128]{2,1,0:T(8,128)} %get-tuple-element.16), calls=%async_computation | async-start | bytes 2097152 | tf_op jit(solution)/shard_map/all_to_all | solution.py:532
  38.8 0.8 dynamic-slice_bitcast_fusion.1.table_ref
  39.6 14.9 %all-to-all-done.parts_ref = f32[16,128,128]{2,1,0:T(8,128)S(1)} async-done(((f32[16,128,128]{2,1,0:T(8,128)}), f32[16,128,128]{2,1,0:T(8,128)S(1)}, u32[]{:S(2)}, u32[]{:S(2)}) %all-to-all-start) | async-done | bytes 1048608 | tf_op jit(solution)/shard_map/all_to_all | solution.py:532
  55.0 25.7 %all_to_all.20.parts_ref = f32[16,64,128]{2,1,0:T(8,128)S(1)} all-to-all(f32[16,64,128]{2,1,0:T(8,128)S(1)} %slab_forward.1), channel_id=1, replica_groups=mesh['slab'=16,'pencil'=16] {'slab'}, dimensions={0} | all-to-all | bytes 1048576 | tf_op jit(solution)/shard_map/all_to_all | solution.py:537
  80.7 1.3 %back.1 = (f32[64,128]{1,0:T(8,128)S(1)}, f32[16,32,128]{2,1,0:T(8,128)}) custom-call(f32[16,64,128]{2,1,0:T(8,128)S(1)} %all_to_all.20.parts_ref, bf16[2,2,2,32,512]{4,3,2,1,0:T(8,128)(2,1)S(1)} %copy-done.9), custom_call_target="tpu_custom_call" | custom-call | tf_op jit(solution)/shard_map/back/pallas_call | solution.py:454
  82.0 4.7 %all-to-all-start.2 = ((f32[16,32,128]{2,1,0:T(8,128)}), f32[16,32,128]{2,1,0:T(8,128)S(1)}, u32[]{:S(2)}, u32[]{:S(2)}) async-start(f32[16,32,128]{2,1,0:T(8,128)} %get-tuple-element.17), calls=%async_computation.2 | async-start | bytes 524288 | tf_op jit(solution)/shard_map/all_to_all | solution.py:541
  86.7 0.9 dynamic-slice_bitcast_fusion.table_ref
  87.5 10.7 %all-to-all-done.2.parts_ref = f32[16,32,128]{2,1,0:T(8,128)S(1)} async-done(((f32[16,32,128]{2,1,0:T(8,128)}), f32[16,32,128]{2,1,0:T(8,128)S(1)}, u32[]{:S(2)}, u32[]{:S(2)}) %all-to-all-start.2) | async-done | bytes 262176 | tf_op jit(solution)/shard_map/all_to_all | solution.py:541
  98.2 1.0 slab_backward.1
  99.2 6.4 %all-to-all-start.3 = ((f32[16,64,128]{2,1,0:T(8,128)}), f32[16,64,128]{2,1,0:T(8,128)S(1)}, u32[]{:S(2)}, u32[]{:S(2)}) async-start(f32[16,64,128]{2,1,0:T(8,128)} %slab_backward.1), calls=%async_computation.3 | async-start | bytes 1048576 | tf_op jit(solution)/shard_map/all_to_all | solution.py:546
  106.0 1.6 %copy-done.3 = bf16[16,256,256]{2,1,0:T(8,128)(2,1)S(1)} copy-done((bf16[16,256,256]{2,1,0:T(8,128)(2,1)S(1)}, bf16[16,256,256]{2,1,0:T(8,128)(2,1)}, u32[]{:S(2)}) %copy-start.3) | copy-done | bytes 2097176
  108.0 1.1 weight_grad.1
  109.1 6.3 %all-to-all-done.3.parts_ref = f32[16,64,128]{2,1,0:T(8,128)S(1)} async-done(((f32[16,64,128]{2,1,0:T(8,128)}), f32[16,64,128]{2,1,0:T(8,128)S(1)}, u32[]{:S(2)}, u32[]{:S(2)}) %all-to-all-start.3) | async-done | bytes 524320 | tf_op jit(solution)/shard_map/all_to_all | solution.py:546
  115.4 4.0 %output.1 = bf16[32,4,16,256]{3,2,1,0:T(8,128)(2,1)} custom-call(s32[1]{0:T(128)} %bitcast.position_ref, f32[544]{0:T(1024)S(1)} %copy-done.12, f32[16,64,128]{2,1,0:T(8,128)S(1)} %all-to-all-done.3.parts_ref, f32[16,128,256]{2,1,0:T(8,128)S(1)} %local.1.local_ref, bf16[96,256]{1,0:T(8,128)(2,1)S(1)} %copy-done.11), custom_call_target="tpu_custom_call" | custom-call | tf_op jit(solution)/shard_map/output/pallas_call | solution.py:454
  (40 shorter events, 4.6 us)
Async XLA Ops:
  0.6 23.9 %copy-start.12 = (f32[544]{0:T(1024)S(1)}, f32[544]{0:T(1024)}, u32[]{:S(2)}) copy-start(f32[544]{0:T(1024)} %constant.25.clone.phase_ref) | copy-start | bytes 6532
  0.6 1.2 %copy-start = (bf16[32,4,16,256]{3,2,1,0:T(8,128)(2,1)S(1)}, bf16[32,4,16,256]{3,2,1,0:T(8,128)(2,1)}, u32[]{:S(2)}) copy-start(bf16[32,4,16,256]{3,2,1,0:T(8,128)(2,1)} %pre_ref.3) | copy-start | bytes 3145732
  1.9 0.8 copy-start.5
  2.6 0.8 copy-start.7
  3.4 0.7 copy-start.13
  4.0 15.9 %copy-start.1 = (bf16[32,4,16,256]{3,2,1,0:T(8,128)(2,1)S(1)}, bf16[32,4,16,256]{3,2,1,0:T(8,128)(2,1)}, u32[]{:S(2)}) copy-start(bf16[32,4,16,256]{3,2,1,0:T(8,128)(2,1)} %pre_ref.3) | copy-start | bytes 3145732
  4.0 20.5 %copy-start.4 = (bf16[32,4,16,256]{3,2,1,0:T(8,128)(2,1)S(1)}, bf16[32,4,16,256]{3,2,1,0:T(8,128)(2,1)}, u32[]{:S(2)}) copy-start(bf16[32,4,16,256]{3,2,1,0:T(8,128)(2,1)} %input_ref.1) | copy-start | bytes 3145732
  4.1 20.5 %copy-start.10 = (bf16[64,256]{1,0:T(8,128)(2,1)S(1)}, bf16[64,256]{1,0:T(8,128)(2,1)}, u32[]{:S(2)}) copy-start(bf16[64,256]{1,0:T(8,128)(2,1)} %constant.26.clone.table_ref) | copy-start | bytes 98308
  6.7 10.8 %collective-permute-start = (f32[4,16,256]{2,1,0:T(8,128)S(1)}, f32[4,16,256]{2,1,0:T(8,128)S(1)}, u32[]{:S(2)}, u32[]{:S(2)}) collective-permute-start(f32[4,16,256]{2,1,0:T(8,128)S(1)} %get-tuple-element.12), channel_id=1, source_target_pairs={{0,16},{16,32},{32,48},{48,64},{64,80},{80,96},{96,112},{112,128},... | collective-permute-start | bytes 196616 | tf_op jit(solution)/shard_map/ppermute | solution.py:489
  10.5 7.0 %collective-permute-start.1 = (f32[4,16,256]{2,1,0:T(8,128)S(1)}, f32[4,16,256]{2,1,0:T(8,128)S(1)}, u32[]{:S(2)}, u32[]{:S(2)}) collective-permute-start(f32[4,16,256]{2,1,0:T(8,128)S(1)} %get-tuple-element.13), channel_id=1, source_target_pairs={{16,0},{32,16},{48,32},{64,48},{80,64},{96,80},{112,96},{128,112},... | collective-permute-start | bytes 196616 | tf_op jit(solution)/shard_map/ppermute | solution.py:490
  18.1 9.0 %collective-permute-start.2 = (f32[32,256]{1,0:T(8,128)}, f32[32,256]{1,0:T(8,128)S(1)}, u32[]{:S(2)}, u32[]{:S(2)}) collective-permute-start(f32[32,256]{1,0:T(8,128)} %get-tuple-element.14), channel_id=1, source_target_pairs={{0,1},{1,2},{2,3},{3,4},{4,5},{5,6},{6,7},{7,8},{8,9},{9,10},{10,1... | collective-permute-start | bytes 98312 | tf_op jit(solution)/shard_map/ppermute | solution.py:494
  19.9 7.2 %collective-permute-start.3 = (f32[32,256]{1,0:T(8,128)S(1)}, f32[32,256]{1,0:T(8,128)S(1)}, u32[]{:S(2)}, u32[]{:S(2)}) collective-permute-start(f32[32,256]{1,0:T(8,128)S(1)} %get-tuple-element.15), channel_id=1, source_target_pairs={{1,0},{2,1},{3,2},{4,3},{5,4},{6,5},{7,6},{8,7},{9,8},{10,9},{11,1... | collective-permute-start | bytes 98312 | tf_op jit(solution)/shard_map/ppermute | solution.py:495
  19.9 0.7 copy-start.14
  20.6 6.5 %copy-start.6 = (bf16[4,16,256]{2,1,0:T(8,128)(2,1)S(1)}, bf16[4,16,256]{2,1,0:T(8,128)(2,1)}, u32[]{:S(2)}) copy-start(bf16[4,16,256]{2,1,0:T(8,128)(2,1)} %coef_ref.5) | copy-start | bytes 98308
  20.6 6.5 %copy-start.8 = (bf16[4,16,256]{2,1,0:T(8,128)(2,1)S(1)}, bf16[4,16,256]{2,1,0:T(8,128)(2,1)}, u32[]{:S(2)}) copy-start(bf16[4,16,256]{2,1,0:T(8,128)(2,1)} %source_ref.5) | copy-start | bytes 98308
  30.3 1.3 %copy-start.2 = (bf16[16,256,256]{2,1,0:T(8,128)(2,1)}, bf16[16,256,256]{2,1,0:T(8,128)(2,1)S(1)}, u32[]{:S(2)}) copy-start(bf16[16,256,256]{2,1,0:T(8,128)(2,1)S(1)} %get-tuple-element.18.act_ref) | copy-start | bytes 6291460
  31.7 49.0 %copy-start.9 = (bf16[2,2,2,32,512]{4,3,2,1,0:T(8,128)(2,1)S(1)}, bf16[2,2,2,32,512]{4,3,2,1,0:T(8,128)(2,1)}, u32[]{:S(2)}) copy-start(bf16[2,2,2,32,512]{4,3,2,1,0:T(8,128)(2,1)} %weight_ref.1) | copy-start | bytes 786436
  31.7 22.9 %all-to-all-start = ((f32[16,128,128]{2,1,0:T(8,128)}), f32[16,128,128]{2,1,0:T(8,128)S(1)}, u32[]{:S(2)}, u32[]{:S(2)}) async-start(f32[16,128,128]{2,1,0:T(8,128)} %get-tuple-element.16), calls=%async_computation | async-start | bytes 2097152 | tf_op jit(solution)/shard_map/all_to_all | solution.py:532
  55.0 50.7 %copy-start.15 = (bf16[32,32]{1,0:T(8,128)(2,1)S(1)}, bf16[32,32]{1,0:T(8,128)(2,1)}, u32[]{:S(2)}) copy-start(bf16[32,32]{1,0:T(8,128)(2,1)} %param.17) | copy-start | bytes 6148
  82.0 16.2 %all-to-all-start.2 = ((f32[16,32,128]{2,1,0:T(8,128)}), f32[16,32,128]{2,1,0:T(8,128)S(1)}, u32[]{:S(2)}, u32[]{:S(2)}) async-start(f32[16,32,128]{2,1,0:T(8,128)} %get-tuple-element.17), calls=%async_computation.2 | async-start | bytes 524288 | tf_op jit(solution)/shard_map/all_to_all | solution.py:541
  99.2 16.1 %all-to-all-start.3 = ((f32[16,64,128]{2,1,0:T(8,128)}), f32[16,64,128]{2,1,0:T(8,128)S(1)}, u32[]{:S(2)}, u32[]{:S(2)}) async-start(f32[16,64,128]{2,1,0:T(8,128)} %slab_backward.1), calls=%async_computation.3 | async-start | bytes 1048576 | tf_op jit(solution)/shard_map/all_to_all | solution.py:546
  105.9 1.6 %copy-start.3 = (bf16[16,256,256]{2,1,0:T(8,128)(2,1)S(1)}, bf16[16,256,256]{2,1,0:T(8,128)(2,1)}, u32[]{:S(2)}) copy-start(bf16[16,256,256]{2,1,0:T(8,128)(2,1)} %copy-done.2) | copy-start | bytes 6291460
  107.5 7.8 %copy-start.11 = (bf16[96,256]{1,0:T(8,128)(2,1)S(1)}, bf16[96,256]{1,0:T(8,128)(2,1)}, u32[]{:S(2)}) copy-start(bf16[96,256]{1,0:T(8,128)(2,1)} %constant.27.clone.table_ref) | copy-start | bytes 147460

commit v2 on v1

--- a/solution.py
+++ b/solution.py
@@ -18,7 +18,10 @@
 KZ = 16
 LANES = CX * C
 CELLS = float(NX * NY * NZ)
-VMEM_LIMIT = 40 * 1024 * 1024
+VMEM_LIMIT = 24 * 1024 * 1024
+PITCH = 68
+Y_PITCH = LANES + 8
+CHUNKS = 4
 
 
 def split_2(table):
@@ -85,13 +88,45 @@
     return bell, poly * t * bell
 
 
-def field_kernel(pre_ref, coef_ref, source_ref, proj_ref, field_ref, up_ref, down_ref):
+def field_kernel(
+    pre_hbm,
+    coef_hbm,
+    source_hbm,
+    proj_hbm,
+    field_ref,
+    up_ref,
+    down_ref,
+    proj_tile_ref,
+    pre_ref,
+    coef_ref,
+    source_ref,
+    proj_ref,
+    sems,
+):
+    size = C // CHUNKS
+    copies = [pltpu.make_async_copy(proj_hbm, proj_ref, sems.at[CHUNKS])]
+    for i in range(CHUNKS):
+        part = pl.ds(i * size, size)
+        copies.append(pltpu.make_async_copy(pre_hbm.at[part], pre_ref.at[part], sems.at[i]))
+    copies.append(pltpu.make_async_copy(coef_hbm, coef_ref, sems.at[CHUNKS + 1]))
+    copies.append(pltpu.make_async_copy(source_hbm, source_ref, sems.at[CHUNKS + 2]))
+    for copy in copies:
+        copy.start()
+    copies[0].wait()
+    for c in range(C):
+        proj_tile_ref[c : c + 1, :] = jnp.full((1, 128), proj_ref[c], F32)
+
     def add_channel(c, total):
         values = pre_ref[c].astype(F32)
         _, tail = normal_tail(values)
         return total + proj_ref[c] * (jnp.maximum(values, 0.0) - jnp.abs(values) * tail)
 
-    total = lax.fori_loop(0, C, add_channel, jnp.zeros((CX, CY, NZ), F32), unroll=2)
+    total = jnp.zeros((CX, CY, NZ), F32)
+    for i in range(CHUNKS):
+        copies[1 + i].wait()
+        total = lax.fori_loop(i * size, (i + 1) * size, add_channel, total, unroll=2)
+    copies[-2].wait()
+    copies[-1].wait()
     field_ref[...] = total
     up_ref[0:2] = total[2:4]
     down_ref[0:2] = total[0:2]
@@ -106,11 +141,12 @@
         values = pre_ref[c].astype(F32)
         bell, tail = normal_tail(values)
         below = jnp.where(values >= 0.0, 1.0 - tail, tail)
-        slope = proj_ref[c] * (below + values * (bell * (1.0 / math.sqrt(2.0 * math.pi))))
+        slope = below + values * (bell * (1.0 / math.sqrt(2.0 * math.pi)))
+        weight = proj_ref[pl.ds(c, 1), :]
         for x in range(CX):
             for side in range(2):
-                piece = slope[x, :, side * 128 : (side + 1) * 128]
-                slope_ref[side, pl.ds(x * C + c, CY, stride=LANES), :] = piece
+                piece = slope[x, :, side * 128 : (side + 1) * 128] * weight
+                slope_ref[side, pl.ds(x * C + c, CY, stride=Y_PITCH), :] = piece
         return carry
 
     lax.fori_loop(0, C, one_channel, 0, unroll=2)
@@ -124,7 +160,7 @@
     return lax.dot_general(left, right, (((0,), (0,)), ((), ())), preferred_element_type=F32)
 
 
-def pencil_forward(modes_ref, phase_ref, position, out_ref, base):
+def pencil_forward(modes_ref, phase_ref, position, out_refs):
     for half in range(2):
         sums, diffs = [], []
         for part in range(2):
@@ -147,27 +183,54 @@
                 if k < 16:
                     results.append((k, even[0] - odd[1], even[1] + odd[0], w_sin))
             for index, real, imag, sin in results:
-                row = base + (index % 2) * 32 + 8 * half
-                out_ref[index // 2, pl.ds(row, 8), :] = w_cos * real + sin * imag
-                out_ref[index // 2, pl.ds(row + KZ, 8), :] = w_cos * imag - sin * real
-
-
-def input_kernel(position_ref, phase_ref, input_ref, table_ref, out_ref, rows_ref, modes_ref):
+                row = (index % 2) * 32 + 8 * half
+                out_ref = out_refs[index // 2 % 2]
+                out_ref[index // 4, pl.ds(row, 8), :] = w_cos * real + sin * imag
+                out_ref[index // 4, pl.ds(row + KZ, 8), :] = w_cos * imag - sin * real
+
+
+def by_core(position, function, own_ref, other_ref):
+    @pl.when(position % 2 == 0)
+    def _():
+        function((own_ref, other_ref))
+
+    @pl.when(position % 2 == 1)
+    def _():
+        function((other_ref, own_ref))
+
+
+def input_kernel(
+    position_ref,
+    phase_ref,
+    input_ref,
+    table_hbm,
+    own_ref,
+    other_ref,
+    rows_ref,
+    modes_ref,
+    table_ref,
+    sem,
+):
+    copy = pltpu.make_async_copy(table_hbm, table_ref, sem)
+    copy.start()
     for side in range(2):
-        piece = input_ref[:, :, :, side * 128 : (side + 1) * 128]
-        rows_ref[side] = piece.astype(F32).reshape(C * CX * CY, 128)
+        for c in range(C):
+            piece = input_ref[c, :, :, side * 128 : (side + 1) * 128].astype(F32)
+            rows_ref[side, c * PITCH : c * PITCH + CX * CY, :] = piece.reshape(CX * CY, 128)
+    copy.wait()
     for y in range(CY):
         sides = [
             jnp.concatenate(
-                [rows_ref[side, pl.ds(x * CY + y, C, stride=CX * CY), :] for x in range(CX)],
-                axis=0,
+                [rows_ref[side, pl.ds(x * CY + y, C, stride=PITCH), :] for x in range(CX)], axis=0
             )
             for side in range(2)
         ]
         values = jnp.concatenate(sides, axis=1).astype(BF16)
         both = nt_dot(table_ref[...], values)
         modes_ref[y] = both[:32] + both[32:]
-    pencil_forward(modes_ref, phase_ref, position_ref[0], out_ref, 0)
+    position = position_ref[0]
+    forward = functools.partial(pencil_forward, modes_ref, phase_ref, position)
+    by_core(position, forward, own_ref, other_ref)
 
 
 def pack_kernel(field_ref, coef_ref, source_ref, before_ref, after_ref, up_ref, down_ref):
@@ -198,6 +261,17 @@
     return 0.5 * (values[:-2] + values[2:]) + values[1:-1]
 
 
+def act_parts(slope_ref, grad_ref, y):
+    grads = []
+    for x in range(CX):
+        rows = slice(y * Y_PITCH + x * C, y * Y_PITCH + (x + 1) * C)
+        slope = jnp.concatenate([slope_ref[0, rows, :], slope_ref[1, rows, :]], axis=1)
+        grads.append(slope * grad_ref[x, 8 + y : 9 + y, :])
+    act = jnp.concatenate(grads, axis=0)
+    high = act.astype(BF16)
+    return high, (act - high.astype(F32)).astype(BF16)
+
+
 def grad_kernel(
     position_ref,
     phase_ref,
@@ -209,16 +283,19 @@
     low_ref,
     high_ref,
     slope_ref,
-    table_ref,
-    input_part_ref,
-    out_ref,
-    act_ref,
+    table_hbm,
+    own_ref,
+    other_ref,
+    grad_ref,
     wide_field,
     wide_coef,
     wide_source,
-    grad_ref,
     modes_ref,
+    table_ref,
+    sem,
 ):
+    copy = pltpu.make_async_copy(table_hbm, table_ref, sem)
+    copy.start()
     own = slice(8, 24)
     wide_field[...] = jnp.zeros_like(wide_field)
     wide_coef[...] = jnp.zeros_like(wide_coef)
@@ -229,9 +306,9 @@
     for x in range(8):
         wide_field[x, 6:8, :] = low_ref[2 * x : 2 * x + 2, :]
         wide_field[x, 24:26, :] = high_ref[2 * x : 2 * x + 2, :]
-    for wide, own_ref, part, base in ((wide_coef, coef_ref, 2, 16), (wide_source, source_ref, 3, 22)):
+    for wide, cells, part, base in ((wide_coef, coef_ref, 2, 16), (wide_source, source_ref, 3, 22)):
         wide[0, own, :] = before_ref[part]
-        wide[1:5, own, :] = own_ref[...].astype(F32)
+        wide[1:5, own, :] = cells[...].astype(F32)
         wide[5, own, :] = after_ref[part]
         for x in range(6):
             wide[x, 7:8, :] = low_ref[base + x : base + x + 1, :]
@@ -240,26 +317,25 @@
     center = field[1:7]
     residual = (16.0 / 3.0 - wide_coef[...]) * center - (2.0 / 3.0) * smooth(field) - wide_source[...]
     grad_ref[...] = (16.0 / 3.0 - wide_coef[1:5]) * residual[1:5] - (2.0 / 3.0) * smooth(residual)
+    copy.wait()
     for y in range(CY):
-        grads = []
-        for x in range(CX):
-            rows = slice(y * LANES + x * C, y * LANES + (x + 1) * C)
-            slope = jnp.concatenate([slope_ref[0, rows, :], slope_ref[1, rows, :]], axis=1)
-            grads.append(slope * grad_ref[x, 8 + y : 9 + y, :])
-        act = jnp.concatenate(grads, axis=0)
-        high = act.astype(BF16)
-        low = (act - high.astype(F32)).astype(BF16)
-        act_ref[y, 0:LANES, :] = high
-        act_ref[y, LANES : 2 * LANES, :] = low
+        high, low = act_parts(slope_ref, grad_ref, y)
         both = nt_dot(table_ref[...], high)
         modes_ref[y] = both[:32] + both[32:] + nt_dot(table_ref[0:32, :], low)
-    out_ref[:, 0:64, :] = input_part_ref[...]
-    pencil_forward(modes_ref, phase_ref, position_ref[0], out_ref, 64)
-
-
-def local_kernel(pointwise_ref, act_ref, out_ref):
+    position = position_ref[0]
+    forward = functools.partial(pencil_forward, modes_ref, phase_ref, position)
+    by_core(position, forward, own_ref, other_ref)
+
+
+def combine_kernel(own_in_ref, got_in_ref, own_ref, got_ref, out_ref):
+    out_ref[:, 0:64, :] = own_in_ref[...] + got_in_ref[...]
+    out_ref[:, 64:128, :] = own_ref[...] + got_ref[...]
+
+
+def local_kernel(pointwise_ref, slope_ref, grad_ref, out_ref):
     for y in range(CY):
-        out_ref[y] = jnp.dot(pointwise_ref[...], act_ref[y], preferred_element_type=F32)
+        act = jnp.concatenate(act_parts(slope_ref, grad_ref, y), axis=0)
+        out_ref[y] = jnp.dot(pointwise_ref[...], act, preferred_element_type=F32)
 
 
 def slab_forward_kernel(parts_ref, table_ref, out_ref):
@@ -269,7 +345,7 @@
             for part in range(2):
                 rows = pl.ds(block * 32 + part * KZ + 8 * half, 8)
                 total = parts_ref[0, rows, :]
-                for source in range(1, N):
+                for source in range(1, N // 2):
                     total = total + parts_ref[source, rows, :]
                 pieces.append([total] + [pltpu.roll(total, 32 * d, 1) for d in range(1, 4)])
             for owner in range(N):
@@ -364,51 +440,64 @@
                 result = totals[part][0]
                 for d in range(1, 4):
                     result = result + pltpu.roll(totals[part][d], 32 * d, 1)
-                for device in range(N):
+                for device in range(N // 2):
                     out_ref[device, pl.ds(ky * 32 + part * KZ + 8 * half, 8), :] = result
 
 
-def output_kernel(
-    position_ref, phase_ref, parts_ref, local_ref, table_ref, out_ref, modes_ref, rows_ref
-):
-    position = position_ref[0]
+def turn_modes(phase_ref, position, modes_ref, parts_refs):
+    def turned(index, w_cos, w_sin, rows):
+        ref = parts_refs[index // 2 % 2]
+        row = (index % 2) * 32 + rows
+        real = ref[index // 4, pl.ds(row, 8), :]
+        imag = ref[index // 4, pl.ds(row + KZ, 8), :]
+        return w_cos * real - w_sin * imag, w_cos * imag + w_sin * real
+
     for half in range(2):
-        evens, odds = [], []
         for k in range(17):
             w_cos = phase_ref[position * 34 + k]
             w_sin = phase_ref[position * 34 + 17 + k]
-
-            def turned(index, sin):
-                row = (index % 2) * 32 + 8 * half
-                real = parts_ref[index // 2, pl.ds(row, 8), :]
-                imag = parts_ref[index // 2, pl.ds(row + KZ, 8), :]
-                return w_cos * real - sin * imag, w_cos * imag + sin * real
-
             if k == 0:
-                evens.append(turned(0, w_sin))
-                odds.append(None)
+                even = turned(0, w_cos, w_sin, 8 * half)
+                odd = None
             elif k == 16:
-                real, imag = turned(16, -w_sin)
-                evens.append((real, imag))
-                odds.append((-real, -imag))
+                even = turned(16, w_cos, -w_sin, 8 * half)
+                odd = [-part for part in even]
             else:
-                plus, minus = turned(k, w_sin), turned(32 - k, -w_sin)
-                evens.append((plus[0] + minus[0], plus[1] + minus[1]))
-                odds.append((plus[0] - minus[0], plus[1] - minus[1]))
-            modes_ref[0, k, 0] = evens[-1][0]
-            modes_ref[0, k, 1] = evens[-1][1]
-            if k:
-                modes_ref[1, k, 0] = odds[-1][0]
-                modes_ref[1, k, 1] = odds[-1][1]
+                plus = turned(k, w_cos, w_sin, 8 * half)
+                minus = turned(32 - k, w_cos, -w_sin, 8 * half)
+                even = [p + m for p, m in zip(plus, minus)]
+                odd = [p - m for p, m in zip(plus, minus)]
+            for part in range(2):
+                modes_ref[half, 0, k, part] = even[part]
+                if odd is not None:
+                    modes_ref[half, 1, k, part] = odd[part]
+
+
+def output_kernel(
+    position_ref,
+    phase_ref,
+    own_ref,
+    other_ref,
+    local_ref,
+    table_ref,
+    out_ref,
+    modes_ref,
+    rows_ref,
+    flat_ref,
+):
+    position = position_ref[0]
+    turn = functools.partial(turn_modes, phase_ref, position, modes_ref)
+    by_core(position, turn, own_ref, other_ref)
+    for half in range(2):
         for y in range(8):
-            even = [modes_ref[0, 0, 0], modes_ref[0, 0, 1]]
+            even = [modes_ref[half, 0, 0, 0], modes_ref[half, 0, 0, 1]]
             odd = [None, None]
             for k in range(1, 17):
                 angle = 2.0 * math.pi * k * (y - 7.5) / NY
                 cos, sin = math.cos(angle), math.sin(angle)
                 for part in range(2):
-                    even[part] = even[part] + cos * modes_ref[0, k, part]
-                    term = sin * modes_ref[1, k, part]
+                    even[part] = even[part] + cos * modes_ref[half, 0, k, part]
+                    term = sin * modes_ref[half, 1, k, part]
                     odd[part] = term if odd[part] is None else odd[part] + term
             rows = pl.ds(8 * half, 8)
             more = pl.ds(KZ + 8 * half, 8)
@@ -416,9 +505,6 @@
             rows_ref[y, more, :] = even[1] + odd[0]
             rows_ref[15 - y, rows, :] = even[0] + odd[1]
             rows_ref[15 - y, more, :] = even[1] - odd[0]
-
-
-def finish_kernel(rows_ref, local_ref, table_ref, out_ref, flat_ref):
     for y in range(CY):
         values = rows_ref[y]
         high = values.astype(BF16)
@@ -428,26 +514,24 @@
         for x in range(CX):
             for side in range(2):
                 piece = result[x * C : (x + 1) * C, side * 128 : (side + 1) * 128]
-                flat_ref[side, pl.ds(x * CY + y, C, stride=CX * CY), :] = piece
+                flat_ref[side, pl.ds(x * CY + y, C, stride=PITCH), :] = piece
     for side in range(2):
-        piece = flat_ref[side].astype(BF16).reshape(C, CX, CY, 128)
-        out_ref[:, :, :, side * 128 : (side + 1) * 128] = piece
-
-
-def last_kernel(
-    position_ref, phase_ref, parts_ref, local_ref, table_ref, out_ref, modes_ref, rows_ref, flat_ref
-):
-    output_kernel(
-        position_ref, phase_ref, parts_ref, local_ref, table_ref, out_ref, modes_ref, rows_ref
-    )
-    finish_kernel(rows_ref, local_ref, table_ref, out_ref, flat_ref)
-
-
-def call(kernel, name, out, scratch=(), scalars=()):
+        for c in range(C):
+            piece = flat_ref[side, c * PITCH : c * PITCH + CX * CY].astype(BF16)
+            out_ref[c, :, :, side * 128 : (side + 1) * 128] = piece.reshape(CX, CY, 128)
+
+
+def call(kernel, name, out, scratch=(), scalars=(), hbm=()):
     def run(*args):
+        args = [
+            pltpu.with_memory_space_constraint(arg, pltpu.HBM) if i in hbm else arg
+            for i, arg in enumerate(args)
+        ]
         single = not isinstance(out, list)
         specs = [
-            pl.BlockSpec(memory_space=pltpu.SMEM if i in scalars else pltpu.VMEM)
+            pl.BlockSpec(
+                memory_space=pltpu.SMEM if i in scalars else pltpu.HBM if i in hbm else pltpu.VMEM
+            )
             for i in range(len(args))
         ]
         shapes = [jax.ShapeDtypeStruct(*o) for o in ([out] if single else out)]
@@ -456,7 +540,7 @@
             out_shape=shapes,
             in_specs=specs,
             out_specs=[pl.BlockSpec(memory_space=pltpu.VMEM)] * len(shapes),
-            scratch_shapes=[pltpu.VMEM(*s) for s in scratch],
+            scratch_shapes=[pltpu.VMEM(*s) if isinstance(s, tuple) else s for s in scratch],
             compiler_params=pltpu.CompilerParams(vmem_limit_bytes=VMEM_LIMIT),
             name=name,
         )(*args)
@@ -470,6 +554,8 @@
 ):
     up = [(i, (i + 1) % N) for i in range(N)]
     down = [(j, i) for i, j in up]
+    swap = [(i, i ^ 1) for i in range(N)]
+    same_core = [[i for i in range(N) if i % 2 == core] for core in range(2)]
     slab = lax.axis_index("slab")
     pencil = lax.axis_index("pencil").reshape(1)
     phases = jnp.asarray(PENCIL_PHASES)
@@ -480,41 +566,60 @@
     pointwise_4 = jnp.kron(jnp.eye(CX, dtype=BF16), pointwise)
     pointwise_8 = jnp.concatenate([pointwise_4, pointwise_4], axis=1)
 
-    field, edge_up, edge_down = call(
+    edge = ((4, CY, NZ), F32)
+    field, edge_up, edge_down, proj_tile = call(
         field_kernel,
         "field",
-        [((CX, CY, NZ), F32), ((4, CY, NZ), F32), ((4, CY, NZ), F32)],
-        scalars=(3,),
+        [((CX, CY, NZ), F32), edge, edge, ((C, 128), F32)],
+        scratch=[
+            ((C, CX, CY, NZ), BF16),
+            ((CX, CY, NZ), BF16),
+            ((CX, CY, NZ), BF16),
+            pltpu.SMEM((C,), F32),
+            pltpu.SemaphoreType.DMA((CHUNKS + 3,)),
+        ],
+        hbm=(0, 1, 2, 3),
     )(pre_activation, coefficient, source, projection)
     before = lax.ppermute(edge_up, "slab", up)
     after = lax.ppermute(edge_down, "slab", down)
+    slope = call(slope_kernel, "slope", ((2, CY * Y_PITCH, 128), F32))(pre_activation, proj_tile)
+    half_modes = ((N // 2, 64, LANES), F32)
+    own_in, other_in = call(
+        input_kernel,
+        "input_modes",
+        [half_modes, half_modes],
+        scratch=[
+            ((2, C * PITCH, 128), F32),
+            ((CY, 32, LANES), F32),
+            (DEPTH_FORWARD.shape, BF16),
+            pltpu.SemaphoreType.DMA(()),
+        ],
+        scalars=(0, 1),
+        hbm=(3,),
+    )(pencil, phases, layer_input, depth_forward)
+    before, after, slope, own_in, other_in = lax.optimization_barrier(
+        (before, after, slope, own_in, other_in)
+    )
+    got_in = lax.ppermute(other_in, "pencil", swap)
     side_up, side_down = call(pack_kernel, "pack", [((32, NZ), F32), ((32, NZ), F32)])(
         field, coefficient, source, before, after
     )
     low = lax.ppermute(side_up, "pencil", up)
     high = lax.ppermute(side_down, "pencil", down)
-    slope = call(slope_kernel, "slope", ((2, CY * LANES, 128), F32), scalars=(1,))(
-        pre_activation, projection
-    )
-    input_part = call(
-        input_kernel,
-        "input_modes",
-        ((N, 64, LANES), F32),
-        scratch=[((2, C * CX * CY, 128), F32), ((CY, 32, LANES), F32)],
-        scalars=(0, 1),
-    )(pencil, phases, layer_input, depth_forward)
-    to_pencil, act = call(
+    own, other, grad = call(
         grad_kernel,
         "grad_modes",
-        [((N, 128, LANES), F32), ((CY, 2 * LANES, NZ), BF16)],
+        [half_modes, half_modes, ((CX, 32, NZ), F32)],
         scratch=[
             ((8, 32, NZ), F32),
             ((6, 32, NZ), F32),
             ((6, 32, NZ), F32),
-            ((4, 32, NZ), F32),
             ((CY, 32, LANES), F32),
+            (DEPTH_FORWARD.shape, BF16),
+            pltpu.SemaphoreType.DMA(()),
         ],
         scalars=(0, 1),
+        hbm=(10,),
     )(
         pencil,
         phases,
@@ -527,10 +632,16 @@
         high,
         slope,
         depth_forward,
-        input_part,
-    )
-    from_pencil = lax.all_to_all(to_pencil, "pencil", 0, 0, tiled=True)
-    local = call(local_kernel, "local", ((CY, LANES, NZ), F32))(pointwise_8, act)
+    )
+    got = lax.ppermute(other, "pencil", swap)
+    to_pencil = call(combine_kernel, "combine", ((N // 2, 128, LANES), F32))(
+        own_in, got_in, own, got
+    )
+    from_pencil = lax.all_to_all(
+        to_pencil, "pencil", 0, 0, axis_index_groups=same_core, tiled=True
+    )
+    local = call(local_kernel, "local", ((CY, LANES, NZ), F32))(pointwise_8, slope, grad)
+    from_pencil, local = lax.optimization_barrier((from_pencil, local))
     to_slab = call(slab_forward_kernel, "slab_forward", ((N, 64, LANES), F32))(
         from_pencil, slab_forward
     )
@@ -540,21 +651,20 @@
     )
     from_slab = lax.all_to_all(to_slab, "slab", 0, 0, tiled=True)
     weight_grad = call(weight_grad_kernel, "weight_grad", (spectral_weight.shape, BF16))(modes)
-    to_pencil = call(slab_backward_kernel, "slab_backward", ((N, 64, LANES), F32))(
-        from_slab, slab_backward
-    )
-    from_pencil = lax.all_to_all(to_pencil, "pencil", 0, 0, tiled=True)
+    to_pencil = call(slab_backward_kernel, "slab_backward", half_modes)(from_slab, slab_backward)
+    own = lax.all_to_all(to_pencil, "pencil", 0, 0, axis_index_groups=same_core, tiled=True)
+    other = lax.ppermute(own, "pencil", swap)
     input_grad = call(
-        last_kernel,
+        output_kernel,
         "output",
         ((C, CX, CY, NZ), BF16),
         scratch=[
-            ((2, 17, 2, 8, LANES), F32),
+            ((2, 2, 17, 2, 8, LANES), F32),
             ((CY, 32, LANES), F32),
-            ((2, C * CX * CY, 128), F32),
+            ((2, C * PITCH, 128), F32),
         ],
         scalars=(0, 1),
-    )(pencil, phases, from_pencil, local, depth_backward)
+    )(pencil, phases, own, other, local, depth_backward)
     return (input_grad, weight_grad)
 
 

time: 120 us -> 105 us (0.88)
  waiting for transfers between devices: 33.5 us -> 17.7 us
  blocking collectives: 25.7 us -> 32 us
  Pallas kernels: 21.2 us -> 17.9 us
  local copies, waits for them, and re-layouts: 8.83 us -> 5.72 us
    all_to_all x2 -> x1, waiting for transfers between devices: 21.2 us -> 6.18 us  [shards(): lax.all_to_all(to_pencil, 'pencil', 0, 0, axis_index_groups=same_core, ti...]
    ppermute x0 -> x3, starting transfers between devices: none -> 9.99 us  [the longest x1 4.74 us: shards(): other = lax.ppermute(own, 'pencil', swap)]
    all_to_all x0 -> x1, blocking collectives: none -> 9.35 us  [shards(): lax.all_to_all(to_pencil, 'pencil', 0, 0, axis_index_groups=same_core, ti...]
    all_to_all x2 -> x1, starting transfers between devices: 13.6 us -> 5.11 us  [shards(): lax.all_to_all(to_pencil, 'pencil', 0, 0, axis_index_groups=same_core, ti...]
    pallas_call x11 -> x12, Pallas kernels: 21.2 us -> 17.9 us  [run(): pl.pallas_call(kernel, out_shape=shapes, in_specs=specs, out_specs=[pl.Bl...]
    unnamed x32 -> x24, local copies, waits for them, and re-layouts: 7.01 us -> 3.9 us
    all_to_all x1, blocking collectives: 25.7 us -> 22.6 us  [shards(): from_slab = lax.all_to_all(to_slab, 'slab', 0, 0, tiled=True)]
    ppermute x1, waiting for transfers between devices: 1.57 us -> 0.01 us  [shards(): before = lax.ppermute(edge_up, 'slab', up)]
  transfers between devices with their start and end apart: 7 -> 9, of which waited for: 4 -> 4; matrix products, arithmetic and copies ran while one was open for 2% -> 2% of each run, Pallas kernels for 7% -> 8%
where the time goes in v2:
time: 105 us; the launch traced here: 104 us
  blocking collectives  32 us (30%)
  starting transfers between devices  29.8 us (28%)
  Pallas kernels  17.9 us (17%)
  waiting for transfers between devices  17.7 us (17%)
  local copies, waits for them, and re-layouts  5.72 us (5%)
    all_to_all x1, blocking collectives, shards(): from_slab = lax.all_to_all(to_slab, 'slab', 0, 0, tiled=True)  22.6 us
    pallas_call x12, Pallas kernels, run(): pl.pallas_call(kernel, out_shape=shapes, in_specs=specs, out_specs=[pl.Bl...  17.9 us
    all_to_all x1, waiting for transfers between devices, shards(): from_slab = lax.all_to_all(to_slab, 'slab', 0, 0, tiled=True)  10.3 us
    all_to_all x1, blocking collectives, shards(): lax.all_to_all(to_pencil, 'pencil', 0, 0, axis_index_groups=same_core, ti...  9.35 us
    all_to_all x1, waiting for transfers between devices, shards(): lax.all_to_all(to_pencil, 'pencil', 0, 0, axis_index_groups=same_core, ti...  6.18 us
    ppermute x1, starting transfers between devices, shards(): after = lax.ppermute(edge_down, 'slab', down)  5.3 us
    all_to_all x1, starting transfers between devices, shards(): lax.all_to_all(to_pencil, 'pencil', 0, 0, axis_index_groups=same_core, ti...  5.11 us
    ppermute x1, starting transfers between devices, shards(): other = lax.ppermute(own, 'pencil', swap)  4.74 us
  transfers between devices with their start and end apart: 9, of which 4 were waited for; matrix products, arithmetic and copies ran while one was open for 2% of the time, Pallas kernels for 8%

profile of v2, /device:TPU:1, one launch (start us, length us, event | category | flops | bytes accessed | tf_op | source)
XLA Modules:
  0.0 104.0 jit_solution(11740416325704822847)
XLA Ops:
  0.7 3.9 %field.1 = (f32[4,16,256]{2,1,0:T(8,128)S(1)}, f32[4,16,256]{2,1,0:T(8,128)}, f32[4,16,256]{2,1,0:T(8,128)}, f32[32,128]{1,0:T(8,128)S(1)}) custom-call(bf16[32,4,16,256]{3,2,1,0:T(8,128)(2,1)} %pre_ref.1, bf16[4,16,256]{2,1,0:T(8,128)(2,1)} %coef_ref.3, bf16[4,16,256]{2,1,0:T(8,128)(2,1)} %source_ref.3, f32[32]{0:T(128)} %proj_hbm.1), custom_call_target="tpu_custom_call" | custom-call | tf_op jit(solution)/shard_map/field/pallas_call | solution.py:538
  5.1 3.7 %collective-permute-start = (f32[4,16,256]{2,1,0:T(8,128)}, f32[4,16,256]{2,1,0:T(8,128)S(1)}, u32[]{:S(2)}, u32[]{:S(2)}) collective-permute-start(f32[4,16,256]{2,1,0:T(8,128)} %get-tuple-element.22), channel_id=1, source_target_pairs={{0,16},{16,32},{32,48},{48,64},{64,80},{80,96},{96,112},{112,128},... | collective-permute-start | bytes 196616 | tf_op jit(solution)/shard_map/ppermute | solution.py:583
  8.9 5.3 %collective-permute-start.1 = (f32[4,16,256]{2,1,0:T(8,128)}, f32[4,16,256]{2,1,0:T(8,128)S(1)}, u32[]{:S(2)}, u32[]{:S(2)}) collective-permute-start(f32[4,16,256]{2,1,0:T(8,128)} %get-tuple-element.23), channel_id=1, source_target_pairs={{16,0},{32,16},{48,32},{64,48},{80,64},{96,80},{112,96},{128,112},... | collective-permute-start | bytes 196616 | tf_op jit(solution)/shard_map/ppermute | solution.py:584
  14.2 1.2 %copy-done.2 = bf16[32,4,16,256]{3,2,1,0:T(8,128)(2,1)S(1)} copy-done((bf16[32,4,16,256]{3,2,1,0:T(8,128)(2,1)S(1)}, bf16[32,4,16,256]{3,2,1,0:T(8,128)(2,1)}, u32[]{:S(2)}) %copy-start.2) | copy-done | bytes 1048600
  16.1 2.2 %slope.1.slope_ref = f32[2,2176,128]{2,1,0:T(8,128)S(1)} custom-call(bf16[32,4,16,256]{3,2,1,0:T(8,128)(2,1)S(1)} %copy-done.2, f32[32,128]{1,0:T(8,128)S(1)} %copy-done.10), custom_call_target="tpu_custom_call" | custom-call | tf_op jit(solution)/shard_map/slope/pallas_call | solution.py:538
  18.3 2.2 %input_modes.1 = (f32[8,64,128]{2,1,0:T(8,128)S(1)}, f32[8,64,128]{2,1,0:T(8,128)S(1)}) custom-call(s32[1]{0:T(128)} %bitcast.position_ref, f32[544]{0:T(1024)S(1)} %copy-done.8, bf16[32,4,16,256]{3,2,1,0:T(8,128)(2,1)S(1)} %copy-done.3, bf16[64,256]{1,0:T(8,128)(2,1)} %constant.26.clone.table_hbm), custom_call_target="tpu_custom_call" | custom-call | tf_op jit(solution)/shard_map/input_modes/pallas_call | solution.py:538
  20.6 1.3 %collective-permute-start.3 = (f32[32,256]{1,0:T(8,128)S(1)}, f32[32,256]{1,0:T(8,128)S(1)}, u32[]{:S(2)}, u32[]{:S(2)}) collective-permute-start(f32[32,256]{1,0:T(8,128)S(1)} %get-tuple-element.32), channel_id=1, source_target_pairs={{0,1},{1,2},{2,3},{3,4},{4,5},{5,6},{6,7},{7,8},{8,9},{9,10},{10,1... | collective-permute-start | bytes 98312 | tf_op jit(solution)/shard_map/ppermute | solution.py:607
  21.9 3.6 %collective-permute-start.2 = (f32[8,64,128]{2,1,0:T(8,128)S(1)}, f32[8,64,128]{2,1,0:T(8,128)S(1)}, u32[]{:S(2)}, u32[]{:S(2)}) collective-permute-start(f32[8,64,128]{2,1,0:T(8,128)S(1)} %get-tuple-element.28), channel_id=1, source_target_pairs={{0,1},{1,0},{2,3},{3,2},{4,5},{5,4},{6,7},{7,6},{8,9},{9,8},{10,11... | collective-permute-start | bytes 786440 | tf_op jit(solution)/shard_map/ppermute | solution.py:603
  25.5 2.8 %grad_modes.1 = (f32[8,64,128]{2,1,0:T(8,128)S(1)}, f32[8,64,128]{2,1,0:T(8,128)S(1)}, f32[4,32,256]{2,1,0:T(8,128)S(1)}) custom-call(s32[1]{0:T(128)} %bitcast.position_ref, f32[544]{0:T(1024)S(1)} %copy-done.8, f32[4,16,256]{2,1,0:T(8,128)S(1)} %get-tuple-element.29.field_ref, bf16[4,16,256]{2,1,0:T(8,128)(2,1)S(1)} %copy-done.4, ...), custom_call_target="tpu_custom_call" | custom-call | tf_op jit(solution)/shard_map/grad_modes/pallas_call | solution.py:538
  28.3 1.7 %collective-permute-start.5 = (f32[8,64,128]{2,1,0:T(8,128)S(1)}, f32[8,64,128]{2,1,0:T(8,128)S(1)}, u32[]{:S(2)}, u32[]{:S(2)}) collective-permute-start(f32[8,64,128]{2,1,0:T(8,128)S(1)} %get-tuple-element.36), channel_id=1, source_target_pairs={{0,1},{1,0},{2,3},{3,2},{4,5},{5,4},{6,7},{7,6},{8,9},{9,8},{10,11... | collective-permute-start | bytes 786440 | tf_op jit(solution)/shard_map/ppermute | solution.py:636
  30.0 1.2 %collective-permute-done.5.got_ref = f32[8,64,128]{2,1,0:T(8,128)S(1)} collective-permute-done((f32[8,64,128]{2,1,0:T(8,128)S(1)}, f32[8,64,128]{2,1,0:T(8,128)S(1)}, u32[]{:S(2)}, u32[]{:S(2)}) %collective-permute-start.5) | collective-permute-done | bytes 262176 | tf_op jit(solution)/shard_map/ppermute | solution.py:636
  32.0 5.1 %all-to-all-start = ((f32[8,128,128]{2,1,0:T(8,128)}), f32[8,128,128]{2,1,0:T(8,128)S(1)}, u32[]{:S(2)}, u32[]{:S(2)}) async-start(f32[8,128,128]{2,1,0:T(8,128)} %combine.1), calls=%async_computation | async-start | bytes 1048576 | tf_op jit(solution)/shard_map/all_to_all | solution.py:640
  37.4 0.9 dynamic-slice_bitcast_fusion.1.table_ref
  38.8 1.3 %copy-done = f32[16,128,256]{2,1,0:T(8,128)} copy-done((f32[16,128,256]{2,1,0:T(8,128)}, f32[16,128,256]{2,1,0:T(8,128)S(1)}, u32[]{:S(2)}) %copy-start) | copy-done | bytes 2097176
  40.1 6.2 %all-to-all-done.parts_ref = f32[8,128,128]{2,1,0:T(8,128)S(1)} async-done(((f32[8,128,128]{2,1,0:T(8,128)}), f32[8,128,128]{2,1,0:T(8,128)S(1)}, u32[]{:S(2)}, u32[]{:S(2)}) %all-to-all-start) | async-done | bytes 524320 | tf_op jit(solution)/shard_map/all_to_all | solution.py:640
  46.7 22.6 %all_to_all.20.parts_ref = f32[16,64,128]{2,1,0:T(8,128)S(1)} all-to-all(f32[16,64,128]{2,1,0:T(8,128)S(1)} %slab_forward.1), channel_id=1, replica_groups=mesh['slab'=16,'pencil'=16] {'slab'}, dimensions={0} | all-to-all | bytes 1048576 | tf_op jit(solution)/shard_map/all_to_all | solution.py:648
  69.3 1.3 %back.1 = (f32[64,128]{1,0:T(8,128)S(1)}, f32[16,32,128]{2,1,0:T(8,128)}) custom-call(f32[16,64,128]{2,1,0:T(8,128)S(1)} %all_to_all.20.parts_ref, bf16[2,2,2,32,512]{4,3,2,1,0:T(8,128)(2,1)S(1)} %copy-done.6), custom_call_target="tpu_custom_call" | custom-call | tf_op jit(solution)/shard_map/back/pallas_call | solution.py:538
  70.6 4.3 %all-to-all-start.2 = ((f32[16,32,128]{2,1,0:T(8,128)}), f32[16,32,128]{2,1,0:T(8,128)S(1)}, u32[]{:S(2)}, u32[]{:S(2)}) async-start(f32[16,32,128]{2,1,0:T(8,128)} %get-tuple-element.39), calls=%async_computation.2 | async-start | bytes 524288 | tf_op jit(solution)/shard_map/all_to_all | solution.py:652
  75.0 0.9 dynamic-slice_bitcast_fusion.table_ref
  75.8 10.3 %all-to-all-done.2.parts_ref = f32[16,32,128]{2,1,0:T(8,128)S(1)} async-done(((f32[16,32,128]{2,1,0:T(8,128)}), f32[16,32,128]{2,1,0:T(8,128)S(1)}, u32[]{:S(2)}, u32[]{:S(2)}) %all-to-all-start.2) | async-done | bytes 262176 | tf_op jit(solution)/shard_map/all_to_all | solution.py:652
  86.3 9.4 %all_to_all.21.own_ref = f32[8,64,128]{2,1,0:T(8,128)S(1)} all-to-all(f32[8,64,128]{2,1,0:T(8,128)S(1)} %slab_backward.1), channel_id=1, replica_groups={{0,2,4,6,8,10,12,14},{1,3,5,7,9,11,13,15},{16,18,20,22,24,26,28,30},{17..., dimensions={0} | all-to-all | bytes 524288 | tf_op jit(solution)/shard_map/all_to_all | solution.py:655
  95.6 4.7 %collective-permute-start.6 = (f32[8,64,128]{2,1,0:T(8,128)S(1)}, f32[8,64,128]{2,1,0:T(8,128)S(1)}, u32[]{:S(2)}, u32[]{:S(2)}) collective-permute-start(f32[8,64,128]{2,1,0:T(8,128)S(1)} %all_to_all.21.own_ref), channel_id=1, source_target_pairs={{0,1},{1,0},{2,3},{3,2},{4,5},{5,4},{6,7},{7,6},{8,9},{9,8},{10,11... | collective-permute-start | bytes 786440 | tf_op jit(solution)/shard_map/ppermute | solution.py:656
  100.4 1.1 %weight_grad.1 = bf16[2,2,2,32,512]{4,3,2,1,0:T(8,128)(2,1)} custom-call(f32[64,128]{1,0:T(8,128)S(1)} %get-tuple-element.41.modes_ref), custom_call_target="tpu_custom_call" | custom-call | tf_op jit(solution)/shard_map/weight_grad/pallas_call | solution.py:538
  101.5 2.5 %output.1 = bf16[32,4,16,256]{3,2,1,0:T(8,128)(2,1)} custom-call(s32[1]{0:T(128)} %bitcast.position_ref, f32[544]{0:T(1024)S(1)} %copy-done.8, f32[8,64,128]{2,1,0:T(8,128)S(1)} %all_to_all.21.own_ref, f32[8,64,128]{2,1,0:T(8,128)S(1)} %collective-permute-done.6.other_ref, f32[16,128,256]{2,1,0:T(8,128)S(1)} %copy-done.1, bf16[96,256]{1,0:T(8,128)(2,1)S(1)} %copy-done.7), custom_call_target="tpu_custom_call" | custom-call | tf_op jit(solution)/shard_map/output/pallas_call | solution.py:538
  (38 shorter events, 3.6 us)
Async XLA Ops:
  0.6 17.7 %copy-start.8 = (f32[544]{0:T(1024)S(1)}, f32[544]{0:T(1024)}, u32[]{:S(2)}) copy-start(f32[544]{0:T(1024)} %constant.25.clone.phase_ref) | copy-start | bytes 6532
  0.6 17.7 %copy-start.3 = (bf16[32,4,16,256]{3,2,1,0:T(8,128)(2,1)S(1)}, bf16[32,4,16,256]{3,2,1,0:T(8,128)(2,1)}, u32[]{:S(2)}) copy-start(bf16[32,4,16,256]{3,2,1,0:T(8,128)(2,1)} %input_ref.1) | copy-start | bytes 3145732
  0.7 19.9 %copy-start.4 = (bf16[4,16,256]{2,1,0:T(8,128)(2,1)S(1)}, bf16[4,16,256]{2,1,0:T(8,128)(2,1)}, u32[]{:S(2)}) copy-start(bf16[4,16,256]{2,1,0:T(8,128)(2,1)} %coef_ref.3) | copy-start | bytes 98308
  0.7 19.9 %copy-start.5 = (bf16[4,16,256]{2,1,0:T(8,128)(2,1)S(1)}, bf16[4,16,256]{2,1,0:T(8,128)(2,1)}, u32[]{:S(2)}) copy-start(bf16[4,16,256]{2,1,0:T(8,128)(2,1)} %source_ref.3) | copy-start | bytes 98308
  4.5 0.6 copy-start.9
  5.1 15.4 %collective-permute-start = (f32[4,16,256]{2,1,0:T(8,128)}, f32[4,16,256]{2,1,0:T(8,128)S(1)}, u32[]{:S(2)}, u32[]{:S(2)}) collective-permute-start(f32[4,16,256]{2,1,0:T(8,128)} %get-tuple-element.22), channel_id=1, source_target_pairs={{0,16},{16,32},{32,48},{48,64},{64,80},{80,96},{96,112},{112,128},... | collective-permute-start | bytes 196616 | tf_op jit(solution)/shard_map/ppermute | solution.py:583
  8.9 11.6 %collective-permute-start.1 = (f32[4,16,256]{2,1,0:T(8,128)}, f32[4,16,256]{2,1,0:T(8,128)S(1)}, u32[]{:S(2)}, u32[]{:S(2)}) collective-permute-start(f32[4,16,256]{2,1,0:T(8,128)} %get-tuple-element.23), channel_id=1, source_target_pairs={{16,0},{32,16},{48,32},{64,48},{80,64},{96,80},{112,96},{128,112},... | collective-permute-start | bytes 196616 | tf_op jit(solution)/shard_map/ppermute | solution.py:584
  14.2 1.2 %copy-start.2 = (bf16[32,4,16,256]{3,2,1,0:T(8,128)(2,1)S(1)}, bf16[32,4,16,256]{3,2,1,0:T(8,128)(2,1)}, u32[]{:S(2)}) copy-start(bf16[32,4,16,256]{3,2,1,0:T(8,128)(2,1)} %pre_ref.1) | copy-start | bytes 3145732
  15.4 0.7 copy-start.10
  20.6 4.9 %collective-permute-start.3 = (f32[32,256]{1,0:T(8,128)S(1)}, f32[32,256]{1,0:T(8,128)S(1)}, u32[]{:S(2)}, u32[]{:S(2)}) collective-permute-start(f32[32,256]{1,0:T(8,128)S(1)} %get-tuple-element.32), channel_id=1, source_target_pairs={{0,1},{1,2},{2,3},{3,4},{4,5},{5,6},{6,7},{7,8},{8,9},{9,10},{10,1... | collective-permute-start | bytes 98312 | tf_op jit(solution)/shard_map/ppermute | solution.py:607
  21.9 15.2 %copy-start.11 = (bf16[32,32]{1,0:T(8,128)(2,1)S(1)}, bf16[32,32]{1,0:T(8,128)(2,1)}, u32[]{:S(2)}) copy-start(bf16[32,32]{1,0:T(8,128)(2,1)} %param.17) | copy-start | bytes 6148
  21.9 3.6 %collective-permute-start.4 = (f32[32,256]{1,0:T(8,128)S(1)}, f32[32,256]{1,0:T(8,128)S(1)}, u32[]{:S(2)}, u32[]{:S(2)}) collective-permute-start(f32[32,256]{1,0:T(8,128)S(1)} %get-tuple-element.33), channel_id=1, source_target_pairs={{1,0},{2,1},{3,2},{4,3},{5,4},{6,5},{7,6},{8,7},{9,8},{10,9},{11,1... | collective-permute-start | bytes 98312 | tf_op jit(solution)/shard_map/ppermute | solution.py:608
  21.9 8.1 %collective-permute-start.2 = (f32[8,64,128]{2,1,0:T(8,128)S(1)}, f32[8,64,128]{2,1,0:T(8,128)S(1)}, u32[]{:S(2)}, u32[]{:S(2)}) collective-permute-start(f32[8,64,128]{2,1,0:T(8,128)S(1)} %get-tuple-element.28), channel_id=1, source_target_pairs={{0,1},{1,0},{2,3},{3,2},{4,5},{5,4},{6,7},{7,6},{8,9},{9,8},{10,11... | collective-permute-start | bytes 786440 | tf_op jit(solution)/shard_map/ppermute | solution.py:603
  28.3 2.8 %collective-permute-start.5 = (f32[8,64,128]{2,1,0:T(8,128)S(1)}, f32[8,64,128]{2,1,0:T(8,128)S(1)}, u32[]{:S(2)}, u32[]{:S(2)}) collective-permute-start(f32[8,64,128]{2,1,0:T(8,128)S(1)} %get-tuple-element.36), channel_id=1, source_target_pairs={{0,1},{1,0},{2,3},{3,2},{4,5},{5,4},{6,7},{7,6},{8,9},{9,8},{10,11... | collective-permute-start | bytes 786440 | tf_op jit(solution)/shard_map/ppermute | solution.py:636
  32.0 14.3 %all-to-all-start = ((f32[8,128,128]{2,1,0:T(8,128)}), f32[8,128,128]{2,1,0:T(8,128)S(1)}, u32[]{:S(2)}, u32[]{:S(2)}) async-start(f32[8,128,128]{2,1,0:T(8,128)} %combine.1), calls=%async_computation | async-start | bytes 1048576 | tf_op jit(solution)/shard_map/all_to_all | solution.py:640
  38.3 31.1 %copy-start.6 = (bf16[2,2,2,32,512]{4,3,2,1,0:T(8,128)(2,1)S(1)}, bf16[2,2,2,32,512]{4,3,2,1,0:T(8,128)(2,1)}, u32[]{:S(2)}) copy-start(bf16[2,2,2,32,512]{4,3,2,1,0:T(8,128)(2,1)} %weight_ref.1) | copy-start | bytes 786436
  38.8 1.3 %copy-start = (f32[16,128,256]{2,1,0:T(8,128)}, f32[16,128,256]{2,1,0:T(8,128)S(1)}, u32[]{:S(2)}) copy-start(f32[16,128,256]{2,1,0:T(8,128)S(1)} %local.1.local_ref) | copy-start | bytes 6291460
  46.7 54.9 %copy-start.1 = (f32[16,128,256]{2,1,0:T(8,128)S(1)}, f32[16,128,256]{2,1,0:T(8,128)}, u32[]{:S(2)}) copy-start(f32[16,128,256]{2,1,0:T(8,128)} %copy-done) | copy-start | bytes 6291460
  46.7 54.9 %copy-start.7 = (bf16[96,256]{1,0:T(8,128)(2,1)S(1)}, bf16[96,256]{1,0:T(8,128)(2,1)}, u32[]{:S(2)}) copy-start(bf16[96,256]{1,0:T(8,128)(2,1)} %constant.27.clone.table_ref) | copy-start | bytes 147460
  70.6 15.4 %all-to-all-start.2 = ((f32[16,32,128]{2,1,0:T(8,128)}), f32[16,32,128]{2,1,0:T(8,128)S(1)}, u32[]{:S(2)}, u32[]{:S(2)}) async-start(f32[16,32,128]{2,1,0:T(8,128)} %get-tuple-element.39), calls=%async_computation.2 | async-start | bytes 524288 | tf_op jit(solution)/shard_map/all_to_all | solution.py:652
  95.6 5.9 %collective-permute-start.6 = (f32[8,64,128]{2,1,0:T(8,128)S(1)}, f32[8,64,128]{2,1,0:T(8,128)S(1)}, u32[]{:S(2)}, u32[]{:S(2)}) collective-permute-start(f32[8,64,128]{2,1,0:T(8,128)S(1)} %all_to_all.21.own_ref), channel_id=1, source_target_pairs={{0,1},{1,0},{2,3},{3,2},{4,5},{5,4},{6,7},{7,6},{8,9},{9,8},{10,11... | collective-permute-start | bytes 786440 | tf_op jit(solution)/shard_map/ppermute | solution.py:656

commit v3 on v2

--- a/solution.py
+++ b/solution.py
@@ -22,6 +22,7 @@
 PITCH = 68
 Y_PITCH = LANES + 8
 CHUNKS = 4
+BYTES_PER_US = 3_690_000
 
 
 def split_2(table):
@@ -93,13 +94,15 @@
     coef_hbm,
     source_hbm,
     proj_hbm,
+    input_hbm,
     field_ref,
     up_ref,
     down_ref,
-    proj_tile_ref,
     pre_ref,
     coef_ref,
     source_ref,
+    input_ref,
+    proj_tile_ref,
     proj_ref,
     sems,
 ):
@@ -110,6 +113,7 @@
         copies.append(pltpu.make_async_copy(pre_hbm.at[part], pre_ref.at[part], sems.at[i]))
     copies.append(pltpu.make_async_copy(coef_hbm, coef_ref, sems.at[CHUNKS + 1]))
     copies.append(pltpu.make_async_copy(source_hbm, source_ref, sems.at[CHUNKS + 2]))
+    copies.append(pltpu.make_async_copy(input_hbm, input_ref, sems.at[CHUNKS + 3]))
     for copy in copies:
         copy.start()
     copies[0].wait()
@@ -125,8 +129,8 @@
     for i in range(CHUNKS):
         copies[1 + i].wait()
         total = lax.fori_loop(i * size, (i + 1) * size, add_channel, total, unroll=2)
-    copies[-2].wait()
-    copies[-1].wait()
+    for copy in copies[1 + CHUNKS :]:
+        copy.wait()
     field_ref[...] = total
     up_ref[0:2] = total[2:4]
     down_ref[0:2] = total[0:2]
@@ -200,7 +204,6 @@
 
 
 def input_kernel(
-    position_ref,
     phase_ref,
     input_ref,
     table_hbm,
@@ -228,7 +231,7 @@
         values = jnp.concatenate(sides, axis=1).astype(BF16)
         both = nt_dot(table_ref[...], values)
         modes_ref[y] = both[:32] + both[32:]
-    position = position_ref[0]
+    position = lax.axis_index("pencil")
     forward = functools.partial(pencil_forward, modes_ref, phase_ref, position)
     by_core(position, forward, own_ref, other_ref)
 
@@ -273,7 +276,6 @@
 
 
 def grad_kernel(
-    position_ref,
     phase_ref,
     field_ref,
     coef_ref,
@@ -322,7 +324,7 @@
         high, low = act_parts(slope_ref, grad_ref, y)
         both = nt_dot(table_ref[...], high)
         modes_ref[y] = both[:32] + both[32:] + nt_dot(table_ref[0:32, :], low)
-    position = position_ref[0]
+    position = lax.axis_index("pencil")
     forward = functools.partial(pencil_forward, modes_ref, phase_ref, position)
     by_core(position, forward, own_ref, other_ref)
 
@@ -332,10 +334,38 @@
     out_ref[:, 64:128, :] = own_ref[...] + got_ref[...]
 
 
-def local_kernel(pointwise_ref, slope_ref, grad_ref, out_ref):
+def local_kernel(
+    pointwise_ref,
+    slope_ref,
+    grad_ref,
+    forward_hbm,
+    backward_hbm,
+    out_ref,
+    forward_ref,
+    backward_ref,
+    sems,
+):
+    slab = lax.axis_index("slab")
+    copies = [
+        pltpu.make_async_copy(forward_hbm.at[slab], forward_ref, sems.at[0]),
+        pltpu.make_async_copy(backward_hbm.at[slab], backward_ref, sems.at[1]),
+    ]
+    for copy in copies:
+        copy.start()
+    rows = lax.broadcasted_iota(jnp.int32, (C, LANES), 0)
+    lanes = lax.broadcasted_iota(jnp.int32, (C, LANES), 1)
+    repeat = jnp.where(lanes % C == rows, 1.0, 0.0).astype(BF16)
+    wide = jnp.dot(pointwise_ref[...], repeat, preferred_element_type=F32)
+    wide = jnp.concatenate([wide] * CX, axis=0)
+    rows = lax.broadcasted_iota(jnp.int32, (LANES, LANES), 0)
+    lanes = lax.broadcasted_iota(jnp.int32, (LANES, LANES), 1)
+    wide = jnp.where(rows // C == lanes // C, wide, 0.0).astype(BF16)
+    wide = jnp.concatenate([wide, wide], axis=1)
     for y in range(CY):
         act = jnp.concatenate(act_parts(slope_ref, grad_ref, y), axis=0)
-        out_ref[y] = jnp.dot(pointwise_ref[...], act, preferred_element_type=F32)
+        out_ref[y] = jnp.dot(wide, act, preferred_element_type=F32)
+    for copy in copies:
+        copy.wait()
 
 
 def slab_forward_kernel(parts_ref, table_ref, out_ref):
@@ -474,18 +504,21 @@
 
 
 def output_kernel(
-    position_ref,
     phase_ref,
     own_ref,
     other_ref,
     local_ref,
-    table_ref,
+    table_hbm,
     out_ref,
     modes_ref,
     rows_ref,
     flat_ref,
+    table_ref,
+    sem,
 ):
-    position = position_ref[0]
+    copy = pltpu.make_async_copy(table_hbm, table_ref, sem)
+    copy.start()
+    position = lax.axis_index("pencil")
     turn = functools.partial(turn_modes, phase_ref, position, modes_ref)
     by_core(position, turn, own_ref, other_ref)
     for half in range(2):
@@ -505,6 +538,7 @@
             rows_ref[y, more, :] = even[1] + odd[0]
             rows_ref[15 - y, rows, :] = even[0] + odd[1]
             rows_ref[15 - y, more, :] = even[1] - odd[0]
+    copy.wait()
     for y in range(CY):
         values = rows_ref[y]
         high = values.astype(BF16)
@@ -521,7 +555,7 @@
             out_ref[c, :, :, side * 128 : (side + 1) * 128] = piece.reshape(CX, CY, 128)
 
 
-def call(kernel, name, out, scratch=(), scalars=(), hbm=()):
+def call(kernel, name, out, scratch=(), scalars=(), hbm=(), us=1):
     def run(*args):
         args = [
             pltpu.with_memory_space_constraint(arg, pltpu.HBM) if i in hbm else arg
@@ -542,6 +576,9 @@
             out_specs=[pl.BlockSpec(memory_space=pltpu.VMEM)] * len(shapes),
             scratch_shapes=[pltpu.VMEM(*s) if isinstance(s, tuple) else s for s in scratch],
             compiler_params=pltpu.CompilerParams(vmem_limit_bytes=VMEM_LIMIT),
+            cost_estimate=pl.CostEstimate(
+                flops=0, transcendentals=0, bytes_accessed=int(us * BYTES_PER_US)
+            ),
             name=name,
         )(*args)
         return result[0] if single else result
@@ -556,33 +593,30 @@
     down = [(j, i) for i, j in up]
     swap = [(i, i ^ 1) for i in range(N)]
     same_core = [[i for i in range(N) if i % 2 == core] for core in range(2)]
-    slab = lax.axis_index("slab")
-    pencil = lax.axis_index("pencil").reshape(1)
     phases = jnp.asarray(PENCIL_PHASES)
     depth_forward = jnp.asarray(DEPTH_FORWARD)
     depth_backward = jnp.asarray(DEPTH_BACKWARD)
-    slab_forward = lax.dynamic_index_in_dim(jnp.asarray(SLAB_FORWARD), slab, 0, False)
-    slab_backward = lax.dynamic_index_in_dim(jnp.asarray(SLAB_BACKWARD), slab, 0, False)
-    pointwise_4 = jnp.kron(jnp.eye(CX, dtype=BF16), pointwise)
-    pointwise_8 = jnp.concatenate([pointwise_4, pointwise_4], axis=1)
-
     edge = ((4, CY, NZ), F32)
-    field, edge_up, edge_down, proj_tile = call(
+    field, edge_up, edge_down, pre_activation, coefficient, source, layer_input, proj_tile = call(
         field_kernel,
         "field",
-        [((CX, CY, NZ), F32), edge, edge, ((C, 128), F32)],
-        scratch=[
+        [
+            ((CX, CY, NZ), F32),
+            edge,
+            edge,
             ((C, CX, CY, NZ), BF16),
             ((CX, CY, NZ), BF16),
             ((CX, CY, NZ), BF16),
-            pltpu.SMEM((C,), F32),
-            pltpu.SemaphoreType.DMA((CHUNKS + 3,)),
+            ((C, CX, CY, NZ), BF16),
+            ((C, 128), F32),
         ],
-        hbm=(0, 1, 2, 3),
-    )(pre_activation, coefficient, source, projection)
+        scratch=[pltpu.SMEM((C,), F32), pltpu.SemaphoreType.DMA((CHUNKS + 4,))],
+        hbm=(0, 1, 2, 3, 4),
+        us=4,
+    )(pre_activation, coefficient, source, projection, layer_input)
     before = lax.ppermute(edge_up, "slab", up)
     after = lax.ppermute(edge_down, "slab", down)
-    slope = call(slope_kernel, "slope", ((2, CY * Y_PITCH, 128), F32))(pre_activation, proj_tile)
+    slope = call(slope_kernel, "slope", ((2, CY * Y_PITCH, 128), F32), us=2)(pre_activation, proj_tile)
     half_modes = ((N // 2, 64, LANES), F32)
     own_in, other_in = call(
         input_kernel,
@@ -594,9 +628,10 @@
             (DEPTH_FORWARD.shape, BF16),
             pltpu.SemaphoreType.DMA(()),
         ],
-        scalars=(0, 1),
-        hbm=(3,),
-    )(pencil, phases, layer_input, depth_forward)
+        scalars=(0,),
+        hbm=(2,),
+        us=2,
+    )(phases, layer_input, depth_forward)
     before, after, slope, own_in, other_in = lax.optimization_barrier(
         (before, after, slope, own_in, other_in)
     )
@@ -618,10 +653,10 @@
             (DEPTH_FORWARD.shape, BF16),
             pltpu.SemaphoreType.DMA(()),
         ],
-        scalars=(0, 1),
-        hbm=(10,),
+        scalars=(0,),
+        hbm=(9,),
+        us=3,
     )(
-        pencil,
         phases,
         field,
         coefficient,
@@ -634,14 +669,23 @@
         depth_forward,
     )
     got = lax.ppermute(other, "pencil", swap)
+    table = (SLAB_FORWARD.shape[1:], F32)
+    local, slab_forward, slab_backward = call(
+        local_kernel,
+        "local",
+        [((CY, LANES, NZ), F32), table, table],
+        scratch=[pltpu.SemaphoreType.DMA((2,))],
+        hbm=(3, 4),
+    )(pointwise, slope, grad, jnp.asarray(SLAB_FORWARD), jnp.asarray(SLAB_BACKWARD))
+    got, local, slab_forward, slab_backward = lax.optimization_barrier(
+        (got, local, slab_forward, slab_backward)
+    )
     to_pencil = call(combine_kernel, "combine", ((N // 2, 128, LANES), F32))(
         own_in, got_in, own, got
     )
     from_pencil = lax.all_to_all(
         to_pencil, "pencil", 0, 0, axis_index_groups=same_core, tiled=True
     )
-    local = call(local_kernel, "local", ((CY, LANES, NZ), F32))(pointwise_8, slope, grad)
-    from_pencil, local = lax.optimization_barrier((from_pencil, local))
     to_slab = call(slab_forward_kernel, "slab_forward", ((N, 64, LANES), F32))(
         from_pencil, slab_forward
     )
@@ -662,9 +706,12 @@
             ((2, 2, 17, 2, 8, LANES), F32),
             ((CY, 32, LANES), F32),
             ((2, C * PITCH, 128), F32),
+            (DEPTH_BACKWARD.shape, BF16),
+            pltpu.SemaphoreType.DMA(()),
         ],
-        scalars=(0, 1),
-    )(pencil, phases, own, other, local, depth_backward)
+        scalars=(0,),
+        hbm=(4,),
+    )(phases, own, other, local, depth_backward)
     return (input_grad, weight_grad)
 
 

time: 105 us -> 100 us (0.952)
  blocking collectives: 32 us -> 62.2 us
  waiting for transfers between devices: 17.7 us -> 3.47 us
  starting transfers between devices: 29.8 us -> 16.1 us
  local copies, waits for them, and re-layouts: 5.72 us -> 0.02 us
    all_to_all x2 -> x0, waiting for transfers between devices: 16.5 us -> none  [the longest x1 10.3 us: shards(): from_slab = lax.all_to_all(to_slab, 'slab', 0, 0, tiled=True)]
    all_to_all x1 -> x2, blocking collectives: 9.35 us -> 24.5 us  [shards(): lax.all_to_all(to_pencil, 'pencil', 0, 0, axis_index_groups=same_core, ti...]
    all_to_all x1 -> x2, blocking collectives: 22.6 us -> 37.7 us  [shards(): from_slab = lax.all_to_all(to_slab, 'slab', 0, 0, tiled=True)]
    all_to_all x2 -> x0, starting transfers between devices: 9.41 us -> none  [the longest x1 5.11 us: shards(): lax.all_to_all(to_pencil, 'pencil', 0, 0, axis_index_groups=same_core, ti...]
    unnamed x24 -> x6, local copies, waits for them, and re-layouts: 3.9 us -> 0.02 us
    ppermute x1, starting transfers between devices: 3.57 us -> 0.1 us  [shards(): got_in = lax.ppermute(other_in, 'pencil', swap)]
    ppermute x1, waiting for transfers between devices: 0.01 us -> 2.32 us  [shards(): high = lax.ppermute(side_down, 'pencil', down)]
    squeeze x2 -> x0, local copies, waits for them, and re-layouts: 1.7 us -> none  [the longest x1 0.85 us: shards(): lax.dynamic_index_in_dim(jnp.asarray(SLAB_FORWARD), slab, 0, False)]
  transfers between devices with their start and end apart: 9 -> 7, of which waited for: 4 -> 4; matrix products, arithmetic and copies ran while one was open for 2% -> 0% of each run, Pallas kernels for 8% -> 7%
where the time goes in v3:
time: 100 us; the launch traced here: 99.7 us
  blocking collectives  62.2 us (62%)
  Pallas kernels  17.1 us (17%)
  starting transfers between devices  16.1 us (16%)
  waiting for transfers between devices  3.47 us (3%)
    all_to_all x2, blocking collectives, shards(): from_slab = lax.all_to_all(to_slab, 'slab', 0, 0, tiled=True)  37.7 us
    all_to_all x2, blocking collectives, shards(): lax.all_to_all(to_pencil, 'pencil', 0, 0, axis_index_groups=same_core, ti...  24.5 us
    pallas_call x12, Pallas kernels, run(): pl.pallas_call(kernel, out_shape=shapes, in_specs=specs, out_specs=[pl.Bl...  17.1 us
    ppermute x1, starting transfers between devices, shards(): after = lax.ppermute(edge_down, 'slab', down)  5.38 us
    ppermute x1, starting transfers between devices, shards(): before = lax.ppermute(edge_up, 'slab', up)  3.82 us
    ppermute x1, starting transfers between devices, shards(): other = lax.ppermute(own, 'pencil', swap)  3.6 us
    ppermute x1, waiting for transfers between devices, shards(): high = lax.ppermute(side_down, 'pencil', down)  2.32 us
  transfers between devices with their start and end apart: 7, of which 4 were waited for; matrix products, arithmetic and copies ran while one was open for 0% of the time, Pallas kernels for 7%

profile of v3, /device:TPU:1, one launch (start us, length us, event | category | flops | bytes accessed | tf_op | source)
XLA Modules:
  0.0 99.7 jit_solution(16756030125789992429)
XLA Ops:
  0.6 3.1 %field.1 = (f32[4,16,256]{2,1,0:T(8,128)S(1)}, f32[4,16,256]{2,1,0:T(8,128)S(1)}, f32[4,16,256]{2,1,0:T(8,128)S(1)}, bf16[32,4,16,256]{3,2,1,0:T(8,128)(2,1)S(1)...) custom-call(bf16[32,4,16,256]{3,2,1,0:T(8,128)(2,1)} %pre_hbm.1, ...), custom_call_target="tpu_custom_call" | custom-call | bytes 14760000 | tf_op jit(solution)/shard_map/field/pallas_call | solution.py:572
  3.8 3.8 %collective-permute-start = (f32[4,16,256]{2,1,0:T(8,128)S(1)}, f32[4,16,256]{2,1,0:T(8,128)S(1)}, u32[]{:S(2)}, u32[]{:S(2)}) collective-permute-start(f32[4,16,256]{2,1,0:T(8,128)S(1)} %get-tuple-element.31), channel_id=1, source_target_pairs={{0,16},{16,32},{32,48},{48,64},{64,80},{80,96},{96,112},{112,128},... | collective-permute-start | bytes 196616 | tf_op jit(solution)/shard_map/ppermute | solution.py:617
  7.6 5.4 %collective-permute-start.1 = (f32[4,16,256]{2,1,0:T(8,128)S(1)}, f32[4,16,256]{2,1,0:T(8,128)S(1)}, u32[]{:S(2)}, u32[]{:S(2)}) collective-permute-start(f32[4,16,256]{2,1,0:T(8,128)S(1)} %get-tuple-element.32), channel_id=1, source_target_pairs={{16,0},{32,16},{48,32},{64,48},{80,64},{96,80},{112,96},{128,112},... | collective-permute-start | bytes 196616 | tf_op jit(solution)/shard_map/ppermute | solution.py:618
  13.0 2.2 %slope.1.slope_ref = f32[2,2176,128]{2,1,0:T(8,128)S(1)} custom-call(bf16[32,4,16,256]{3,2,1,0:T(8,128)(2,1)S(1)} %get-tuple-element.33.pre_ref, f32[32,128]{1,0:T(8,128)S(1)} %get-tuple-element.34.proj_ref), custom_call_target="tpu_custom_call" | custom-call | bytes 7380000 | tf_op jit(solution)/shard_map/slope/pallas_call | solution.py:572
  15.2 2.2 %input_modes.1 = (f32[8,64,128]{2,1,0:T(8,128)S(1)}, f32[8,64,128]{2,1,0:T(8,128)S(1)}) custom-call(f32[544]{0:T(1024)S(1)} %copy-done.1, bf16[32,4,16,256]{3,2,1,0:T(8,128)(2,1)S(1)} %get-tuple-element.35.input_ref, bf16[64,256]{1,0:T(8,128)(2,1)} %constant.11.clone.table_hbm), custom_call_target="tpu_custom_call" | custom-call | bytes 7380000 | tf_op jit(solution)/shard_map/input_modes/pallas_call | solution.py:572
  17.4 1.3 %collective-permute-start.3 = (f32[32,256]{1,0:T(8,128)S(1)}, f32[32,256]{1,0:T(8,128)S(1)}, u32[]{:S(2)}, u32[]{:S(2)}) collective-permute-start(f32[32,256]{1,0:T(8,128)S(1)} %get-tuple-element.45), channel_id=1, source_target_pairs={{0,1},{1,2},{2,3},{3,4},{4,5},{5,6},{6,7},{7,8},{8,9},{9,10},{10,1... | collective-permute-start | bytes 98312 | tf_op jit(solution)/shard_map/ppermute | solution.py:642
  18.8 1.0 %collective-permute-done.3.low_ref = f32[32,256]{1,0:T(8,128)S(1)} collective-permute-done((f32[32,256]{1,0:T(8,128)S(1)}, f32[32,256]{1,0:T(8,128)S(1)}, u32[]{:S(2)}, u32[]{:S(2)}) %collective-permute-start.3) | collective-permute-done | bytes 32800 | tf_op jit(solution)/shard_map/ppermute | solution.py:642
  19.8 2.3 %collective-permute-done.4.high_ref = f32[32,256]{1,0:T(8,128)S(1)} collective-permute-done((f32[32,256]{1,0:T(8,128)S(1)}, f32[32,256]{1,0:T(8,128)S(1)}, u32[]{:S(2)}, u32[]{:S(2)}) %collective-permute-start.4) | collective-permute-done | bytes 32800 | tf_op jit(solution)/shard_map/ppermute | solution.py:643
  22.1 2.9 %grad_modes.1 = (f32[8,64,128]{2,1,0:T(8,128)S(1)}, f32[8,64,128]{2,1,0:T(8,128)S(1)}, f32[4,32,256]{2,1,0:T(8,128)S(1)}) custom-call(f32[544]{0:T(1024)S(1)} %copy-done.1, f32[4,16,256]{2,1,0:T(8,128)S(1)} %get-tuple-element.40.field_ref, bf16[4,16,256]{2,1,0:T(8,128)(2,1)S(1)} %get-tuple-element.41.coef_ref, ...), custom_call_target="tpu_custom_call" | custom-call | bytes 11070000 | tf_op jit(solution)/shard_map/grad_modes/pallas_call | solution.py:572
  25.0 1.9 %collective-permute-start.5 = (f32[8,64,128]{2,1,0:T(8,128)S(1)}, f32[8,64,128]{2,1,0:T(8,128)S(1)}, u32[]{:S(2)}, u32[]{:S(2)}) collective-permute-start(f32[8,64,128]{2,1,0:T(8,128)S(1)} %get-tuple-element.49), channel_id=1, source_target_pairs={{0,1},{1,0},{2,3},{3,2},{4,5},{5,4},{6,7},{7,6},{8,9},{9,8},{10,11... | collective-permute-start | bytes 786440 | tf_op jit(solution)/shard_map/ppermute | solution.py:671
  26.9 0.1 collective-permute-start.2
  27.0 1.3 %local.1 = (f32[16,128,256]{2,1,0:T(8,128)S(1)}, f32[128,128]{1,0:T(8,128)S(1)}, f32[128,128]{1,0:T(8,128)S(1)}) custom-call(bf16[32,32]{1,0:T(8,128)(2,1)S(1)} %copy-done.2, f32[2,2176,128]{2,1,0:T(8,128)S(1)} %slope.1.slope_ref, f32[4,32,256]{2,1,0:T(8,128)S(1)} %get-tuple-element.50.grad_ref, f32[16,128,128]{2,1,0:T(8,128)} %constant.13.clone.forward_hbm, ...), custom_call_target="tpu_custom_call" | custom-call | bytes 3690000 | tf_op jit(solution)/shard_map/local/pallas_call | solution.py:572
  28.4 0.1 collective-permute-done.2.got_in_ref
  28.4 0.1 combine.1
  28.5 14.2 %all_to_all.20.parts_ref = f32[8,128,128]{2,1,0:T(8,128)S(1)} all-to-all(f32[8,128,128]{2,1,0:T(8,128)S(1)} %combine.1), channel_id=1, replica_groups={{0,2,4,6,8,10,12,14},{1,3,5,7,9,11,13,15},{16,18,20,22,24,26,28,30},{17..., dimensions={0} | all-to-all | bytes 1048576 | tf_op jit(solution)/shard_map/all_to_all | solution.py:686
  42.7 0.4 slab_forward.1
  43.1 22.4 %all_to_all.21.parts_ref = f32[16,64,128]{2,1,0:T(8,128)S(1)} all-to-all(f32[16,64,128]{2,1,0:T(8,128)S(1)} %slab_forward.1), channel_id=1, replica_groups=mesh['slab'=16,'pencil'=16] {'slab'}, dimensions={0} | all-to-all | bytes 1048576 | tf_op jit(solution)/shard_map/all_to_all | solution.py:692
  65.5 0.6 back.1
  66.1 15.3 %all_to_all.22.parts_ref = f32[16,32,128]{2,1,0:T(8,128)S(1)} all-to-all(f32[16,32,128]{2,1,0:T(8,128)S(1)} %get-tuple-element.56), channel_id=1, replica_groups=mesh['slab'=16,'pencil'=16] {'slab'}, dimensions={0} | all-to-all | bytes 524288 | tf_op jit(solution)/shard_map/all_to_all | solution.py:696
  81.4 0.2 slab_backward.1
  81.6 10.3 %all_to_all.23.own_ref = f32[8,64,128]{2,1,0:T(8,128)S(1)} all-to-all(f32[8,64,128]{2,1,0:T(8,128)S(1)} %slab_backward.1), channel_id=1, replica_groups={{0,2,4,6,8,10,12,14},{1,3,5,7,9,11,13,15},{16,18,20,22,24,26,28,30},{17..., dimensions={0} | all-to-all | bytes 524288 | tf_op jit(solution)/shard_map/all_to_all | solution.py:699
  91.9 3.6 %collective-permute-start.6 = (f32[8,64,128]{2,1,0:T(8,128)S(1)}, f32[8,64,128]{2,1,0:T(8,128)S(1)}, u32[]{:S(2)}, u32[]{:S(2)}) collective-permute-start(f32[8,64,128]{2,1,0:T(8,128)S(1)} %all_to_all.23.own_ref), channel_id=1, source_target_pairs={{0,1},{1,0},{2,3},{3,2},{4,5},{5,4},{6,7},{7,6},{8,9},{9,8},{10,11... | collective-permute-start | bytes 786440 | tf_op jit(solution)/shard_map/ppermute | solution.py:700
  95.5 1.1 %weight_grad.1 = bf16[2,2,2,32,512]{4,3,2,1,0:T(8,128)(2,1)} custom-call(f32[64,128]{1,0:T(8,128)S(1)} %get-tuple-element.59.modes_ref), custom_call_target="tpu_custom_call" | custom-call | bytes 3690000 | tf_op jit(solution)/shard_map/weight_grad/pallas_call | solution.py:572
  96.7 3.0 %output.1 = bf16[32,4,16,256]{3,2,1,0:T(8,128)(2,1)} custom-call(f32[544]{0:T(1024)S(1)} %copy-done.1, f32[8,64,128]{2,1,0:T(8,128)S(1)} %all_to_all.23.own_ref, f32[8,64,128]{2,1,0:T(8,128)S(1)} %collective-permute-done.6.other_ref, f32[16,128,256]{2,1,0:T(8,128)S(1)} %get-tuple-element.58.local_ref, bf16[96,256]{1,0:T(8,128)(2,1)} %constant.12.clone.table_hbm), custom_call_target="tpu_custom_call" | custom-call | bytes 3690000 | tf_op jit(solution)/shard_map/output/pallas_call | solution.py:572
  (12 shorter events, 0.1 us)
Async XLA Ops:
  0.6 14.6 %copy-start.1 = (f32[544]{0:T(1024)S(1)}, f32[544]{0:T(1024)}, u32[]{:S(2)}) copy-start(f32[544]{0:T(1024)} %constant.10.clone.phase_ref) | copy-start | bytes 6532
  3.8 13.6 %collective-permute-start = (f32[4,16,256]{2,1,0:T(8,128)S(1)}, f32[4,16,256]{2,1,0:T(8,128)S(1)}, u32[]{:S(2)}, u32[]{:S(2)}) collective-permute-start(f32[4,16,256]{2,1,0:T(8,128)S(1)} %get-tuple-element.31), channel_id=1, source_target_pairs={{0,16},{16,32},{32,48},{48,64},{64,80},{80,96},{96,112},{112,128},... | collective-permute-start | bytes 196616 | tf_op jit(solution)/shard_map/ppermute | solution.py:617
  7.6 9.8 %collective-permute-start.1 = (f32[4,16,256]{2,1,0:T(8,128)S(1)}, f32[4,16,256]{2,1,0:T(8,128)S(1)}, u32[]{:S(2)}, u32[]{:S(2)}) collective-permute-start(f32[4,16,256]{2,1,0:T(8,128)S(1)} %get-tuple-element.32), channel_id=1, source_target_pairs={{16,0},{32,16},{48,32},{64,48},{80,64},{96,80},{112,96},{128,112},... | collective-permute-start | bytes 196616 | tf_op jit(solution)/shard_map/ppermute | solution.py:618
  15.2 11.8 %copy-start.2 = (bf16[32,32]{1,0:T(8,128)(2,1)S(1)}, bf16[32,32]{1,0:T(8,128)(2,1)}, u32[]{:S(2)}) copy-start(bf16[32,32]{1,0:T(8,128)(2,1)} %pointwise_ref.1) | copy-start | bytes 6148
  17.4 2.3 %collective-permute-start.3 = (f32[32,256]{1,0:T(8,128)S(1)}, f32[32,256]{1,0:T(8,128)S(1)}, u32[]{:S(2)}, u32[]{:S(2)}) collective-permute-start(f32[32,256]{1,0:T(8,128)S(1)} %get-tuple-element.45), channel_id=1, source_target_pairs={{0,1},{1,2},{2,3},{3,4},{4,5},{5,6},{6,7},{7,8},{8,9},{9,10},{10,1... | collective-permute-start | bytes 98312 | tf_op jit(solution)/shard_map/ppermute | solution.py:642
  18.8 3.3 %collective-permute-start.4 = (f32[32,256]{1,0:T(8,128)S(1)}, f32[32,256]{1,0:T(8,128)S(1)}, u32[]{:S(2)}, u32[]{:S(2)}) collective-permute-start(f32[32,256]{1,0:T(8,128)S(1)} %get-tuple-element.46), channel_id=1, source_target_pairs={{1,0},{2,1},{3,2},{4,3},{5,4},{6,5},{7,6},{8,7},{9,8},{10,9},{11,1... | collective-permute-start | bytes 98312 | tf_op jit(solution)/shard_map/ppermute | solution.py:643
  25.0 3.4 %collective-permute-start.5 = (f32[8,64,128]{2,1,0:T(8,128)S(1)}, f32[8,64,128]{2,1,0:T(8,128)S(1)}, u32[]{:S(2)}, u32[]{:S(2)}) collective-permute-start(f32[8,64,128]{2,1,0:T(8,128)S(1)} %get-tuple-element.49), channel_id=1, source_target_pairs={{0,1},{1,0},{2,3},{3,2},{4,5},{5,4},{6,7},{7,6},{8,9},{9,8},{10,11... | collective-permute-start | bytes 786440 | tf_op jit(solution)/shard_map/ppermute | solution.py:671
  26.9 1.5 %collective-permute-start.2 = (f32[8,64,128]{2,1,0:T(8,128)S(1)}, f32[8,64,128]{2,1,0:T(8,128)S(1)}, u32[]{:S(2)}, u32[]{:S(2)}) collective-permute-start(f32[8,64,128]{2,1,0:T(8,128)S(1)} %get-tuple-element.39), channel_id=1, source_target_pairs={{0,1},{1,0},{2,3},{3,2},{4,5},{5,4},{6,7},{7,6},{8,9},{9,8},{10,11... | collective-permute-start | bytes 786440 | tf_op jit(solution)/shard_map/ppermute | solution.py:638
  28.4 37.0 %copy-start = (bf16[2,2,2,32,512]{4,3,2,1,0:T(8,128)(2,1)S(1)}, bf16[2,2,2,32,512]{4,3,2,1,0:T(8,128)(2,1)}, u32[]{:S(2)}) copy-start(bf16[2,2,2,32,512]{4,3,2,1,0:T(8,128)(2,1)} %weight_ref.1) | copy-start | bytes 786436
  91.9 4.8 %collective-permute-start.6 = (f32[8,64,128]{2,1,0:T(8,128)S(1)}, f32[8,64,128]{2,1,0:T(8,128)S(1)}, u32[]{:S(2)}, u32[]{:S(2)}) collective-permute-start(f32[8,64,128]{2,1,0:T(8,128)S(1)} %all_to_all.23.own_ref), channel_id=1, source_target_pairs={{0,1},{1,0},{2,3},{3,2},{4,5},{5,4},{6,7},{7,6},{8,9},{9,8},{10,11... | collective-permute-start | bytes 786440 | tf_op jit(solution)/shard_map/ppermute | solution.py:700

commit v4 on v3

--- a/solution.py
+++ b/solution.py
@@ -71,9 +71,24 @@
     return forward.astype(np.float32).reshape(shape), backward.astype(np.float32).reshape(shape)
 
 
+def input_table():
+    table = np.zeros((4, N, 4, 2, LANES))
+    for q in range(4):
+        for device in range(N):
+            for shift in range(4):
+                for group in range(4):
+                    other = (group - shift) % 4
+                    angle = 2.0 * math.pi * (((4 * q + group) * (4 * device + other)) % NX) / NX
+                    lanes = slice(group * C, (group + 1) * C)
+                    table[q, device, shift, 0, lanes] = math.cos(angle)
+                    table[q, device, shift, 1, lanes] = math.sin(angle)
+    return table.astype(np.float32).reshape(-1, LANES)
+
+
 DEPTH_FORWARD, DEPTH_BACKWARD = depth_tables()
 PENCIL_PHASES = pencil_phases()
 SLAB_FORWARD, SLAB_BACKWARD = slab_tables()
+INPUT_TABLE = input_table()
 
 
 def normal_tail(values):
@@ -340,15 +355,18 @@
     grad_ref,
     forward_hbm,
     backward_hbm,
+    input_hbm,
     out_ref,
     forward_ref,
     backward_ref,
+    input_ref,
     sems,
 ):
     slab = lax.axis_index("slab")
     copies = [
         pltpu.make_async_copy(forward_hbm.at[slab], forward_ref, sems.at[0]),
         pltpu.make_async_copy(backward_hbm.at[slab], backward_ref, sems.at[1]),
+        pltpu.make_async_copy(input_hbm, input_ref, sems.at[2]),
     ]
     for copy in copies:
         copy.start()
@@ -368,12 +386,19 @@
         copy.wait()
 
 
-def slab_forward_kernel(parts_ref, table_ref, out_ref):
-    for block in range(4):
+def slab_forward_kernel(parts_ref, table_ref, out_ref, raw_ref):
+    raw = parts_ref[0, 0:64, :]
+    for source in range(1, N // 2):
+        raw = raw + parts_ref[source, 0:64, :]
+    raw_ref[0:64, :] = raw
+    raw_ref[64:128, :] = jnp.zeros((64, LANES), F32)
+    for kz in range(KZ):
+        out_ref[kz, 32:40, :] = raw_ref[pl.ds(kz, 8, stride=KZ), :]
+    for ky in range(2):
         for half in range(2):
             pieces = []
             for part in range(2):
-                rows = pl.ds(block * 32 + part * KZ + 8 * half, 8)
+                rows = pl.ds(64 + ky * 32 + part * KZ + 8 * half, 8)
                 total = parts_ref[0, rows, :]
                 for source in range(1, N // 2):
                     total = total + parts_ref[source, rows, :]
@@ -385,7 +410,7 @@
                         row = owner * 8 + d * 2 + part
                         term = pieces[part][d] * table_ref[row : row + 1, :]
                         result = term if result is None else result + term
-                out_ref[owner, pl.ds(block * KZ + 8 * half, 8), :] = result
+                out_ref[owner, pl.ds(ky * KZ + 8 * half, 8), :] = result
 
 
 def flat_modes(block, group):
@@ -409,10 +434,46 @@
     return high, middle, low
 
 
-def back_kernel(parts_ref, weight_ref, modes_ref, out_ref):
-    total = parts_ref[0]
+def minus_i(values, even_row):
+    return jnp.where(even_row, pltpu.roll(values, 7, 0), -pltpu.roll(values, 1, 0))
+
+
+def input_modes_at(parts_ref, table_ref):
+    row = lax.broadcasted_iota(jnp.int32, (8, LANES), 0)
+    group = lax.broadcasted_iota(jnp.int32, (8, LANES), 1) // C
+    even_row = row % 2 == 0
+    totals = [[None] * 4 for _ in range(4)]
+    for source in range(N):
+        values = parts_ref[source, 32:40, :]
+        turned = minus_i(values, even_row)
+        for shift in range(4):
+            if shift:
+                real, imag = pltpu.roll(values, 32 * shift, 1), pltpu.roll(turned, 32 * shift, 1)
+            else:
+                real, imag = values, turned
+            for q in range(4):
+                r = ((q * N + source) * 4 + shift) * 2
+                term = real * table_ref[r : r + 1, :] + imag * table_ref[r + 1 : r + 2, :]
+                last = totals[q][shift]
+                totals[q][shift] = term if last is None else last + term
+    lower, upper = [], []
+    for q in range(4):
+        lower.append(totals[q][0] + totals[q][1] + totals[q][2] + totals[q][3])
+        result = None
+        for shift in range(4):
+            x = (group - shift) % 4
+            cos = jnp.where(x == 0, 1.0, jnp.where(x == 2, -1.0, 0.0))
+            sin = jnp.where(x == 1, -1.0, jnp.where(x == 3, 1.0, 0.0))
+            term = cos * totals[q][shift] + sin * minus_i(totals[q][shift], even_row)
+            result = term if result is None else result + term
+        upper.append(result)
+    return lower + upper
+
+
+def back_kernel(parts_ref, weight_ref, table_ref, modes_ref, out_ref):
+    total = parts_ref[0, 0:32, :]
     for source in range(1, N):
-        total = total + parts_ref[source]
+        total = total + parts_ref[source, 0:32, :]
     modes_ref[...] = total
     rows = lax.broadcasted_iota(jnp.int32, (KZ, KZ * C), 0)
     lanes = lax.broadcasted_iota(jnp.int32, (KZ, KZ * C), 1)
@@ -420,7 +481,7 @@
     kz = lax.broadcasted_iota(jnp.int32, (KZ, LANES), 0)
     scale = jnp.where(kz == 0, 1.0 / CELLS, 2.0 / CELLS)
     for ky in range(2):
-        block = total[32 + ky * KZ : 32 + (ky + 1) * KZ]
+        block = total[ky * KZ : (ky + 1) * KZ]
         products = []
         for kx in range(2):
             real, imag = flat_modes(block, 2 * kx), flat_modes(block, 2 * kx + 1)
@@ -432,24 +493,29 @@
         back = scale * (nt_dot(mask, high) + nt_dot(mask, middle) + nt_dot(mask, low))
         for device in range(N):
             out_ref[device, ky * KZ : (ky + 1) * KZ, :] = back
-
-
-def weight_grad_kernel(modes_ref, out_ref):
+    inputs = input_modes_at(parts_ref, table_ref)
+    for device in range(N):
+        values = inputs[device // 2]
+        out_ref[device, 32:40, :] = values if device % 2 == 0 else pltpu.roll(values, 64, 1)
+
+
+def weight_grad_kernel(modes_ref, parts_ref, out_ref):
     rows = lax.broadcasted_iota(jnp.int32, (KZ, KZ * C), 0)
     lanes = lax.broadcasted_iota(jnp.int32, (KZ, KZ * C), 1)
     mask = jnp.where(lanes // C == rows, 1.0, 0.0).astype(BF16)
     first = lax.broadcasted_iota(jnp.int32, (1, KZ * C), 1) < C
     scale = jnp.where(first, 1.0 / CELLS, 2.0 / CELLS)
     for ky in range(2):
-        inputs = modes_ref[ky * KZ : (ky + 1) * KZ, :]
-        grads = modes_ref[32 + ky * KZ : 32 + (ky + 1) * KZ, :]
-        high, middle, low = split_3(inputs)
-        spread = tn_dot(high, mask) + tn_dot(middle, mask) + tn_dot(low, mask)
+        grads = modes_ref[ky * KZ : (ky + 1) * KZ, :]
+        spread = []
+        for part in range(2):
+            inputs = parts_ref[pl.ds(32 + 2 * ky + part, KZ, stride=40), :]
+            high, middle, low = split_3(inputs)
+            spread.append(tn_dot(high, mask) + tn_dot(middle, mask) + tn_dot(low, mask))
         for kx in range(2):
             real = scale * flat_modes(grads, 2 * kx)
             imag = scale * flat_modes(grads, 2 * kx + 1)
-            in_real = spread[(2 * kx) * C : (2 * kx + 1) * C]
-            in_imag = spread[(2 * kx + 1) * C : (2 * kx + 2) * C]
+            in_real, in_imag = [part[kx * C : (kx + 1) * C] for part in spread]
             out_ref[0, kx, ky] = (in_real * real + in_imag * imag).astype(BF16)
             out_ref[1, kx, ky] = (in_real * imag - in_imag * real).astype(BF16)
 
@@ -670,15 +736,22 @@
     )
     got = lax.ppermute(other, "pencil", swap)
     table = (SLAB_FORWARD.shape[1:], F32)
-    local, slab_forward, slab_backward = call(
+    local, slab_forward, slab_backward, input_phases = call(
         local_kernel,
         "local",
-        [((CY, LANES, NZ), F32), table, table],
-        scratch=[pltpu.SemaphoreType.DMA((2,))],
-        hbm=(3, 4),
-    )(pointwise, slope, grad, jnp.asarray(SLAB_FORWARD), jnp.asarray(SLAB_BACKWARD))
-    got, local, slab_forward, slab_backward = lax.optimization_barrier(
-        (got, local, slab_forward, slab_backward)
+        [((CY, LANES, NZ), F32), table, table, (INPUT_TABLE.shape, F32)],
+        scratch=[pltpu.SemaphoreType.DMA((3,))],
+        hbm=(3, 4, 5),
+    )(
+        pointwise,
+        slope,
+        grad,
+        jnp.asarray(SLAB_FORWARD),
+        jnp.asarray(SLAB_BACKWARD),
+        jnp.asarray(INPUT_TABLE),
+    )
+    got, local, slab_forward, slab_backward, input_phases = lax.optimization_barrier(
+        (got, local, slab_forward, slab_backward, input_phases)
     )
     to_pencil = call(combine_kernel, "combine", ((N // 2, 128, LANES), F32))(
         own_in, got_in, own, got
@@ -686,15 +759,18 @@
     from_pencil = lax.all_to_all(
         to_pencil, "pencil", 0, 0, axis_index_groups=same_core, tiled=True
     )
-    to_slab = call(slab_forward_kernel, "slab_forward", ((N, 64, LANES), F32))(
+    chunks = ((N, 40, LANES), F32)
+    to_slab = call(slab_forward_kernel, "slab_forward", chunks, scratch=[((128, LANES), F32)])(
         from_pencil, slab_forward
     )
     from_slab = lax.all_to_all(to_slab, "slab", 0, 0, tiled=True)
-    modes, to_slab = call(back_kernel, "back", [((64, LANES), F32), ((N, 32, LANES), F32)])(
-        from_slab, spectral_weight
+    modes, to_slab = call(back_kernel, "back", [((32, LANES), F32), chunks])(
+        from_slab, spectral_weight, input_phases
     )
     from_slab = lax.all_to_all(to_slab, "slab", 0, 0, tiled=True)
-    weight_grad = call(weight_grad_kernel, "weight_grad", (spectral_weight.shape, BF16))(modes)
+    weight_grad = call(weight_grad_kernel, "weight_grad", (spectral_weight.shape, BF16))(
+        modes, from_slab.reshape(N * 40, LANES)
+    )
     to_pencil = call(slab_backward_kernel, "slab_backward", half_modes)(from_slab, slab_backward)
     own = lax.all_to_all(to_pencil, "pencil", 0, 0, axis_index_groups=same_core, tiled=True)
     other = lax.ppermute(own, "pencil", swap)

time: 100 us -> 97 us (0.970)
  blocking collectives: 62.2 us -> 58.5 us
    all_to_all x2, blocking collectives: 37.7 us -> 34.4 us  [shards(): from_slab = lax.all_to_all(to_slab, 'slab', 0, 0, tiled=True)]
  transfers between devices with their start and end apart: 7 -> 7, of which waited for: 4 -> 2; matrix products, arithmetic and copies ran while one was open for 0% -> 0% of each run, Pallas kernels for 7% -> 7%
where the time goes in v4:
time: 97 us; the launch traced here: 96.5 us
  blocking collectives  58.5 us (60%)
  Pallas kernels  17.4 us (18%)
  starting transfers between devices  16.5 us (17%)
  waiting for transfers between devices  3.35 us (3%)
    all_to_all x2, blocking collectives, shards(): from_slab = lax.all_to_all(to_slab, 'slab', 0, 0, tiled=True)  34.4 us
    all_to_all x2, blocking collectives, shards(): lax.all_to_all(to_pencil, 'pencil', 0, 0, axis_index_groups=same_core, ti...  24 us
    pallas_call x12, Pallas kernels, run(): pl.pallas_call(kernel, out_shape=shapes, in_specs=specs, out_specs=[pl.Bl...  17.4 us
    ppermute x1, starting transfers between devices, shards(): after = lax.ppermute(edge_down, 'slab', down)  5.38 us
    ppermute x1, starting transfers between devices, shards(): other = lax.ppermute(own, 'pencil', swap)  3.95 us
    ppermute x1, starting transfers between devices, shards(): before = lax.ppermute(edge_up, 'slab', up)  3.82 us
    ppermute x1, waiting for transfers between devices, shards(): high = lax.ppermute(side_down, 'pencil', down)  2.32 us
  transfers between devices with their start and end apart: 7, of which 2 were waited for; matrix products, arithmetic and copies ran while one was open for 0% of the time, Pallas kernels for 7%

profile of v4, /device:TPU:1, one launch (start us, length us, event | category | flops | bytes accessed | tf_op | source)
XLA Modules:
  0.0 96.5 jit_solution(12005293554247186110)
XLA Ops:
  0.6 0.0 copy-start.1
  0.6 3.1 %field.1 = (f32[4,16,256]{2,1,0:T(8,128)S(1)}, f32[4,16,256]{2,1,0:T(8,128)S(1)}, f32[4,16,256]{2,1,0:T(8,128)S(1)}, bf16[32,4,16,256]{3,2,1,0:T(8,128)(2,1)S(1)...) custom-call(bf16[32,4,16,256]{3,2,1,0:T(8,128)(2,1)} %pre_hbm.1, ...), custom_call_target="tpu_custom_call" | custom-call | bytes 14760000 | tf_op jit(solution)/shard_map/field/pallas_call | solution.py:638
  3.8 3.8 %collective-permute-start = (f32[4,16,256]{2,1,0:T(8,128)S(1)}, f32[4,16,256]{2,1,0:T(8,128)S(1)}, u32[]{:S(2)}, u32[]{:S(2)}) collective-permute-start(f32[4,16,256]{2,1,0:T(8,128)S(1)} %get-tuple-element.33), channel_id=1, source_target_pairs={{0,16},{16,32},{32,48},{48,64},{64,80},{80,96},{96,112},{112,128},... | collective-permute-start | bytes 196616 | tf_op jit(solution)/shard_map/ppermute | solution.py:683
  7.6 5.4 %collective-permute-start.1 = (f32[4,16,256]{2,1,0:T(8,128)S(1)}, f32[4,16,256]{2,1,0:T(8,128)S(1)}, u32[]{:S(2)}, u32[]{:S(2)}) collective-permute-start(f32[4,16,256]{2,1,0:T(8,128)S(1)} %get-tuple-element.34), channel_id=1, source_target_pairs={{16,0},{32,16},{48,32},{64,48},{80,64},{96,80},{112,96},{128,112},... | collective-permute-start | bytes 196616 | tf_op jit(solution)/shard_map/ppermute | solution.py:684
  13.0 2.2 %slope.1.slope_ref = f32[2,2176,128]{2,1,0:T(8,128)S(1)} custom-call(bf16[32,4,16,256]{3,2,1,0:T(8,128)(2,1)S(1)} %get-tuple-element.35.pre_ref, f32[32,128]{1,0:T(8,128)S(1)} %get-tuple-element.36.proj_ref), custom_call_target="tpu_custom_call" | custom-call | bytes 7380000 | tf_op jit(solution)/shard_map/slope/pallas_call | solution.py:638
  15.2 2.2 %input_modes.1 = (f32[8,64,128]{2,1,0:T(8,128)S(1)}, f32[8,64,128]{2,1,0:T(8,128)S(1)}) custom-call(f32[544]{0:T(1024)S(1)} %copy-done.1, bf16[32,4,16,256]{3,2,1,0:T(8,128)(2,1)S(1)} %get-tuple-element.37.input_ref, bf16[64,256]{1,0:T(8,128)(2,1)} %constant.13.clone.table_hbm), custom_call_target="tpu_custom_call" | custom-call | bytes 7380000 | tf_op jit(solution)/shard_map/input_modes/pallas_call | solution.py:638
  17.4 1.3 %collective-permute-start.3 = (f32[32,256]{1,0:T(8,128)S(1)}, f32[32,256]{1,0:T(8,128)S(1)}, u32[]{:S(2)}, u32[]{:S(2)}) collective-permute-start(f32[32,256]{1,0:T(8,128)S(1)} %get-tuple-element.47), channel_id=1, source_target_pairs={{0,1},{1,2},{2,3},{3,4},{4,5},{5,6},{6,7},{7,8},{8,9},{9,10},{10,1... | collective-permute-start | bytes 98312 | tf_op jit(solution)/shard_map/ppermute | solution.py:708
  18.8 1.0 %collective-permute-done.3.low_ref = f32[32,256]{1,0:T(8,128)S(1)} collective-permute-done((f32[32,256]{1,0:T(8,128)S(1)}, f32[32,256]{1,0:T(8,128)S(1)}, u32[]{:S(2)}, u32[]{:S(2)}) %collective-permute-start.3) | collective-permute-done | bytes 32800 | tf_op jit(solution)/shard_map/ppermute | solution.py:708
  19.8 2.3 %collective-permute-done.4.high_ref = f32[32,256]{1,0:T(8,128)S(1)} collective-permute-done((f32[32,256]{1,0:T(8,128)S(1)}, f32[32,256]{1,0:T(8,128)S(1)}, u32[]{:S(2)}, u32[]{:S(2)}) %collective-permute-start.4) | collective-permute-done | bytes 32800 | tf_op jit(solution)/shard_map/ppermute | solution.py:709
  22.1 2.9 %grad_modes.1 = (f32[8,64,128]{2,1,0:T(8,128)S(1)}, f32[8,64,128]{2,1,0:T(8,128)S(1)}, f32[4,32,256]{2,1,0:T(8,128)S(1)}) custom-call(f32[544]{0:T(1024)S(1)} %copy-done.1, f32[4,16,256]{2,1,0:T(8,128)S(1)} %get-tuple-element.42.field_ref, bf16[4,16,256]{2,1,0:T(8,128)(2,1)S(1)} %get-tuple-element.43.coef_ref, ...), custom_call_target="tpu_custom_call" | custom-call | bytes 11070000 | tf_op jit(solution)/shard_map/grad_modes/pallas_call | solution.py:638
  25.0 1.9 %collective-permute-start.5 = (f32[8,64,128]{2,1,0:T(8,128)S(1)}, f32[8,64,128]{2,1,0:T(8,128)S(1)}, u32[]{:S(2)}, u32[]{:S(2)}) collective-permute-start(f32[8,64,128]{2,1,0:T(8,128)S(1)} %get-tuple-element.51), channel_id=1, source_target_pairs={{0,1},{1,0},{2,3},{3,2},{4,5},{5,4},{6,7},{7,6},{8,9},{9,8},{10,11... | collective-permute-start | bytes 786440 | tf_op jit(solution)/shard_map/ppermute | solution.py:737
  26.9 0.1 collective-permute-start.2
  27.0 1.5 %local.1 = (f32[16,128,256]{2,1,0:T(8,128)S(1)}, f32[128,128]{1,0:T(8,128)S(1)}, f32[128,128]{1,0:T(8,128)S(1)}, f32[512,128]{1,0:T(8,128)S(1)}) custom-call(bf16[32,32]{1,0:T(8,128)(2,1)S(1)} %copy-done.2, f32[2,2176,128]{2,1,0:T(8,128)S(1)} %slope.1.slope_ref, f32[4,32,256]{2,1,0:T(8,128)S(1)} %get-tuple-element.52.grad_ref, ...), custom_call_target="tpu_custom_call" | custom-call | bytes 3690000 | tf_op jit(solution)/shard_map/local/pallas_call | solution.py:638
  28.5 0.1 combine.1
  28.6 14.3 %all_to_all.20.parts_ref = f32[8,128,128]{2,1,0:T(8,128)S(1)} all-to-all(f32[8,128,128]{2,1,0:T(8,128)S(1)} %combine.1), channel_id=1, replica_groups={{0,2,4,6,8,10,12,14},{1,3,5,7,9,11,13,15},{16,18,20,22,24,26,28,30},{17..., dimensions={0} | all-to-all | bytes 1048576 | tf_op jit(solution)/shard_map/all_to_all | solution.py:759
  42.9 0.2 slab_forward.1
  43.2 18.3 %all_to_all.21.parts_ref = f32[16,40,128]{2,1,0:T(8,128)S(1)} all-to-all(f32[16,40,128]{2,1,0:T(8,128)S(1)} %slab_forward.1), channel_id=1, replica_groups=mesh['slab'=16,'pencil'=16] {'slab'}, dimensions={0} | all-to-all | bytes 655360 | tf_op jit(solution)/shard_map/all_to_all | solution.py:766
  61.5 0.7 back.1
  62.2 16.1 %all_to_all.22.parts_ref = f32[16,40,128]{2,1,0:T(8,128)S(1)} all-to-all(f32[16,40,128]{2,1,0:T(8,128)S(1)} %get-tuple-element.60), channel_id=1, replica_groups=mesh['slab'=16,'pencil'=16] {'slab'}, dimensions={0} | all-to-all | bytes 655360 | tf_op jit(solution)/shard_map/all_to_all | solution.py:770
  78.3 0.2 slab_backward.1
  78.5 9.7 %all_to_all.23.own_ref = f32[8,64,128]{2,1,0:T(8,128)S(1)} all-to-all(f32[8,64,128]{2,1,0:T(8,128)S(1)} %slab_backward.1), channel_id=1, replica_groups={{0,2,4,6,8,10,12,14},{1,3,5,7,9,11,13,15},{16,18,20,22,24,26,28,30},{17..., dimensions={0} | all-to-all | bytes 524288 | tf_op jit(solution)/shard_map/all_to_all | solution.py:775
  88.2 4.0 %collective-permute-start.6 = (f32[8,64,128]{2,1,0:T(8,128)S(1)}, f32[8,64,128]{2,1,0:T(8,128)S(1)}, u32[]{:S(2)}, u32[]{:S(2)}) collective-permute-start(f32[8,64,128]{2,1,0:T(8,128)S(1)} %all_to_all.23.own_ref), channel_id=1, source_target_pairs={{0,1},{1,0},{2,3},{3,2},{4,5},{5,4},{6,7},{7,6},{8,9},{9,8},{10,11... | collective-permute-start | bytes 786440 | tf_op jit(solution)/shard_map/ppermute | solution.py:776
  92.2 1.3 %weight_grad.1 = bf16[2,2,2,32,512]{4,3,2,1,0:T(8,128)(2,1)} custom-call(f32[32,128]{1,0:T(8,128)S(1)} %get-tuple-element.63.modes_ref, f32[640,128]{1,0:T(8,128)S(1)} %bitcast.1), custom_call_target="tpu_custom_call" | custom-call | bytes 3690000 | tf_op jit(solution)/shard_map/weight_grad/pallas_call | solution.py:638
  93.5 3.0 %output.1 = bf16[32,4,16,256]{3,2,1,0:T(8,128)(2,1)} custom-call(f32[544]{0:T(1024)S(1)} %copy-done.1, f32[8,64,128]{2,1,0:T(8,128)S(1)} %all_to_all.23.own_ref, f32[8,64,128]{2,1,0:T(8,128)S(1)} %collective-permute-done.6.other_ref, f32[16,128,256]{2,1,0:T(8,128)S(1)} %get-tuple-element.62.local_ref, bf16[96,256]{1,0:T(8,128)(2,1)} %constant.14.clone.table_hbm), custom_call_target="tpu_custom_call" | custom-call | bytes 3690000 | tf_op jit(solution)/shard_map/output/pallas_call | solution.py:638
  (12 shorter events, 0.1 us)
Async XLA Ops:
  0.6 14.6 %copy-start.1 = (f32[544]{0:T(1024)S(1)}, f32[544]{0:T(1024)}, u32[]{:S(2)}) copy-start(f32[544]{0:T(1024)} %constant.12.clone.phase_ref) | copy-start | bytes 6532
  3.8 13.6 %collective-permute-start = (f32[4,16,256]{2,1,0:T(8,128)S(1)}, f32[4,16,256]{2,1,0:T(8,128)S(1)}, u32[]{:S(2)}, u32[]{:S(2)}) collective-permute-start(f32[4,16,256]{2,1,0:T(8,128)S(1)} %get-tuple-element.33), channel_id=1, source_target_pairs={{0,16},{16,32},{32,48},{48,64},{64,80},{80,96},{96,112},{112,128},... | collective-permute-start | bytes 196616 | tf_op jit(solution)/shard_map/ppermute | solution.py:683
  7.6 9.8 %collective-permute-start.1 = (f32[4,16,256]{2,1,0:T(8,128)S(1)}, f32[4,16,256]{2,1,0:T(8,128)S(1)}, u32[]{:S(2)}, u32[]{:S(2)}) collective-permute-start(f32[4,16,256]{2,1,0:T(8,128)S(1)} %get-tuple-element.34), channel_id=1, source_target_pairs={{16,0},{32,16},{48,32},{64,48},{80,64},{96,80},{112,96},{128,112},... | collective-permute-start | bytes 196616 | tf_op jit(solution)/shard_map/ppermute | solution.py:684
  15.2 11.8 %copy-start.2 = (bf16[32,32]{1,0:T(8,128)(2,1)S(1)}, bf16[32,32]{1,0:T(8,128)(2,1)}, u32[]{:S(2)}) copy-start(bf16[32,32]{1,0:T(8,128)(2,1)} %pointwise_ref.1) | copy-start | bytes 6148
  17.4 2.3 %collective-permute-start.3 = (f32[32,256]{1,0:T(8,128)S(1)}, f32[32,256]{1,0:T(8,128)S(1)}, u32[]{:S(2)}, u32[]{:S(2)}) collective-permute-start(f32[32,256]{1,0:T(8,128)S(1)} %get-tuple-element.47), channel_id=1, source_target_pairs={{0,1},{1,2},{2,3},{3,4},{4,5},{5,6},{6,7},{7,8},{8,9},{9,10},{10,1... | collective-permute-start | bytes 98312 | tf_op jit(solution)/shard_map/ppermute | solution.py:708
  18.8 3.3 %collective-permute-start.4 = (f32[32,256]{1,0:T(8,128)S(1)}, f32[32,256]{1,0:T(8,128)S(1)}, u32[]{:S(2)}, u32[]{:S(2)}) collective-permute-start(f32[32,256]{1,0:T(8,128)S(1)} %get-tuple-element.48), channel_id=1, source_target_pairs={{1,0},{2,1},{3,2},{4,3},{5,4},{6,5},{7,6},{8,7},{9,8},{10,9},{11,1... | collective-permute-start | bytes 98312 | tf_op jit(solution)/shard_map/ppermute | solution.py:709
  25.0 3.5 %collective-permute-start.5 = (f32[8,64,128]{2,1,0:T(8,128)S(1)}, f32[8,64,128]{2,1,0:T(8,128)S(1)}, u32[]{:S(2)}, u32[]{:S(2)}) collective-permute-start(f32[8,64,128]{2,1,0:T(8,128)S(1)} %get-tuple-element.51), channel_id=1, source_target_pairs={{0,1},{1,0},{2,3},{3,2},{4,5},{5,4},{6,7},{7,6},{8,9},{9,8},{10,11... | collective-permute-start | bytes 786440 | tf_op jit(solution)/shard_map/ppermute | solution.py:737
  26.9 1.6 %collective-permute-start.2 = (f32[8,64,128]{2,1,0:T(8,128)S(1)}, f32[8,64,128]{2,1,0:T(8,128)S(1)}, u32[]{:S(2)}, u32[]{:S(2)}) collective-permute-start(f32[8,64,128]{2,1,0:T(8,128)S(1)} %get-tuple-element.41), channel_id=1, source_target_pairs={{0,1},{1,0},{2,3},{3,2},{4,5},{5,4},{6,7},{7,6},{8,9},{9,8},{10,11... | collective-permute-start | bytes 786440 | tf_op jit(solution)/shard_map/ppermute | solution.py:704
  28.5 33.0 %copy-start = (bf16[2,2,2,32,512]{4,3,2,1,0:T(8,128)(2,1)S(1)}, bf16[2,2,2,32,512]{4,3,2,1,0:T(8,128)(2,1)}, u32[]{:S(2)}) copy-start(bf16[2,2,2,32,512]{4,3,2,1,0:T(8,128)(2,1)} %weight_ref.1) | copy-start | bytes 786436
  88.2 5.3 %collective-permute-start.6 = (f32[8,64,128]{2,1,0:T(8,128)S(1)}, f32[8,64,128]{2,1,0:T(8,128)S(1)}, u32[]{:S(2)}, u32[]{:S(2)}) collective-permute-start(f32[8,64,128]{2,1,0:T(8,128)S(1)} %all_to_all.23.own_ref), channel_id=1, source_target_pairs={{0,1},{1,0},{2,3},{3,2},{4,5},{5,4},{6,7},{7,6},{8,9},{9,8},{10,11... | collective-permute-start | bytes 786440 | tf_op jit(solution)/shard_map/ppermute | solution.py:776

commit v5 on v4

--- a/solution.py
+++ b/solution.py
@@ -45,7 +45,8 @@
 def pencil_phases():
     position = 16.0 * np.arange(N)[:, None] + 7.5
     angles = 2.0 * math.pi * np.arange(17)[None, :] * position / NY
-    return np.concatenate([np.cos(angles), np.sin(angles)], axis=1).astype(np.float32).reshape(-1)
+    rows = np.concatenate([np.cos(angles), np.sin(angles), np.zeros((N, 6))], axis=1)
+    return np.repeat(rows[:, :, None], LANES, axis=2).astype(np.float32)
 
 
 def slab_tables():
@@ -91,17 +92,14 @@
 INPUT_TABLE = input_table()
 
 
-def normal_tail(values):
-    size = jnp.abs(values)
-    bell = jnp.exp(-0.5 * values * values)
-    denominator = 1.0 + (0.3275911 / math.sqrt(2.0)) * size
-    t = pl.reciprocal(denominator, approx=True)
-    t = t * (2.0 - denominator * t)
-    poly = 0.5 * 1.061405429 * t - 0.5 * 1.453152027
-    poly = poly * t + 0.5 * 1.421413741
-    poly = poly * t - 0.5 * 0.284496736
-    poly = poly * t + 0.5 * 0.254829592
-    return bell, poly * t * bell
+def by_parity(position, function, first_ref, second_ref):
+    @pl.when(position % 2 == 0)
+    def _():
+        function((first_ref, second_ref))
+
+    @pl.when(position % 2 == 1)
+    def _():
+        function((second_ref, first_ref))
 
 
 def field_kernel(
@@ -110,14 +108,18 @@
     source_hbm,
     proj_hbm,
     input_hbm,
+    phase_hbm,
+    table_hbm,
     field_ref,
-    up_ref,
-    down_ref,
+    edge_a_ref,
+    edge_b_ref,
     pre_ref,
     coef_ref,
     source_ref,
     input_ref,
     proj_tile_ref,
+    phase_ref,
+    table_ref,
     proj_ref,
     sems,
 ):
@@ -129,6 +131,9 @@
     copies.append(pltpu.make_async_copy(coef_hbm, coef_ref, sems.at[CHUNKS + 1]))
     copies.append(pltpu.make_async_copy(source_hbm, source_ref, sems.at[CHUNKS + 2]))
     copies.append(pltpu.make_async_copy(input_hbm, input_ref, sems.at[CHUNKS + 3]))
+    phases = phase_hbm.at[lax.axis_index("pencil")]
+    copies.append(pltpu.make_async_copy(phases, phase_ref, sems.at[CHUNKS + 4]))
+    copies.append(pltpu.make_async_copy(table_hbm, table_ref, sems.at[CHUNKS + 5]))
     for copy in copies:
         copy.start()
     copies[0].wait()
@@ -137,8 +142,8 @@
 
     def add_channel(c, total):
         values = pre_ref[c].astype(F32)
-        _, tail = normal_tail(values)
-        return total + proj_ref[c] * (jnp.maximum(values, 0.0) - jnp.abs(values) * tail)
+        both = values + values * lax.erf(values * math.sqrt(0.5))
+        return total + (0.5 * proj_ref[c]) * both
 
     total = jnp.zeros((CX, CY, NZ), F32)
     for i in range(CHUNKS):
@@ -147,19 +152,47 @@
     for copy in copies[1 + CHUNKS :]:
         copy.wait()
     field_ref[...] = total
-    up_ref[0:2] = total[2:4]
-    down_ref[0:2] = total[0:2]
-    up_ref[2] = coef_ref[3].astype(F32)
-    up_ref[3] = source_ref[3].astype(F32)
-    down_ref[2] = coef_ref[0].astype(F32)
-    down_ref[3] = source_ref[0].astype(F32)
-
-
-def slope_kernel(pre_ref, proj_ref, slope_ref):
+
+    def edges(refs):
+        up_ref, down_ref = refs
+        up_ref[0:2] = total[2:4]
+        down_ref[0:2] = total[0:2]
+        up_ref[2] = coef_ref[3].astype(F32)
+        up_ref[3] = source_ref[3].astype(F32)
+        down_ref[2] = coef_ref[0].astype(F32)
+        down_ref[3] = source_ref[0].astype(F32)
+
+    by_parity(lax.axis_index("slab"), edges, edge_a_ref, edge_b_ref)
+
+
+def slope_kernel(
+    pre_ref,
+    proj_ref,
+    forward_hbm,
+    backward_hbm,
+    input_hbm,
+    depth_hbm,
+    slope_ref,
+    forward_ref,
+    backward_ref,
+    input_ref,
+    depth_ref,
+    sems,
+):
+    slab = lax.axis_index("slab")
+    copies = [
+        pltpu.make_async_copy(forward_hbm.at[slab], forward_ref, sems.at[0]),
+        pltpu.make_async_copy(backward_hbm.at[slab], backward_ref, sems.at[1]),
+        pltpu.make_async_copy(input_hbm, input_ref, sems.at[2]),
+        pltpu.make_async_copy(depth_hbm, depth_ref, sems.at[3]),
+    ]
+    for copy in copies:
+        copy.start()
+
     def one_channel(c, carry):
         values = pre_ref[c].astype(F32)
-        bell, tail = normal_tail(values)
-        below = jnp.where(values >= 0.0, 1.0 - tail, tail)
+        below = 0.5 + 0.5 * lax.erf(values * math.sqrt(0.5))
+        bell = jnp.exp(-0.5 * values * values)
         slope = below + values * (bell * (1.0 / math.sqrt(2.0 * math.pi)))
         weight = proj_ref[pl.ds(c, 1), :]
         for x in range(CX):
@@ -169,6 +202,8 @@
         return carry
 
     lax.fori_loop(0, C, one_channel, 0, unroll=2)
+    for copy in copies:
+        copy.wait()
 
 
 def nt_dot(left, right):
@@ -179,7 +214,7 @@
     return lax.dot_general(left, right, (((0,), (0,)), ((), ())), preferred_element_type=F32)
 
 
-def pencil_forward(modes_ref, phase_ref, position, out_refs):
+def pencil_forward(modes_ref, phase_ref, out_refs):
     for half in range(2):
         sums, diffs = [], []
         for part in range(2):
@@ -192,8 +227,8 @@
             cosines = [math.cos(2.0 * math.pi * k * (7.5 - j) / NY) for j in range(8)]
             sines = [math.sin(2.0 * math.pi * k * (7.5 - j) / NY) for j in range(8)]
             even = [sum(w * v for w, v in zip(cosines, part)) for part in sums]
-            w_cos = phase_ref[position * 34 + k]
-            w_sin = phase_ref[position * 34 + 17 + k]
+            w_cos = phase_ref[k : k + 1, :]
+            w_sin = phase_ref[17 + k : 18 + k, :]
             if k == 0:
                 results = [(0, even[0], even[1], w_sin)]
             else:
@@ -208,34 +243,19 @@
                 out_ref[index // 4, pl.ds(row + KZ, 8), :] = w_cos * imag - sin * real
 
 
-def by_core(position, function, own_ref, other_ref):
-    @pl.when(position % 2 == 0)
-    def _():
-        function((own_ref, other_ref))
-
-    @pl.when(position % 2 == 1)
-    def _():
-        function((other_ref, own_ref))
-
-
 def input_kernel(
     phase_ref,
     input_ref,
-    table_hbm,
+    table_ref,
     own_ref,
     other_ref,
     rows_ref,
     modes_ref,
-    table_ref,
-    sem,
 ):
-    copy = pltpu.make_async_copy(table_hbm, table_ref, sem)
-    copy.start()
     for side in range(2):
         for c in range(C):
             piece = input_ref[c, :, :, side * 128 : (side + 1) * 128].astype(F32)
             rows_ref[side, c * PITCH : c * PITCH + CX * CY, :] = piece.reshape(CX * CY, 128)
-    copy.wait()
     for y in range(CY):
         sides = [
             jnp.concatenate(
@@ -247,30 +267,41 @@
         both = nt_dot(table_ref[...], values)
         modes_ref[y] = both[:32] + both[32:]
     position = lax.axis_index("pencil")
-    forward = functools.partial(pencil_forward, modes_ref, phase_ref, position)
-    by_core(position, forward, own_ref, other_ref)
-
-
-def pack_kernel(field_ref, coef_ref, source_ref, before_ref, after_ref, up_ref, down_ref):
-    for out_ref, cells, cell in ((up_ref, slice(14, 16), slice(15, 16)), (down_ref, slice(0, 2), slice(0, 1))):
-        for x in range(8):
-            if x < 2:
-                rows = before_ref[x, cells, :]
-            elif x < 6:
-                rows = field_ref[x - 2, cells, :]
-            else:
-                rows = after_ref[x - 6, cells, :]
-            out_ref[2 * x : 2 * x + 2, :] = rows
-        for base, part, own_ref in ((16, 2, coef_ref), (22, 3, source_ref)):
-            for x in range(6):
-                if x == 0:
-                    row = before_ref[part, cell, :]
-                elif x == 5:
-                    row = after_ref[part, cell, :]
+    forward = functools.partial(pencil_forward, modes_ref, phase_ref)
+    by_parity(position, forward, own_ref, other_ref)
+
+
+def pack_kernel(field_ref, coef_ref, source_ref, got_a_ref, got_b_ref, out_a_ref, out_b_ref):
+    def pack(x_refs, y_refs):
+        after_ref, before_ref = x_refs
+        up_ref, down_ref = y_refs
+        for out_ref, first in ((up_ref, 14), (down_ref, 0)):
+            cells = slice(first, first + 2)
+            cell = slice(15, 16) if first else slice(0, 1)
+            for x in range(8):
+                if x < 2:
+                    rows = before_ref[x, cells, :]
+                elif x < 6:
+                    rows = field_ref[x - 2, cells, :]
                 else:
-                    row = own_ref[x - 1].astype(F32)[cell, :]
-                out_ref[base + x : base + x + 1, :] = row
-        out_ref[28:32, :] = jnp.zeros((4, NZ), F32)
+                    rows = after_ref[x - 6, cells, :]
+                out_ref[2 * x : 2 * x + 2, :] = rows
+            for base, part, own_ref in ((16, 2, coef_ref), (22, 3, source_ref)):
+                for x in range(6):
+                    if x == 0:
+                        row = before_ref[part, cell, :]
+                    elif x == 5:
+                        row = after_ref[part, cell, :]
+                    else:
+                        row = own_ref[x - 1].astype(F32)[cell, :]
+                    out_ref[base + x : base + x + 1, :] = row
+            out_ref[28:32, :] = jnp.zeros((4, NZ), F32)
+
+    def with_x(x_refs):
+        y = lax.axis_index("pencil")
+        by_parity(y, functools.partial(pack, x_refs), out_a_ref, out_b_ref)
+
+    by_parity(lax.axis_index("slab"), with_x, got_a_ref, got_b_ref)
 
 
 def smooth(values):
@@ -295,12 +326,12 @@
     field_ref,
     coef_ref,
     source_ref,
-    before_ref,
-    after_ref,
-    low_ref,
-    high_ref,
+    x_a_ref,
+    x_b_ref,
+    y_a_ref,
+    y_b_ref,
     slope_ref,
-    table_hbm,
+    table_ref,
     own_ref,
     other_ref,
     grad_ref,
@@ -308,40 +339,43 @@
     wide_coef,
     wide_source,
     modes_ref,
-    table_ref,
-    sem,
 ):
-    copy = pltpu.make_async_copy(table_hbm, table_ref, sem)
-    copy.start()
     own = slice(8, 24)
-    wide_field[...] = jnp.zeros_like(wide_field)
-    wide_coef[...] = jnp.zeros_like(wide_coef)
-    wide_source[...] = jnp.zeros_like(wide_source)
-    wide_field[0:2, own, :] = before_ref[0:2]
     wide_field[2:6, own, :] = field_ref[...]
-    wide_field[6:8, own, :] = after_ref[0:2]
-    for x in range(8):
-        wide_field[x, 6:8, :] = low_ref[2 * x : 2 * x + 2, :]
-        wide_field[x, 24:26, :] = high_ref[2 * x : 2 * x + 2, :]
-    for wide, cells, part, base in ((wide_coef, coef_ref, 2, 16), (wide_source, source_ref, 3, 22)):
-        wide[0, own, :] = before_ref[part]
-        wide[1:5, own, :] = cells[...].astype(F32)
-        wide[5, own, :] = after_ref[part]
-        for x in range(6):
-            wide[x, 7:8, :] = low_ref[base + x : base + x + 1, :]
-            wide[x, 24:25, :] = high_ref[base + x : base + x + 1, :]
+    wide_coef[1:5, own, :] = coef_ref[...].astype(F32)
+    wide_source[1:5, own, :] = source_ref[...].astype(F32)
+
+    def x_sides(refs):
+        after_ref, before_ref = refs
+        wide_field[0:2, own, :] = before_ref[0:2]
+        wide_field[6:8, own, :] = after_ref[0:2]
+        for wide, part in ((wide_coef, 2), (wide_source, 3)):
+            wide[0, own, :] = before_ref[part]
+            wide[5, own, :] = after_ref[part]
+
+    def y_sides(refs):
+        high_ref, low_ref = refs
+        for x in range(8):
+            wide_field[x, 6:8, :] = low_ref[2 * x : 2 * x + 2, :]
+            wide_field[x, 24:26, :] = high_ref[2 * x : 2 * x + 2, :]
+        for wide, base in ((wide_coef, 16), (wide_source, 22)):
+            for x in range(6):
+                wide[x, 7:8, :] = low_ref[base + x : base + x + 1, :]
+                wide[x, 24:25, :] = high_ref[base + x : base + x + 1, :]
+
+    by_parity(lax.axis_index("slab"), x_sides, x_a_ref, x_b_ref)
+    by_parity(lax.axis_index("pencil"), y_sides, y_a_ref, y_b_ref)
     field = wide_field[...]
     center = field[1:7]
     residual = (16.0 / 3.0 - wide_coef[...]) * center - (2.0 / 3.0) * smooth(field) - wide_source[...]
     grad_ref[...] = (16.0 / 3.0 - wide_coef[1:5]) * residual[1:5] - (2.0 / 3.0) * smooth(residual)
-    copy.wait()
     for y in range(CY):
         high, low = act_parts(slope_ref, grad_ref, y)
         both = nt_dot(table_ref[...], high)
         modes_ref[y] = both[:32] + both[32:] + nt_dot(table_ref[0:32, :], low)
     position = lax.axis_index("pencil")
-    forward = functools.partial(pencil_forward, modes_ref, phase_ref, position)
-    by_core(position, forward, own_ref, other_ref)
+    forward = functools.partial(pencil_forward, modes_ref, phase_ref)
+    by_parity(position, forward, own_ref, other_ref)
 
 
 def combine_kernel(own_in_ref, got_in_ref, own_ref, got_ref, out_ref):
@@ -349,27 +383,7 @@
     out_ref[:, 64:128, :] = own_ref[...] + got_ref[...]
 
 
-def local_kernel(
-    pointwise_ref,
-    slope_ref,
-    grad_ref,
-    forward_hbm,
-    backward_hbm,
-    input_hbm,
-    out_ref,
-    forward_ref,
-    backward_ref,
-    input_ref,
-    sems,
-):
-    slab = lax.axis_index("slab")
-    copies = [
-        pltpu.make_async_copy(forward_hbm.at[slab], forward_ref, sems.at[0]),
-        pltpu.make_async_copy(backward_hbm.at[slab], backward_ref, sems.at[1]),
-        pltpu.make_async_copy(input_hbm, input_ref, sems.at[2]),
-    ]
-    for copy in copies:
-        copy.start()
+def local_kernel(pointwise_ref, slope_ref, grad_ref, out_ref):
     rows = lax.broadcasted_iota(jnp.int32, (C, LANES), 0)
     lanes = lax.broadcasted_iota(jnp.int32, (C, LANES), 1)
     repeat = jnp.where(lanes % C == rows, 1.0, 0.0).astype(BF16)
@@ -382,8 +396,6 @@
     for y in range(CY):
         act = jnp.concatenate(act_parts(slope_ref, grad_ref, y), axis=0)
         out_ref[y] = jnp.dot(wide, act, preferred_element_type=F32)
-    for copy in copies:
-        copy.wait()
 
 
 def slab_forward_kernel(parts_ref, table_ref, out_ref, raw_ref):
@@ -540,7 +552,7 @@
                     out_ref[device, pl.ds(ky * 32 + part * KZ + 8 * half, 8), :] = result
 
 
-def turn_modes(phase_ref, position, modes_ref, parts_refs):
+def turn_modes(phase_ref, modes_ref, parts_refs):
     def turned(index, w_cos, w_sin, rows):
         ref = parts_refs[index // 2 % 2]
         row = (index % 2) * 32 + rows
@@ -550,8 +562,8 @@
 
     for half in range(2):
         for k in range(17):
-            w_cos = phase_ref[position * 34 + k]
-            w_sin = phase_ref[position * 34 + 17 + k]
+            w_cos = phase_ref[k : k + 1, :]
+            w_sin = phase_ref[17 + k : 18 + k, :]
             if k == 0:
                 even = turned(0, w_cos, w_sin, 8 * half)
                 odd = None
@@ -574,19 +586,15 @@
     own_ref,
     other_ref,
     local_ref,
-    table_hbm,
+    table_ref,
     out_ref,
     modes_ref,
     rows_ref,
     flat_ref,
-    table_ref,
-    sem,
 ):
-    copy = pltpu.make_async_copy(table_hbm, table_ref, sem)
-    copy.start()
     position = lax.axis_index("pencil")
-    turn = functools.partial(turn_modes, phase_ref, position, modes_ref)
-    by_core(position, turn, own_ref, other_ref)
+    turn = functools.partial(turn_modes, phase_ref, modes_ref)
+    by_parity(position, turn, own_ref, other_ref)
     for half in range(2):
         for y in range(8):
             even = [modes_ref[half, 0, 0, 0], modes_ref[half, 0, 0, 1]]
@@ -604,7 +612,6 @@
             rows_ref[y, more, :] = even[1] + odd[0]
             rows_ref[15 - y, rows, :] = even[0] + odd[1]
             rows_ref[15 - y, more, :] = even[1] - odd[0]
-    copy.wait()
     for y in range(CY):
         values = rows_ref[y]
         high = values.astype(BF16)
@@ -655,15 +662,22 @@
 def shards(
     layer_input, pre_activation, coefficient, source, projection, pointwise, spectral_weight
 ):
-    up = [(i, (i + 1) % N) for i in range(N)]
-    down = [(j, i) for i, j in up]
     swap = [(i, i ^ 1) for i in range(N)]
+    swap_odd = [(i, (i + 1 if i % 2 else i - 1) % N) for i in range(N)]
     same_core = [[i for i in range(N) if i % 2 == core] for core in range(2)]
-    phases = jnp.asarray(PENCIL_PHASES)
-    depth_forward = jnp.asarray(DEPTH_FORWARD)
-    depth_backward = jnp.asarray(DEPTH_BACKWARD)
     edge = ((4, CY, NZ), F32)
-    field, edge_up, edge_down, pre_activation, coefficient, source, layer_input, proj_tile = call(
+    (
+        field,
+        edge_a,
+        edge_b,
+        pre_activation,
+        coefficient,
+        source,
+        layer_input,
+        proj_tile,
+        phases,
+        depth_forward,
+    ) = call(
         field_kernel,
         "field",
         [
@@ -675,14 +689,45 @@
             ((CX, CY, NZ), BF16),
             ((C, CX, CY, NZ), BF16),
             ((C, 128), F32),
+            (PENCIL_PHASES.shape[1:], F32),
+            (DEPTH_FORWARD.shape, BF16),
         ],
-        scratch=[pltpu.SMEM((C,), F32), pltpu.SemaphoreType.DMA((CHUNKS + 4,))],
-        hbm=(0, 1, 2, 3, 4),
+        scratch=[pltpu.SMEM((C,), F32), pltpu.SemaphoreType.DMA((CHUNKS + 6,))],
+        hbm=(0, 1, 2, 3, 4, 5, 6),
         us=4,
-    )(pre_activation, coefficient, source, projection, layer_input)
-    before = lax.ppermute(edge_up, "slab", up)
-    after = lax.ppermute(edge_down, "slab", down)
-    slope = call(slope_kernel, "slope", ((2, CY * Y_PITCH, 128), F32), us=2)(pre_activation, proj_tile)
+    )(
+        pre_activation,
+        coefficient,
+        source,
+        projection,
+        layer_input,
+        jnp.asarray(PENCIL_PHASES),
+        jnp.asarray(DEPTH_FORWARD),
+    )
+    x_a = lax.ppermute(edge_a, "slab", swap)
+    x_b = lax.ppermute(edge_b, "slab", swap_odd)
+    table = (SLAB_FORWARD.shape[1:], F32)
+    slope, slab_forward, slab_backward, input_phases, depth_backward = call(
+        slope_kernel,
+        "slope",
+        [
+            ((2, CY * Y_PITCH, 128), F32),
+            table,
+            table,
+            (INPUT_TABLE.shape, F32),
+            (DEPTH_BACKWARD.shape, BF16),
+        ],
+        scratch=[pltpu.SemaphoreType.DMA((4,))],
+        hbm=(2, 3, 4, 5),
+        us=2,
+    )(
+        pre_activation,
+        proj_tile,
+        jnp.asarray(SLAB_FORWARD),
+        jnp.asarray(SLAB_BACKWARD),
+        jnp.asarray(INPUT_TABLE),
+        jnp.asarray(DEPTH_BACKWARD),
+    )
     half_modes = ((N // 2, 64, LANES), F32)
     own_in, other_in = call(
         input_kernel,
@@ -691,22 +736,19 @@
         scratch=[
             ((2, C * PITCH, 128), F32),
             ((CY, 32, LANES), F32),
-            (DEPTH_FORWARD.shape, BF16),
-            pltpu.SemaphoreType.DMA(()),
         ],
-        scalars=(0,),
-        hbm=(2,),
         us=2,
     )(phases, layer_input, depth_forward)
-    before, after, slope, own_in, other_in = lax.optimization_barrier(
-        (before, after, slope, own_in, other_in)
+    x_a, x_b, slope, own_in, other_in = lax.optimization_barrier(
+        (x_a, x_b, slope, own_in, other_in)
     )
     got_in = lax.ppermute(other_in, "pencil", swap)
-    side_up, side_down = call(pack_kernel, "pack", [((32, NZ), F32), ((32, NZ), F32)])(
-        field, coefficient, source, before, after
-    )
-    low = lax.ppermute(side_up, "pencil", up)
-    high = lax.ppermute(side_down, "pencil", down)
+    side_a, side_b = call(pack_kernel, "pack", [((32, NZ), F32), ((32, NZ), F32)])(
+        field, coefficient, source, x_a, x_b
+    )
+    y_a = lax.ppermute(side_a, "pencil", swap)
+    y_b = lax.ppermute(side_b, "pencil", swap_odd)
+    y_a, y_b, got_in = lax.optimization_barrier((y_a, y_b, got_in))
     own, other, grad = call(
         grad_kernel,
         "grad_modes",
@@ -716,43 +758,23 @@
             ((6, 32, NZ), F32),
             ((6, 32, NZ), F32),
             ((CY, 32, LANES), F32),
-            (DEPTH_FORWARD.shape, BF16),
-            pltpu.SemaphoreType.DMA(()),
         ],
-        scalars=(0,),
-        hbm=(9,),
         us=3,
     )(
         phases,
         field,
         coefficient,
         source,
-        before,
-        after,
-        low,
-        high,
+        x_a,
+        x_b,
+        y_a,
+        y_b,
         slope,
         depth_forward,
     )
     got = lax.ppermute(other, "pencil", swap)
-    table = (SLAB_FORWARD.shape[1:], F32)
-    local, slab_forward, slab_backward, input_phases = call(
-        local_kernel,
-        "local",
-        [((CY, LANES, NZ), F32), table, table, (INPUT_TABLE.shape, F32)],
-        scratch=[pltpu.SemaphoreType.DMA((3,))],
-        hbm=(3, 4, 5),
-    )(
-        pointwise,
-        slope,
-        grad,
-        jnp.asarray(SLAB_FORWARD),
-        jnp.asarray(SLAB_BACKWARD),
-        jnp.asarray(INPUT_TABLE),
-    )
-    got, local, slab_forward, slab_backward, input_phases = lax.optimization_barrier(
-        (got, local, slab_forward, slab_backward, input_phases)
-    )
+    local = call(local_kernel, "local", ((CY, LANES, NZ), F32))(pointwise, slope, grad)
+    got, local = lax.optimization_barrier((got, local))
     to_pencil = call(combine_kernel, "combine", ((N // 2, 128, LANES), F32))(
         own_in, got_in, own, got
     )
@@ -782,11 +804,7 @@
             ((2, 2, 17, 2, 8, LANES), F32),
             ((CY, 32, LANES), F32),
             ((2, C * PITCH, 128), F32),
-            (DEPTH_BACKWARD.shape, BF16),
-            pltpu.SemaphoreType.DMA(()),
         ],
-        scalars=(0,),
-        hbm=(4,),
     )(phases, own, other, local, depth_backward)
     return (input_grad, weight_grad)
 

time: 97 us -> 92.6 us (0.955)
  Pallas kernels: 17.4 us -> 10.4 us
  starting transfers between devices: 16.5 us -> 18.8 us
  blocking collectives: 58.5 us -> 60 us
  waiting for transfers between devices: 3.35 us -> 2.28 us
    pallas_call x12, Pallas kernels: 17.4 us -> 10.4 us  [run(): pl.pallas_call(kernel, out_shape=shapes, in_specs=specs, out_specs=[pl.Bl...]
    ppermute x4, waiting for transfers between devices: 3.34 us -> 1.76 us  [the longest x1 1.75 us: shards(): y_b = lax.ppermute(side_b, 'pencil', swap_odd)]
    ppermute x1, starting transfers between devices: 0.1 us -> 1.37 us  [shards(): got_in = lax.ppermute(other_in, 'pencil', swap)]
    all_to_all x2, blocking collectives: 24 us -> 25 us  [shards(): lax.all_to_all(to_pencil, 'pencil', 0, 0, axis_index_groups=same_core, ti...]
  transfers between devices with their start and end apart: 7 -> 7, of which waited for: 2 -> 2; matrix products, arithmetic and copies ran while one was open for 0% -> 0% of each run, Pallas kernels for 7% -> 4%
where the time goes in v5:
time: 92.6 us; the launch traced here: 92.3 us
  blocking collectives  60 us (65%)
  starting transfers between devices  18.8 us (20%)
  Pallas kernels  10.4 us (11%)
  waiting for transfers between devices  2.28 us (2%)
    all_to_all x2, blocking collectives, shards(): from_slab = lax.all_to_all(to_slab, 'slab', 0, 0, tiled=True)  35 us
    all_to_all x2, blocking collectives, shards(): lax.all_to_all(to_pencil, 'pencil', 0, 0, axis_index_groups=same_core, ti...  25 us
    pallas_call x12, Pallas kernels, run(): pl.pallas_call(kernel, out_shape=shapes, in_specs=specs, out_specs=[pl.Bl...  10.4 us
    ppermute x1, starting transfers between devices, shards(): x_b = lax.ppermute(edge_b, 'slab', swap_odd)  5.39 us
    ppermute x1, starting transfers between devices, shards(): other = lax.ppermute(own, 'pencil', swap)  3.88 us
    ppermute x1, starting transfers between devices, shards(): x_a = lax.ppermute(edge_a, 'slab', swap)  3.83 us
    ppermute x1, starting transfers between devices, shards(): got = lax.ppermute(other, 'pencil', swap)  2.61 us
  transfers between devices with their start and end apart: 7, of which 2 were waited for; matrix products, arithmetic and copies ran while one was open for 0% of the time, Pallas kernels for 4%

profile of v5, /device:TPU:1, one launch (start us, length us, event | category | flops | bytes accessed | tf_op | source)
XLA Modules:
  0.0 92.3 jit_solution(9158809294779894373)
XLA Ops:
  0.6 1.7 %field.1 = (f32[4,16,256]{2,1,0:T(8,128)S(1)}, f32[4,16,256]{2,1,0:T(8,128)S(1)}, f32[4,16,256]{2,1,0:T(8,128)S(1)}, bf16[32,4,16,256]{3,2,1,0:T(8,128)(2,1)S(1)...) custom-call(bf16[32,4,16,256]{3,2,1,0:T(8,128)(2,1)} %pre_hbm.1, ...), custom_call_target="tpu_custom_call" | custom-call | bytes 14760000 | tf_op jit(solution)/shard_map/field/pallas_call | solution.py:645
  2.3 3.8 %collective-permute-start = (f32[4,16,256]{2,1,0:T(8,128)S(1)}, f32[4,16,256]{2,1,0:T(8,128)S(1)}, u32[]{:S(2)}, u32[]{:S(2)}) collective-permute-start(f32[4,16,256]{2,1,0:T(8,128)S(1)} %get-tuple-element.37), channel_id=1, source_target_pairs={{0,16},{16,0},{32,48},{48,32},{64,80},{80,64},{96,112},{112,96},{1... | collective-permute-start | bytes 196616 | tf_op jit(solution)/shard_map/ppermute | solution.py:707
  6.2 5.4 %collective-permute-start.1 = (f32[4,16,256]{2,1,0:T(8,128)S(1)}, f32[4,16,256]{2,1,0:T(8,128)S(1)}, u32[]{:S(2)}, u32[]{:S(2)}) collective-permute-start(f32[4,16,256]{2,1,0:T(8,128)S(1)} %get-tuple-element.38), channel_id=1, source_target_pairs={{0,240},{16,32},{32,16},{48,64},{64,48},{80,96},{96,80},{112,128},... | collective-permute-start | bytes 196616 | tf_op jit(solution)/shard_map/ppermute | solution.py:708
  11.6 0.9 input_modes.1
  12.5 1.1 %slope.1 = (f32[2,2176,128]{2,1,0:T(8,128)S(1)}, f32[128,128]{1,0:T(8,128)S(1)}, f32[128,128]{1,0:T(8,128)S(1)}, f32[512,128]{1,0:T(8,128)S(1)}, bf16[96,256]{1,0:T(8,128)(2,1)S(1)}) custom-call(bf16[32,4,16,256]{3,2,1,0:T(8,128)(2,1)S(1)} %get-tuple-element.39.pre_ref, f32[32,128]{1,0:T(8,128)S(1)} %get-tuple-element.40.proj_ref, ...), custom_call_target="tpu_custom_call" | custom-call | bytes 7380000 | tf_op jit(solution)/shard_map/slope/pallas_call | solution.py:645
  13.6 1.4 %collective-permute-start.4 = (f32[8,64,128]{2,1,0:T(8,128)S(1)}, f32[8,64,128]{2,1,0:T(8,128)S(1)}, u32[]{:S(2)}, u32[]{:S(2)}) collective-permute-start(f32[8,64,128]{2,1,0:T(8,128)S(1)} %get-tuple-element.54), channel_id=1, source_target_pairs={{0,1},{1,0},{2,3},{3,2},{4,5},{5,4},{6,7},{7,6},{8,9},{9,8},{10,11... | collective-permute-start | bytes 786440 | tf_op jit(solution)/shard_map/ppermute | solution.py:745
  15.0 0.1 collective-permute-start.2
  15.1 1.7 %collective-permute-start.3 = (f32[32,256]{1,0:T(8,128)S(1)}, f32[32,256]{1,0:T(8,128)S(1)}, u32[]{:S(2)}, u32[]{:S(2)}) collective-permute-start(f32[32,256]{1,0:T(8,128)S(1)} %get-tuple-element.53), channel_id=1, source_target_pairs={{0,15},{1,2},{2,1},{3,4},{4,3},{5,6},{6,5},{7,8},{8,7},{9,10},{10,... | collective-permute-start | bytes 98312 | tf_op jit(solution)/shard_map/ppermute | solution.py:750
  16.8 1.8 %collective-permute-done.3.y_b_ref = f32[32,256]{1,0:T(8,128)S(1)} collective-permute-done((f32[32,256]{1,0:T(8,128)S(1)}, f32[32,256]{1,0:T(8,128)S(1)}, u32[]{:S(2)}, u32[]{:S(2)}) %collective-permute-start.3) | collective-permute-done | bytes 32800 | tf_op jit(solution)/shard_map/ppermute | solution.py:750
  18.6 1.6 %grad_modes.1 = (f32[8,64,128]{2,1,0:T(8,128)S(1)}, f32[8,64,128]{2,1,0:T(8,128)S(1)}, f32[4,32,256]{2,1,0:T(8,128)S(1)}) custom-call(f32[40,128]{1,0:T(8,128)S(1)} %get-tuple-element.36.phase_ref, f32[4,16,256]{2,1,0:T(8,128)S(1)} %get-tuple-element.47.field_ref, bf16[4,16,256]{2,1,0:T(8,128)(2,1)S(1)} %get-tuple-element.48.coef_ref, ...), custom_call_target="tpu_custom_call" | custom-call | bytes 11070000 | tf_op jit(solution)/shard_map/grad_modes/pallas_call | solution.py:645
  20.2 2.6 %collective-permute-start.5 = (f32[8,64,128]{2,1,0:T(8,128)S(1)}, f32[8,64,128]{2,1,0:T(8,128)S(1)}, u32[]{:S(2)}, u32[]{:S(2)}) collective-permute-start(f32[8,64,128]{2,1,0:T(8,128)S(1)} %get-tuple-element.60), channel_id=1, source_target_pairs={{0,1},{1,0},{2,3},{3,2},{4,5},{5,4},{6,7},{7,6},{8,9},{9,8},{10,11... | collective-permute-start | bytes 786440 | tf_op jit(solution)/shard_map/ppermute | solution.py:775
  22.8 0.6 local.1.local_ref
  23.4 0.5 collective-permute-done.5.got_ref
  24.0 0.1 combine.1
  24.0 13.7 %all_to_all.20.parts_ref = f32[8,128,128]{2,1,0:T(8,128)S(1)} all-to-all(f32[8,128,128]{2,1,0:T(8,128)S(1)} %combine.1), channel_id=1, replica_groups={{0,2,4,6,8,10,12,14},{1,3,5,7,9,11,13,15},{16,18,20,22,24,26,28,30},{17..., dimensions={0} | all-to-all | bytes 1048576 | tf_op jit(solution)/shard_map/all_to_all | solution.py:781
  37.7 0.2 slab_forward.1
  37.9 19.6 %all_to_all.21.parts_ref = f32[16,40,128]{2,1,0:T(8,128)S(1)} all-to-all(f32[16,40,128]{2,1,0:T(8,128)S(1)} %slab_forward.1), channel_id=1, replica_groups=mesh['slab'=16,'pencil'=16] {'slab'}, dimensions={0} | all-to-all | bytes 655360 | tf_op jit(solution)/shard_map/all_to_all | solution.py:788
  57.5 0.7 back.1
  58.2 15.4 %all_to_all.22.parts_ref = f32[16,40,128]{2,1,0:T(8,128)S(1)} all-to-all(f32[16,40,128]{2,1,0:T(8,128)S(1)} %get-tuple-element.65), channel_id=1, replica_groups=mesh['slab'=16,'pencil'=16] {'slab'}, dimensions={0} | all-to-all | bytes 655360 | tf_op jit(solution)/shard_map/all_to_all | solution.py:792
  73.6 0.2 slab_backward.1
  73.8 11.4 %all_to_all.23.own_ref = f32[8,64,128]{2,1,0:T(8,128)S(1)} all-to-all(f32[8,64,128]{2,1,0:T(8,128)S(1)} %slab_backward.1), channel_id=1, replica_groups={{0,2,4,6,8,10,12,14},{1,3,5,7,9,11,13,15},{16,18,20,22,24,26,28,30},{17..., dimensions={0} | all-to-all | bytes 524288 | tf_op jit(solution)/shard_map/all_to_all | solution.py:797
  85.2 3.9 %collective-permute-start.6 = (f32[8,64,128]{2,1,0:T(8,128)S(1)}, f32[8,64,128]{2,1,0:T(8,128)S(1)}, u32[]{:S(2)}, u32[]{:S(2)}) collective-permute-start(f32[8,64,128]{2,1,0:T(8,128)S(1)} %all_to_all.23.own_ref), channel_id=1, source_target_pairs={{0,1},{1,0},{2,3},{3,2},{4,5},{5,4},{6,7},{7,6},{8,9},{9,8},{10,11... | collective-permute-start | bytes 786440 | tf_op jit(solution)/shard_map/ppermute | solution.py:798
  89.1 1.3 %weight_grad.1 = bf16[2,2,2,32,512]{4,3,2,1,0:T(8,128)(2,1)} custom-call(f32[32,128]{1,0:T(8,128)S(1)} %get-tuple-element.69.modes_ref, f32[640,128]{1,0:T(8,128)S(1)} %bitcast.1), custom_call_target="tpu_custom_call" | custom-call | bytes 3690000 | tf_op jit(solution)/shard_map/weight_grad/pallas_call | solution.py:645
  90.4 1.9 %output.1 = bf16[32,4,16,256]{3,2,1,0:T(8,128)(2,1)} custom-call(f32[40,128]{1,0:T(8,128)S(1)} %get-tuple-element.36.phase_ref, f32[8,64,128]{2,1,0:T(8,128)S(1)} %all_to_all.23.own_ref, f32[8,64,128]{2,1,0:T(8,128)S(1)} %collective-permute-done.6.other_ref, f32[16,128,256]{2,1,0:T(8,128)S(1)} %local.1.local_ref, bf16[96,256]{1,0:T(8,128)(2,1)S(1)} %get-tuple-element.68.table_ref), custom_call_target="tpu_custom_call" | custom-call | bytes 3690000 | tf_op jit(solution)/shard_map/output/pallas_call | solution.py:645
  (10 shorter events, 0.1 us)
Async XLA Ops:
  2.3 11.3 %collective-permute-start = (f32[4,16,256]{2,1,0:T(8,128)S(1)}, f32[4,16,256]{2,1,0:T(8,128)S(1)}, u32[]{:S(2)}, u32[]{:S(2)}) collective-permute-start(f32[4,16,256]{2,1,0:T(8,128)S(1)} %get-tuple-element.37), channel_id=1, source_target_pairs={{0,16},{16,0},{32,48},{48,32},{64,80},{80,64},{96,112},{112,96},{1... | collective-permute-start | bytes 196616 | tf_op jit(solution)/shard_map/ppermute | solution.py:707
  6.2 7.5 %collective-permute-start.1 = (f32[4,16,256]{2,1,0:T(8,128)S(1)}, f32[4,16,256]{2,1,0:T(8,128)S(1)}, u32[]{:S(2)}, u32[]{:S(2)}) collective-permute-start(f32[4,16,256]{2,1,0:T(8,128)S(1)} %get-tuple-element.38), channel_id=1, source_target_pairs={{0,240},{16,32},{32,16},{48,64},{64,48},{80,96},{96,80},{112,128},... | collective-permute-start | bytes 196616 | tf_op jit(solution)/shard_map/ppermute | solution.py:708
  13.6 9.2 %copy-start.1 = (bf16[32,32]{1,0:T(8,128)(2,1)S(1)}, bf16[32,32]{1,0:T(8,128)(2,1)}, u32[]{:S(2)}) copy-start(bf16[32,32]{1,0:T(8,128)(2,1)} %pointwise_ref.1) | copy-start | bytes 6148
  13.6 4.9 %collective-permute-start.4 = (f32[8,64,128]{2,1,0:T(8,128)S(1)}, f32[8,64,128]{2,1,0:T(8,128)S(1)}, u32[]{:S(2)}, u32[]{:S(2)}) collective-permute-start(f32[8,64,128]{2,1,0:T(8,128)S(1)} %get-tuple-element.54), channel_id=1, source_target_pairs={{0,1},{1,0},{2,3},{3,2},{4,5},{5,4},{6,7},{7,6},{8,9},{9,8},{10,11... | collective-permute-start | bytes 786440 | tf_op jit(solution)/shard_map/ppermute | solution.py:745
  15.0 1.8 %collective-permute-start.2 = (f32[32,256]{1,0:T(8,128)S(1)}, f32[32,256]{1,0:T(8,128)S(1)}, u32[]{:S(2)}, u32[]{:S(2)}) collective-permute-start(f32[32,256]{1,0:T(8,128)S(1)} %get-tuple-element.52), channel_id=1, source_target_pairs={{0,1},{1,0},{2,3},{3,2},{4,5},{5,4},{6,7},{7,6},{8,9},{9,8},{10,11... | collective-permute-start | bytes 98312 | tf_op jit(solution)/shard_map/ppermute | solution.py:749
  15.1 3.4 %collective-permute-start.3 = (f32[32,256]{1,0:T(8,128)S(1)}, f32[32,256]{1,0:T(8,128)S(1)}, u32[]{:S(2)}, u32[]{:S(2)}) collective-permute-start(f32[32,256]{1,0:T(8,128)S(1)} %get-tuple-element.53), channel_id=1, source_target_pairs={{0,15},{1,2},{2,1},{3,4},{4,3},{5,6},{6,5},{7,8},{8,7},{9,10},{10,... | collective-permute-start | bytes 98312 | tf_op jit(solution)/shard_map/ppermute | solution.py:750
  20.2 3.8 %collective-permute-start.5 = (f32[8,64,128]{2,1,0:T(8,128)S(1)}, f32[8,64,128]{2,1,0:T(8,128)S(1)}, u32[]{:S(2)}, u32[]{:S(2)}) collective-permute-start(f32[8,64,128]{2,1,0:T(8,128)S(1)} %get-tuple-element.60), channel_id=1, source_target_pairs={{0,1},{1,0},{2,3},{3,2},{4,5},{5,4},{6,7},{7,6},{8,9},{9,8},{10,11... | collective-permute-start | bytes 786440 | tf_op jit(solution)/shard_map/ppermute | solution.py:775
  23.4 34.1 %copy-start = (bf16[2,2,2,32,512]{4,3,2,1,0:T(8,128)(2,1)S(1)}, bf16[2,2,2,32,512]{4,3,2,1,0:T(8,128)(2,1)}, u32[]{:S(2)}) copy-start(bf16[2,2,2,32,512]{4,3,2,1,0:T(8,128)(2,1)} %weight_ref.1) | copy-start | bytes 786436
  85.2 5.2 %collective-permute-start.6 = (f32[8,64,128]{2,1,0:T(8,128)S(1)}, f32[8,64,128]{2,1,0:T(8,128)S(1)}, u32[]{:S(2)}, u32[]{:S(2)}) collective-permute-start(f32[8,64,128]{2,1,0:T(8,128)S(1)} %all_to_all.23.own_ref), channel_id=1, source_target_pairs={{0,1},{1,0},{2,3},{3,2},{4,5},{5,4},{6,7},{7,6},{8,9},{9,8},{10,11... | collective-permute-start | bytes 786440 | tf_op jit(solution)/shard_map/ppermute | solution.py:798

commit v6 on v5

--- a/solution.py
+++ b/solution.py
@@ -17,6 +17,10 @@
 N = 16
 KZ = 16
 LANES = CX * C
+SLAB_ORDER = [2 * z + y for y in range(2) for z in (0, 3, 6, 1, 4, 7, 2, 5)]
+SLAB_RANK = [SLAB_ORDER.index(device) for device in range(N)]
+CHIP_ORDER = [0, 1, 3, 2, 6, 7, 5, 4]
+CHIP_RANK = [CHIP_ORDER.index(chip) for chip in range(N // 2)]
 CELLS = float(NX * NY * NZ)
 VMEM_LIMIT = 24 * 1024 * 1024
 PITCH = 68
@@ -239,8 +243,9 @@
             for index, real, imag, sin in results:
                 row = (index % 2) * 32 + 8 * half
                 out_ref = out_refs[index // 2 % 2]
-                out_ref[index // 4, pl.ds(row, 8), :] = w_cos * real + sin * imag
-                out_ref[index // 4, pl.ds(row + KZ, 8), :] = w_cos * imag - sin * real
+                chip = CHIP_RANK[index // 4]
+                out_ref[chip, pl.ds(row, 8), :] = w_cos * real + sin * imag
+                out_ref[chip, pl.ds(row + KZ, 8), :] = w_cos * imag - sin * real
 
 
 def input_kernel(
@@ -405,7 +410,7 @@
     raw_ref[0:64, :] = raw
     raw_ref[64:128, :] = jnp.zeros((64, LANES), F32)
     for kz in range(KZ):
-        out_ref[kz, 32:40, :] = raw_ref[pl.ds(kz, 8, stride=KZ), :]
+        out_ref[SLAB_RANK[kz], 32:40, :] = raw_ref[pl.ds(kz, 8, stride=KZ), :]
     for ky in range(2):
         for half in range(2):
             pieces = []
@@ -422,7 +427,7 @@
                         row = owner * 8 + d * 2 + part
                         term = pieces[part][d] * table_ref[row : row + 1, :]
                         result = term if result is None else result + term
-                out_ref[owner, pl.ds(ky * KZ + 8 * half, 8), :] = result
+                out_ref[SLAB_RANK[owner], pl.ds(ky * KZ + 8 * half, 8), :] = result
 
 
 def flat_modes(block, group):
@@ -456,7 +461,7 @@
     even_row = row % 2 == 0
     totals = [[None] * 4 for _ in range(4)]
     for source in range(N):
-        values = parts_ref[source, 32:40, :]
+        values = parts_ref[SLAB_RANK[source], 32:40, :]
         turned = minus_i(values, even_row)
         for shift in range(4):
             if shift:
@@ -508,13 +513,16 @@
     inputs = input_modes_at(parts_ref, table_ref)
     for device in range(N):
         values = inputs[device // 2]
-        out_ref[device, 32:40, :] = values if device % 2 == 0 else pltpu.roll(values, 64, 1)
+        if device % 2:
+            values = pltpu.roll(values, 64, 1)
+        out_ref[SLAB_RANK[device], 32:40, :] = values
 
 
 def weight_grad_kernel(modes_ref, parts_ref, out_ref):
     rows = lax.broadcasted_iota(jnp.int32, (KZ, KZ * C), 0)
     lanes = lax.broadcasted_iota(jnp.int32, (KZ, KZ * C), 1)
-    mask = jnp.where(lanes // C == rows, 1.0, 0.0).astype(BF16)
+    kz = sum(jnp.where(rows == rank, SLAB_ORDER[rank], 0) for rank in range(N))
+    mask = jnp.where(lanes // C == kz, 1.0, 0.0).astype(BF16)
     first = lax.broadcasted_iota(jnp.int32, (1, KZ * C), 1) < C
     scale = jnp.where(first, 1.0 / CELLS, 2.0 / CELLS)
     for ky in range(2):
@@ -537,7 +545,7 @@
         for half in range(2):
             totals = [[None] * 4, [None] * 4]
             for source in range(N):
-                values = parts_ref[source, pl.ds(ky * KZ + 8 * half, 8), :]
+                values = parts_ref[SLAB_RANK[source], pl.ds(ky * KZ + 8 * half, 8), :]
                 for d in range(4):
                     for part in range(2):
                         row = source * 8 + d * 2 + part
@@ -556,8 +564,9 @@
     def turned(index, w_cos, w_sin, rows):
         ref = parts_refs[index // 2 % 2]
         row = (index % 2) * 32 + rows
-        real = ref[index // 4, pl.ds(row, 8), :]
-        imag = ref[index // 4, pl.ds(row + KZ, 8), :]
+        chip = CHIP_RANK[index // 4]
+        real = ref[chip, pl.ds(row, 8), :]
+        imag = ref[chip, pl.ds(row + KZ, 8), :]
         return w_cos * real - w_sin * imag, w_cos * imag + w_sin * real
 
     for half in range(2):
@@ -664,7 +673,8 @@
 ):
     swap = [(i, i ^ 1) for i in range(N)]
     swap_odd = [(i, (i + 1 if i % 2 else i - 1) % N) for i in range(N)]
-    same_core = [[i for i in range(N) if i % 2 == core] for core in range(2)]
+    same_core = [[2 * chip + core for chip in CHIP_ORDER] for core in range(2)]
+    all_slabs = [SLAB_ORDER]
     edge = ((4, CY, NZ), F32)
     (
         field,
@@ -785,11 +795,11 @@
     to_slab = call(slab_forward_kernel, "slab_forward", chunks, scratch=[((128, LANES), F32)])(
         from_pencil, slab_forward
     )
-    from_slab = lax.all_to_all(to_slab, "slab", 0, 0, tiled=True)
+    from_slab = lax.all_to_all(to_slab, "slab", 0, 0, axis_index_groups=all_slabs, tiled=True)
     modes, to_slab = call(back_kernel, "back", [((32, LANES), F32), chunks])(
         from_slab, spectral_weight, input_phases
     )
-    from_slab = lax.all_to_all(to_slab, "slab", 0, 0, tiled=True)
+    from_slab = lax.all_to_all(to_slab, "slab", 0, 0, axis_index_groups=all_slabs, tiled=True)
     weight_grad = call(weight_grad_kernel, "weight_grad", (spectral_weight.shape, BF16))(
         modes, from_slab.reshape(N * 40, LANES)
     )

time: 92.6 us -> 90.8 us (0.981)
  blocking collectives: 60 us -> 56.3 us
  starting transfers between devices: 18.8 us -> 20.7 us
    all_to_all x2, blocking collectives: 35 us -> 32.8 us  [shards(): lax.all_to_all(to_slab, 'slab', 0, 0, axis_index_groups=all_slabs, tiled=...]
    ppermute x1, starting transfers between devices: 3.88 us -> 5.78 us  [shards(): other = lax.ppermute(own, 'pencil', swap)]
    all_to_all x2, blocking collectives: 25 us -> 23.5 us  [shards(): lax.all_to_all(to_pencil, 'pencil', 0, 0, axis_index_groups=same_core, ti...]
where the time goes in v6:
time: 90.8 us; the launch traced here: 90.5 us
  blocking collectives  56.3 us (62%)
  starting transfers between devices  20.7 us (23%)
  Pallas kernels  10.4 us (11%)
  waiting for transfers between devices  2.28 us (3%)
    all_to_all x2, blocking collectives, shards(): lax.all_to_all(to_slab, 'slab', 0, 0, axis_index_groups=all_slabs, tiled=...  32.8 us
    all_to_all x2, blocking collectives, shards(): lax.all_to_all(to_pencil, 'pencil', 0, 0, axis_index_groups=same_core, ti...  23.5 us
    pallas_call x12, Pallas kernels, run(): pl.pallas_call(kernel, out_shape=shapes, in_specs=specs, out_specs=[pl.Bl...  10.4 us
    ppermute x1, starting transfers between devices, shards(): other = lax.ppermute(own, 'pencil', swap)  5.78 us
    ppermute x1, starting transfers between devices, shards(): x_b = lax.ppermute(edge_b, 'slab', swap_odd)  5.39 us
    ppermute x1, starting transfers between devices, shards(): x_a = lax.ppermute(edge_a, 'slab', swap)  3.83 us
    ppermute x1, starting transfers between devices, shards(): got = lax.ppermute(other, 'pencil', swap)  2.61 us
  transfers between devices with their start and end apart: 7, of which 2 were waited for; matrix products, arithmetic and copies ran while one was open for 0% of the time, Pallas kernels for 4%

profile of v6, /device:TPU:1, one launch (start us, length us, event | category | flops | bytes accessed | tf_op | source)
XLA Modules:
  0.0 90.5 jit_solution(1539633286993371688)
XLA Ops:
  0.6 1.7 %field.1 = (f32[4,16,256]{2,1,0:T(8,128)S(1)}, f32[4,16,256]{2,1,0:T(8,128)S(1)}, f32[4,16,256]{2,1,0:T(8,128)S(1)}, bf16[32,4,16,256]{3,2,1,0:T(8,128)(2,1)S(1)...) custom-call(bf16[32,4,16,256]{3,2,1,0:T(8,128)(2,1)} %pre_hbm.1, ...), custom_call_target="tpu_custom_call" | custom-call | bytes 14760000 | tf_op jit(solution)/shard_map/field/pallas_call | solution.py:654
  2.3 3.8 %collective-permute-start = (f32[4,16,256]{2,1,0:T(8,128)S(1)}, f32[4,16,256]{2,1,0:T(8,128)S(1)}, u32[]{:S(2)}, u32[]{:S(2)}) collective-permute-start(f32[4,16,256]{2,1,0:T(8,128)S(1)} %get-tuple-element.37), channel_id=1, source_target_pairs={{0,16},{16,0},{32,48},{48,32},{64,80},{80,64},{96,112},{112,96},{1... | collective-permute-start | bytes 196616 | tf_op jit(solution)/shard_map/ppermute | solution.py:717
  6.2 5.4 %collective-permute-start.1 = (f32[4,16,256]{2,1,0:T(8,128)S(1)}, f32[4,16,256]{2,1,0:T(8,128)S(1)}, u32[]{:S(2)}, u32[]{:S(2)}) collective-permute-start(f32[4,16,256]{2,1,0:T(8,128)S(1)} %get-tuple-element.38), channel_id=1, source_target_pairs={{0,240},{16,32},{32,16},{48,64},{64,48},{80,96},{96,80},{112,128},... | collective-permute-start | bytes 196616 | tf_op jit(solution)/shard_map/ppermute | solution.py:718
  11.6 0.9 %input_modes.1 = (f32[8,64,128]{2,1,0:T(8,128)S(1)}, f32[8,64,128]{2,1,0:T(8,128)S(1)}) custom-call(f32[40,128]{1,0:T(8,128)S(1)} %get-tuple-element.36.phase_ref, bf16[32,4,16,256]{3,2,1,0:T(8,128)(2,1)S(1)} %get-tuple-element.42.input_ref, bf16[64,256]{1,0:T(8,128)(2,1)S(1)} %get-tuple-element.43.table_ref), custom_call_target="tpu_custom_call" | custom-call | bytes 7380000 | tf_op jit(solution)/shard_map/input_modes/pallas_call | solution.py:654
  12.5 1.1 %slope.1 = (f32[2,2176,128]{2,1,0:T(8,128)S(1)}, f32[128,128]{1,0:T(8,128)S(1)}, f32[128,128]{1,0:T(8,128)S(1)}, f32[512,128]{1,0:T(8,128)S(1)}, bf16[96,256]{1,0:T(8,128)(2,1)S(1)}) custom-call(bf16[32,4,16,256]{3,2,1,0:T(8,128)(2,1)S(1)} %get-tuple-element.39.pre_ref, f32[32,128]{1,0:T(8,128)S(1)} %get-tuple-element.40.proj_ref, ...), custom_call_target="tpu_custom_call" | custom-call | bytes 7380000 | tf_op jit(solution)/shard_map/slope/pallas_call | solution.py:654
  13.6 1.4 %collective-permute-start.4 = (f32[8,64,128]{2,1,0:T(8,128)S(1)}, f32[8,64,128]{2,1,0:T(8,128)S(1)}, u32[]{:S(2)}, u32[]{:S(2)}) collective-permute-start(f32[8,64,128]{2,1,0:T(8,128)S(1)} %get-tuple-element.54), channel_id=1, source_target_pairs={{0,1},{1,0},{2,3},{3,2},{4,5},{5,4},{6,7},{7,6},{8,9},{9,8},{10,11... | collective-permute-start | bytes 786440 | tf_op jit(solution)/shard_map/ppermute | solution.py:755
  15.0 0.1 collective-permute-start.2
  15.1 1.7 %collective-permute-start.3 = (f32[32,256]{1,0:T(8,128)S(1)}, f32[32,256]{1,0:T(8,128)S(1)}, u32[]{:S(2)}, u32[]{:S(2)}) collective-permute-start(f32[32,256]{1,0:T(8,128)S(1)} %get-tuple-element.53), channel_id=1, source_target_pairs={{0,15},{1,2},{2,1},{3,4},{4,3},{5,6},{6,5},{7,8},{8,7},{9,10},{10,... | collective-permute-start | bytes 98312 | tf_op jit(solution)/shard_map/ppermute | solution.py:760
  16.8 1.8 %collective-permute-done.3.y_b_ref = f32[32,256]{1,0:T(8,128)S(1)} collective-permute-done((f32[32,256]{1,0:T(8,128)S(1)}, f32[32,256]{1,0:T(8,128)S(1)}, u32[]{:S(2)}, u32[]{:S(2)}) %collective-permute-start.3) | collective-permute-done | bytes 32800 | tf_op jit(solution)/shard_map/ppermute | solution.py:760
  18.6 1.6 %grad_modes.1 = (f32[8,64,128]{2,1,0:T(8,128)S(1)}, f32[8,64,128]{2,1,0:T(8,128)S(1)}, f32[4,32,256]{2,1,0:T(8,128)S(1)}) custom-call(f32[40,128]{1,0:T(8,128)S(1)} %get-tuple-element.36.phase_ref, f32[4,16,256]{2,1,0:T(8,128)S(1)} %get-tuple-element.47.field_ref, bf16[4,16,256]{2,1,0:T(8,128)(2,1)S(1)} %get-tuple-element.48.coef_ref, ...), custom_call_target="tpu_custom_call" | custom-call | bytes 11070000 | tf_op jit(solution)/shard_map/grad_modes/pallas_call | solution.py:654
  20.2 2.6 %collective-permute-start.5 = (f32[8,64,128]{2,1,0:T(8,128)S(1)}, f32[8,64,128]{2,1,0:T(8,128)S(1)}, u32[]{:S(2)}, u32[]{:S(2)}) collective-permute-start(f32[8,64,128]{2,1,0:T(8,128)S(1)} %get-tuple-element.60), channel_id=1, source_target_pairs={{0,1},{1,0},{2,3},{3,2},{4,5},{5,4},{6,7},{7,6},{8,9},{9,8},{10,11... | collective-permute-start | bytes 786440 | tf_op jit(solution)/shard_map/ppermute | solution.py:785
  22.8 0.6 local.1.local_ref
  23.4 0.5 collective-permute-done.5.got_ref
  24.0 0.1 combine.1
  24.0 14.3 %all_to_all.20.parts_ref = f32[8,128,128]{2,1,0:T(8,128)S(1)} all-to-all(f32[8,128,128]{2,1,0:T(8,128)S(1)} %combine.1), channel_id=1, replica_groups={{0,2,6,4,12,14,10,8},{1,3,7,5,13,15,11,9},{16,18,22,20,28,30,26,24},{17..., dimensions={0} | all-to-all | bytes 1048576 | tf_op jit(solution)/shard_map/all_to_all | solution.py:791
  38.3 0.2 slab_forward.1
  38.6 16.5 %all_to_all.21.parts_ref = f32[16,40,128]{2,1,0:T(8,128)S(1)} all-to-all(f32[16,40,128]{2,1,0:T(8,128)S(1)} %slab_forward.1), channel_id=1, replica_groups={{0,96,192,32,128,224,64,160,16,112,208,48,144,240,80,176},{1,97,193,33,..., dimensions={0} | all-to-all | bytes 655360 | tf_op jit(solution)/shard_map/all_to_all | solution.py:798
  55.1 0.7 back.1
  55.8 16.4 %all_to_all.22.parts_ref = f32[16,40,128]{2,1,0:T(8,128)S(1)} all-to-all(f32[16,40,128]{2,1,0:T(8,128)S(1)} %get-tuple-element.65), channel_id=1, replica_groups={{0,96,192,32,128,224,64,160,16,112,208,48,144,240,80,176},{1,97,193,33,..., dimensions={0} | all-to-all | bytes 655360 | tf_op jit(solution)/shard_map/all_to_all | solution.py:802
  72.1 0.2 slab_backward.1
  72.3 9.2 %all_to_all.23.own_ref = f32[8,64,128]{2,1,0:T(8,128)S(1)} all-to-all(f32[8,64,128]{2,1,0:T(8,128)S(1)} %slab_backward.1), channel_id=1, replica_groups={{0,2,6,4,12,14,10,8},{1,3,7,5,13,15,11,9},{16,18,22,20,28,30,26,24},{17..., dimensions={0} | all-to-all | bytes 524288 | tf_op jit(solution)/shard_map/all_to_all | solution.py:807
  81.5 5.8 %collective-permute-start.6 = (f32[8,64,128]{2,1,0:T(8,128)S(1)}, f32[8,64,128]{2,1,0:T(8,128)S(1)}, u32[]{:S(2)}, u32[]{:S(2)}) collective-permute-start(f32[8,64,128]{2,1,0:T(8,128)S(1)} %all_to_all.23.own_ref), channel_id=1, source_target_pairs={{0,1},{1,0},{2,3},{3,2},{4,5},{5,4},{6,7},{7,6},{8,9},{9,8},{10,11... | collective-permute-start | bytes 786440 | tf_op jit(solution)/shard_map/ppermute | solution.py:808
  87.3 1.3 %weight_grad.1 = bf16[2,2,2,32,512]{4,3,2,1,0:T(8,128)(2,1)} custom-call(f32[32,128]{1,0:T(8,128)S(1)} %get-tuple-element.69.modes_ref, f32[640,128]{1,0:T(8,128)S(1)} %bitcast.1), custom_call_target="tpu_custom_call" | custom-call | bytes 3690000 | tf_op jit(solution)/shard_map/weight_grad/pallas_call | solution.py:654
  88.6 1.9 %output.1 = bf16[32,4,16,256]{3,2,1,0:T(8,128)(2,1)} custom-call(f32[40,128]{1,0:T(8,128)S(1)} %get-tuple-element.36.phase_ref, f32[8,64,128]{2,1,0:T(8,128)S(1)} %all_to_all.23.own_ref, f32[8,64,128]{2,1,0:T(8,128)S(1)} %collective-permute-done.6.other_ref, f32[16,128,256]{2,1,0:T(8,128)S(1)} %local.1.local_ref, bf16[96,256]{1,0:T(8,128)(2,1)S(1)} %get-tuple-element.68.table_ref), custom_call_target="tpu_custom_call" | custom-call | bytes 3690000 | tf_op jit(solution)/shard_map/output/pallas_call | solution.py:654
  (10 shorter events, 0.1 us)
Async XLA Ops:
  2.3 11.3 %collective-permute-start = (f32[4,16,256]{2,1,0:T(8,128)S(1)}, f32[4,16,256]{2,1,0:T(8,128)S(1)}, u32[]{:S(2)}, u32[]{:S(2)}) collective-permute-start(f32[4,16,256]{2,1,0:T(8,128)S(1)} %get-tuple-element.37), channel_id=1, source_target_pairs={{0,16},{16,0},{32,48},{48,32},{64,80},{80,64},{96,112},{112,96},{1... | collective-permute-start | bytes 196616 | tf_op jit(solution)/shard_map/ppermute | solution.py:717
  6.2 7.5 %collective-permute-start.1 = (f32[4,16,256]{2,1,0:T(8,128)S(1)}, f32[4,16,256]{2,1,0:T(8,128)S(1)}, u32[]{:S(2)}, u32[]{:S(2)}) collective-permute-start(f32[4,16,256]{2,1,0:T(8,128)S(1)} %get-tuple-element.38), channel_id=1, source_target_pairs={{0,240},{16,32},{32,16},{48,64},{64,48},{80,96},{96,80},{112,128},... | collective-permute-start | bytes 196616 | tf_op jit(solution)/shard_map/ppermute | solution.py:718
  13.6 9.2 %copy-start.1 = (bf16[32,32]{1,0:T(8,128)(2,1)S(1)}, bf16[32,32]{1,0:T(8,128)(2,1)}, u32[]{:S(2)}) copy-start(bf16[32,32]{1,0:T(8,128)(2,1)} %pointwise_ref.1) | copy-start | bytes 6148
  13.6 4.9 %collective-permute-start.4 = (f32[8,64,128]{2,1,0:T(8,128)S(1)}, f32[8,64,128]{2,1,0:T(8,128)S(1)}, u32[]{:S(2)}, u32[]{:S(2)}) collective-permute-start(f32[8,64,128]{2,1,0:T(8,128)S(1)} %get-tuple-element.54), channel_id=1, source_target_pairs={{0,1},{1,0},{2,3},{3,2},{4,5},{5,4},{6,7},{7,6},{8,9},{9,8},{10,11... | collective-permute-start | bytes 786440 | tf_op jit(solution)/shard_map/ppermute | solution.py:755
  15.0 1.8 %collective-permute-start.2 = (f32[32,256]{1,0:T(8,128)S(1)}, f32[32,256]{1,0:T(8,128)S(1)}, u32[]{:S(2)}, u32[]{:S(2)}) collective-permute-start(f32[32,256]{1,0:T(8,128)S(1)} %get-tuple-element.52), channel_id=1, source_target_pairs={{0,1},{1,0},{2,3},{3,2},{4,5},{5,4},{6,7},{7,6},{8,9},{9,8},{10,11... | collective-permute-start | bytes 98312 | tf_op jit(solution)/shard_map/ppermute | solution.py:759
  15.1 3.4 %collective-permute-start.3 = (f32[32,256]{1,0:T(8,128)S(1)}, f32[32,256]{1,0:T(8,128)S(1)}, u32[]{:S(2)}, u32[]{:S(2)}) collective-permute-start(f32[32,256]{1,0:T(8,128)S(1)} %get-tuple-element.53), channel_id=1, source_target_pairs={{0,15},{1,2},{2,1},{3,4},{4,3},{5,6},{6,5},{7,8},{8,7},{9,10},{10,... | collective-permute-start | bytes 98312 | tf_op jit(solution)/shard_map/ppermute | solution.py:760
  20.2 3.8 %collective-permute-start.5 = (f32[8,64,128]{2,1,0:T(8,128)S(1)}, f32[8,64,128]{2,1,0:T(8,128)S(1)}, u32[]{:S(2)}, u32[]{:S(2)}) collective-permute-start(f32[8,64,128]{2,1,0:T(8,128)S(1)} %get-tuple-element.60), channel_id=1, source_target_pairs={{0,1},{1,0},{2,3},{3,2},{4,5},{5,4},{6,7},{7,6},{8,9},{9,8},{10,11... | collective-permute-start | bytes 786440 | tf_op jit(solution)/shard_map/ppermute | solution.py:785
  23.4 31.6 %copy-start = (bf16[2,2,2,32,512]{4,3,2,1,0:T(8,128)(2,1)S(1)}, bf16[2,2,2,32,512]{4,3,2,1,0:T(8,128)(2,1)}, u32[]{:S(2)}) copy-start(bf16[2,2,2,32,512]{4,3,2,1,0:T(8,128)(2,1)} %weight_ref.1) | copy-start | bytes 786436
  81.5 7.1 %collective-permute-start.6 = (f32[8,64,128]{2,1,0:T(8,128)S(1)}, f32[8,64,128]{2,1,0:T(8,128)S(1)}, u32[]{:S(2)}, u32[]{:S(2)}) collective-permute-start(f32[8,64,128]{2,1,0:T(8,128)S(1)} %all_to_all.23.own_ref), channel_id=1, source_target_pairs={{0,1},{1,0},{2,3},{3,2},{4,5},{5,4},{6,7},{7,6},{8,9},{9,8},{10,11... | collective-permute-start | bytes 786440 | tf_op jit(solution)/shard_map/ppermute | solution.py:808

commit v7 on v6

--- a/solution.py
+++ b/solution.py
@@ -17,7 +17,7 @@
 N = 16
 KZ = 16
 LANES = CX * C
-SLAB_ORDER = [2 * z + y for y in range(2) for z in (0, 3, 6, 1, 4, 7, 2, 5)]
+SLAB_ORDER = [2 * (5 * i % 8) for i in range(8)] + [2 * (3 * i % 8) + 1 for i in range(8)]
 SLAB_RANK = [SLAB_ORDER.index(device) for device in range(N)]
 CHIP_ORDER = [0, 1, 3, 2, 6, 7, 5, 4]
 CHIP_RANK = [CHIP_ORDER.index(chip) for chip in range(N // 2)]

time: 90.8 us -> 90.5 us (level)
  no operation moved by 1% of the time
where the time goes in v7:
time: 90.5 us; the launch traced here: 90.2 us
  blocking collectives  56.3 us (62%)
  starting transfers between devices  20.4 us (23%)
  Pallas kernels  10.4 us (11%)
  waiting for transfers between devices  2.28 us (3%)
    all_to_all x2, blocking collectives, shards(): lax.all_to_all(to_slab, 'slab', 0, 0, axis_index_groups=all_slabs, tiled=...  33 us
    all_to_all x2, blocking collectives, shards(): lax.all_to_all(to_pencil, 'pencil', 0, 0, axis_index_groups=same_core, ti...  23.4 us
    pallas_call x12, Pallas kernels, run(): pl.pallas_call(kernel, out_shape=shapes, in_specs=specs, out_specs=[pl.Bl...  10.4 us
    ppermute x1, starting transfers between devices, shards(): other = lax.ppermute(own, 'pencil', swap)  5.46 us
    ppermute x1, starting transfers between devices, shards(): x_b = lax.ppermute(edge_b, 'slab', swap_odd)  5.39 us
    ppermute x1, starting transfers between devices, shards(): x_a = lax.ppermute(edge_a, 'slab', swap)  3.83 us
    ppermute x1, starting transfers between devices, shards(): got = lax.ppermute(other, 'pencil', swap)  2.61 us
  transfers between devices with their start and end apart: 7, of which 2 were waited for; matrix products, arithmetic and copies ran while one was open for 0% of the time, Pallas kernels for 4%

profile of v7, /device:TPU:1, one launch (start us, length us, event | category | flops | bytes accessed | tf_op | source)
XLA Modules:
  0.0 90.2 jit_solution(15472796800393691459)
XLA Ops:
  0.6 1.7 %field.1 = (f32[4,16,256]{2,1,0:T(8,128)S(1)}, f32[4,16,256]{2,1,0:T(8,128)S(1)}, f32[4,16,256]{2,1,0:T(8,128)S(1)}, bf16[32,4,16,256]{3,2,1,0:T(8,128)(2,1)S(1)...) custom-call(bf16[32,4,16,256]{3,2,1,0:T(8,128)(2,1)} %pre_hbm.1, ...), custom_call_target="tpu_custom_call" | custom-call | bytes 14760000 | tf_op jit(solution)/shard_map/field/pallas_call | solution.py:654
  2.3 3.8 %collective-permute-start = (f32[4,16,256]{2,1,0:T(8,128)S(1)}, f32[4,16,256]{2,1,0:T(8,128)S(1)}, u32[]{:S(2)}, u32[]{:S(2)}) collective-permute-start(f32[4,16,256]{2,1,0:T(8,128)S(1)} %get-tuple-element.37), channel_id=1, source_target_pairs={{0,16},{16,0},{32,48},{48,32},{64,80},{80,64},{96,112},{112,96},{1... | collective-permute-start | bytes 196616 | tf_op jit(solution)/shard_map/ppermute | solution.py:717
  6.2 5.4 %collective-permute-start.1 = (f32[4,16,256]{2,1,0:T(8,128)S(1)}, f32[4,16,256]{2,1,0:T(8,128)S(1)}, u32[]{:S(2)}, u32[]{:S(2)}) collective-permute-start(f32[4,16,256]{2,1,0:T(8,128)S(1)} %get-tuple-element.38), channel_id=1, source_target_pairs={{0,240},{16,32},{32,16},{48,64},{64,48},{80,96},{96,80},{112,128},... | collective-permute-start | bytes 196616 | tf_op jit(solution)/shard_map/ppermute | solution.py:718
  11.6 0.9 %input_modes.1 = (f32[8,64,128]{2,1,0:T(8,128)S(1)}, f32[8,64,128]{2,1,0:T(8,128)S(1)}) custom-call(f32[40,128]{1,0:T(8,128)S(1)} %get-tuple-element.36.phase_ref, bf16[32,4,16,256]{3,2,1,0:T(8,128)(2,1)S(1)} %get-tuple-element.42.input_ref, bf16[64,256]{1,0:T(8,128)(2,1)S(1)} %get-tuple-element.43.table_ref), custom_call_target="tpu_custom_call" | custom-call | bytes 7380000 | tf_op jit(solution)/shard_map/input_modes/pallas_call | solution.py:654
  12.5 1.1 %slope.1 = (f32[2,2176,128]{2,1,0:T(8,128)S(1)}, f32[128,128]{1,0:T(8,128)S(1)}, f32[128,128]{1,0:T(8,128)S(1)}, f32[512,128]{1,0:T(8,128)S(1)}, bf16[96,256]{1,0:T(8,128)(2,1)S(1)}) custom-call(bf16[32,4,16,256]{3,2,1,0:T(8,128)(2,1)S(1)} %get-tuple-element.39.pre_ref, f32[32,128]{1,0:T(8,128)S(1)} %get-tuple-element.40.proj_ref, ...), custom_call_target="tpu_custom_call" | custom-call | bytes 7380000 | tf_op jit(solution)/shard_map/slope/pallas_call | solution.py:654
  13.6 1.4 %collective-permute-start.4 = (f32[8,64,128]{2,1,0:T(8,128)S(1)}, f32[8,64,128]{2,1,0:T(8,128)S(1)}, u32[]{:S(2)}, u32[]{:S(2)}) collective-permute-start(f32[8,64,128]{2,1,0:T(8,128)S(1)} %get-tuple-element.54), channel_id=1, source_target_pairs={{0,1},{1,0},{2,3},{3,2},{4,5},{5,4},{6,7},{7,6},{8,9},{9,8},{10,11... | collective-permute-start | bytes 786440 | tf_op jit(solution)/shard_map/ppermute | solution.py:755
  15.0 0.1 collective-permute-start.2
  15.1 1.7 %collective-permute-start.3 = (f32[32,256]{1,0:T(8,128)S(1)}, f32[32,256]{1,0:T(8,128)S(1)}, u32[]{:S(2)}, u32[]{:S(2)}) collective-permute-start(f32[32,256]{1,0:T(8,128)S(1)} %get-tuple-element.53), channel_id=1, source_target_pairs={{0,15},{1,2},{2,1},{3,4},{4,3},{5,6},{6,5},{7,8},{8,7},{9,10},{10,... | collective-permute-start | bytes 98312 | tf_op jit(solution)/shard_map/ppermute | solution.py:760
  16.8 1.8 %collective-permute-done.3.y_b_ref = f32[32,256]{1,0:T(8,128)S(1)} collective-permute-done((f32[32,256]{1,0:T(8,128)S(1)}, f32[32,256]{1,0:T(8,128)S(1)}, u32[]{:S(2)}, u32[]{:S(2)}) %collective-permute-start.3) | collective-permute-done | bytes 32800 | tf_op jit(solution)/shard_map/ppermute | solution.py:760
  18.6 1.6 %grad_modes.1 = (f32[8,64,128]{2,1,0:T(8,128)S(1)}, f32[8,64,128]{2,1,0:T(8,128)S(1)}, f32[4,32,256]{2,1,0:T(8,128)S(1)}) custom-call(f32[40,128]{1,0:T(8,128)S(1)} %get-tuple-element.36.phase_ref, f32[4,16,256]{2,1,0:T(8,128)S(1)} %get-tuple-element.47.field_ref, bf16[4,16,256]{2,1,0:T(8,128)(2,1)S(1)} %get-tuple-element.48.coef_ref, ...), custom_call_target="tpu_custom_call" | custom-call | bytes 11070000 | tf_op jit(solution)/shard_map/grad_modes/pallas_call | solution.py:654
  20.2 2.6 %collective-permute-start.5 = (f32[8,64,128]{2,1,0:T(8,128)S(1)}, f32[8,64,128]{2,1,0:T(8,128)S(1)}, u32[]{:S(2)}, u32[]{:S(2)}) collective-permute-start(f32[8,64,128]{2,1,0:T(8,128)S(1)} %get-tuple-element.60), channel_id=1, source_target_pairs={{0,1},{1,0},{2,3},{3,2},{4,5},{5,4},{6,7},{7,6},{8,9},{9,8},{10,11... | collective-permute-start | bytes 786440 | tf_op jit(solution)/shard_map/ppermute | solution.py:785
  22.8 0.6 local.1.local_ref
  23.4 0.5 collective-permute-done.5.got_ref
  24.0 0.1 combine.1
  24.0 14.3 %all_to_all.20.parts_ref = f32[8,128,128]{2,1,0:T(8,128)S(1)} all-to-all(f32[8,128,128]{2,1,0:T(8,128)S(1)} %combine.1), channel_id=1, replica_groups={{0,2,6,4,12,14,10,8},{1,3,7,5,13,15,11,9},{16,18,22,20,28,30,26,24},{17..., dimensions={0} | all-to-all | bytes 1048576 | tf_op jit(solution)/shard_map/all_to_all | solution.py:791
  38.3 0.2 slab_forward.1
  38.6 16.5 %all_to_all.21.parts_ref = f32[16,40,128]{2,1,0:T(8,128)S(1)} all-to-all(f32[16,40,128]{2,1,0:T(8,128)S(1)} %slab_forward.1), channel_id=1, replica_groups={{0,160,64,224,128,32,192,96,16,112,208,48,144,240,80,176},{1,161,65,225..., dimensions={0} | all-to-all | bytes 655360 | tf_op jit(solution)/shard_map/all_to_all | solution.py:798
  55.1 0.7 back.1
  55.8 16.5 %all_to_all.22.parts_ref = f32[16,40,128]{2,1,0:T(8,128)S(1)} all-to-all(f32[16,40,128]{2,1,0:T(8,128)S(1)} %get-tuple-element.65), channel_id=1, replica_groups={{0,160,64,224,128,32,192,96,16,112,208,48,144,240,80,176},{1,161,65,225..., dimensions={0} | all-to-all | bytes 655360 | tf_op jit(solution)/shard_map/all_to_all | solution.py:802
  72.3 0.2 slab_backward.1
  72.4 9.1 %all_to_all.23.own_ref = f32[8,64,128]{2,1,0:T(8,128)S(1)} all-to-all(f32[8,64,128]{2,1,0:T(8,128)S(1)} %slab_backward.1), channel_id=1, replica_groups={{0,2,6,4,12,14,10,8},{1,3,7,5,13,15,11,9},{16,18,22,20,28,30,26,24},{17..., dimensions={0} | all-to-all | bytes 524288 | tf_op jit(solution)/shard_map/all_to_all | solution.py:807
  81.5 5.5 %collective-permute-start.6 = (f32[8,64,128]{2,1,0:T(8,128)S(1)}, f32[8,64,128]{2,1,0:T(8,128)S(1)}, u32[]{:S(2)}, u32[]{:S(2)}) collective-permute-start(f32[8,64,128]{2,1,0:T(8,128)S(1)} %all_to_all.23.own_ref), channel_id=1, source_target_pairs={{0,1},{1,0},{2,3},{3,2},{4,5},{5,4},{6,7},{7,6},{8,9},{9,8},{10,11... | collective-permute-start | bytes 786440 | tf_op jit(solution)/shard_map/ppermute | solution.py:808
  87.0 1.3 %weight_grad.1 = bf16[2,2,2,32,512]{4,3,2,1,0:T(8,128)(2,1)} custom-call(f32[32,128]{1,0:T(8,128)S(1)} %get-tuple-element.69.modes_ref, f32[640,128]{1,0:T(8,128)S(1)} %bitcast.1), custom_call_target="tpu_custom_call" | custom-call | bytes 3690000 | tf_op jit(solution)/shard_map/weight_grad/pallas_call | solution.py:654
  88.3 1.9 %output.1 = bf16[32,4,16,256]{3,2,1,0:T(8,128)(2,1)} custom-call(f32[40,128]{1,0:T(8,128)S(1)} %get-tuple-element.36.phase_ref, f32[8,64,128]{2,1,0:T(8,128)S(1)} %all_to_all.23.own_ref, f32[8,64,128]{2,1,0:T(8,128)S(1)} %collective-permute-done.6.other_ref, f32[16,128,256]{2,1,0:T(8,128)S(1)} %local.1.local_ref, bf16[96,256]{1,0:T(8,128)(2,1)S(1)} %get-tuple-element.68.table_ref), custom_call_target="tpu_custom_call" | custom-call | bytes 3690000 | tf_op jit(solution)/shard_map/output/pallas_call | solution.py:654
  (10 shorter events, 0.1 us)
Async XLA Ops:
  2.3 11.3 %collective-permute-start = (f32[4,16,256]{2,1,0:T(8,128)S(1)}, f32[4,16,256]{2,1,0:T(8,128)S(1)}, u32[]{:S(2)}, u32[]{:S(2)}) collective-permute-start(f32[4,16,256]{2,1,0:T(8,128)S(1)} %get-tuple-element.37), channel_id=1, source_target_pairs={{0,16},{16,0},{32,48},{48,32},{64,80},{80,64},{96,112},{112,96},{1... | collective-permute-start | bytes 196616 | tf_op jit(solution)/shard_map/ppermute | solution.py:717
  6.2 7.5 %collective-permute-start.1 = (f32[4,16,256]{2,1,0:T(8,128)S(1)}, f32[4,16,256]{2,1,0:T(8,128)S(1)}, u32[]{:S(2)}, u32[]{:S(2)}) collective-permute-start(f32[4,16,256]{2,1,0:T(8,128)S(1)} %get-tuple-element.38), channel_id=1, source_target_pairs={{0,240},{16,32},{32,16},{48,64},{64,48},{80,96},{96,80},{112,128},... | collective-permute-start | bytes 196616 | tf_op jit(solution)/shard_map/ppermute | solution.py:718
  13.6 9.2 %copy-start.1 = (bf16[32,32]{1,0:T(8,128)(2,1)S(1)}, bf16[32,32]{1,0:T(8,128)(2,1)}, u32[]{:S(2)}) copy-start(bf16[32,32]{1,0:T(8,128)(2,1)} %pointwise_ref.1) | copy-start | bytes 6148
  13.6 4.9 %collective-permute-start.4 = (f32[8,64,128]{2,1,0:T(8,128)S(1)}, f32[8,64,128]{2,1,0:T(8,128)S(1)}, u32[]{:S(2)}, u32[]{:S(2)}) collective-permute-start(f32[8,64,128]{2,1,0:T(8,128)S(1)} %get-tuple-element.54), channel_id=1, source_target_pairs={{0,1},{1,0},{2,3},{3,2},{4,5},{5,4},{6,7},{7,6},{8,9},{9,8},{10,11... | collective-permute-start | bytes 786440 | tf_op jit(solution)/shard_map/ppermute | solution.py:755
  15.0 1.8 %collective-permute-start.2 = (f32[32,256]{1,0:T(8,128)S(1)}, f32[32,256]{1,0:T(8,128)S(1)}, u32[]{:S(2)}, u32[]{:S(2)}) collective-permute-start(f32[32,256]{1,0:T(8,128)S(1)} %get-tuple-element.52), channel_id=1, source_target_pairs={{0,1},{1,0},{2,3},{3,2},{4,5},{5,4},{6,7},{7,6},{8,9},{9,8},{10,11... | collective-permute-start | bytes 98312 | tf_op jit(solution)/shard_map/ppermute | solution.py:759
  15.1 3.4 %collective-permute-start.3 = (f32[32,256]{1,0:T(8,128)S(1)}, f32[32,256]{1,0:T(8,128)S(1)}, u32[]{:S(2)}, u32[]{:S(2)}) collective-permute-start(f32[32,256]{1,0:T(8,128)S(1)} %get-tuple-element.53), channel_id=1, source_target_pairs={{0,15},{1,2},{2,1},{3,4},{4,3},{5,6},{6,5},{7,8},{8,7},{9,10},{10,... | collective-permute-start | bytes 98312 | tf_op jit(solution)/shard_map/ppermute | solution.py:760
  20.2 3.8 %collective-permute-start.5 = (f32[8,64,128]{2,1,0:T(8,128)S(1)}, f32[8,64,128]{2,1,0:T(8,128)S(1)}, u32[]{:S(2)}, u32[]{:S(2)}) collective-permute-start(f32[8,64,128]{2,1,0:T(8,128)S(1)} %get-tuple-element.60), channel_id=1, source_target_pairs={{0,1},{1,0},{2,3},{3,2},{4,5},{5,4},{6,7},{7,6},{8,9},{9,8},{10,11... | collective-permute-start | bytes 786440 | tf_op jit(solution)/shard_map/ppermute | solution.py:785
  23.4 31.6 %copy-start = (bf16[2,2,2,32,512]{4,3,2,1,0:T(8,128)(2,1)S(1)}, bf16[2,2,2,32,512]{4,3,2,1,0:T(8,128)(2,1)}, u32[]{:S(2)}) copy-start(bf16[2,2,2,32,512]{4,3,2,1,0:T(8,128)(2,1)} %weight_ref.1) | copy-start | bytes 786436
  81.5 6.8 %collective-permute-start.6 = (f32[8,64,128]{2,1,0:T(8,128)S(1)}, f32[8,64,128]{2,1,0:T(8,128)S(1)}, u32[]{:S(2)}, u32[]{:S(2)}) collective-permute-start(f32[8,64,128]{2,1,0:T(8,128)S(1)} %all_to_all.23.own_ref), channel_id=1, source_target_pairs={{0,1},{1,0},{2,3},{3,2},{4,5},{5,4},{6,7},{7,6},{8,9},{9,8},{10,11... | collective-permute-start | bytes 786440 | tf_op jit(solution)/shard_map/ppermute | solution.py:808

commit v8 on v7

--- a/solution.py
+++ b/solution.py
@@ -25,7 +25,7 @@
 VMEM_LIMIT = 24 * 1024 * 1024
 PITCH = 68
 Y_PITCH = LANES + 8
-CHUNKS = 4
+CHUNKS = 8
 BYTES_PER_US = 3_690_000
 
 
@@ -111,7 +111,6 @@
     coef_hbm,
     source_hbm,
     proj_hbm,
-    input_hbm,
     phase_hbm,
     table_hbm,
     field_ref,
@@ -120,7 +119,6 @@
     pre_ref,
     coef_ref,
     source_ref,
-    input_ref,
     proj_tile_ref,
     phase_ref,
     table_ref,
@@ -134,10 +132,9 @@
         copies.append(pltpu.make_async_copy(pre_hbm.at[part], pre_ref.at[part], sems.at[i]))
     copies.append(pltpu.make_async_copy(coef_hbm, coef_ref, sems.at[CHUNKS + 1]))
     copies.append(pltpu.make_async_copy(source_hbm, source_ref, sems.at[CHUNKS + 2]))
-    copies.append(pltpu.make_async_copy(input_hbm, input_ref, sems.at[CHUNKS + 3]))
     phases = phase_hbm.at[lax.axis_index("pencil")]
-    copies.append(pltpu.make_async_copy(phases, phase_ref, sems.at[CHUNKS + 4]))
-    copies.append(pltpu.make_async_copy(table_hbm, table_ref, sems.at[CHUNKS + 5]))
+    copies.append(pltpu.make_async_copy(phases, phase_ref, sems.at[CHUNKS + 3]))
+    copies.append(pltpu.make_async_copy(table_hbm, table_ref, sems.at[CHUNKS + 4]))
     for copy in copies:
         copy.start()
     copies[0].wait()
@@ -683,7 +680,6 @@
         pre_activation,
         coefficient,
         source,
-        layer_input,
         proj_tile,
         phases,
         depth_forward,
@@ -697,20 +693,18 @@
             ((C, CX, CY, NZ), BF16),
             ((CX, CY, NZ), BF16),
             ((CX, CY, NZ), BF16),
-            ((C, CX, CY, NZ), BF16),
             ((C, 128), F32),
             (PENCIL_PHASES.shape[1:], F32),
             (DEPTH_FORWARD.shape, BF16),
         ],
-        scratch=[pltpu.SMEM((C,), F32), pltpu.SemaphoreType.DMA((CHUNKS + 6,))],
-        hbm=(0, 1, 2, 3, 4, 5, 6),
+        scratch=[pltpu.SMEM((C,), F32), pltpu.SemaphoreType.DMA((CHUNKS + 5,))],
+        hbm=(0, 1, 2, 3, 4, 5),
         us=4,
     )(
         pre_activation,
         coefficient,
         source,
         projection,
-        layer_input,
         jnp.asarray(PENCIL_PHASES),
         jnp.asarray(DEPTH_FORWARD),
     )

time: 90.5 us -> 90.4 us (level)
  local copies, waits for them, and re-layouts: 0.01 us -> 1.24 us
  blocking collectives: 56.3 us -> 55.2 us
    unnamed x4 -> x6, local copies, waits for them, and re-layouts: 0.01 us -> 1.24 us
    all_to_all x2, blocking collectives: 33 us -> 31.8 us  [shards(): lax.all_to_all(to_slab, 'slab', 0, 0, axis_index_groups=all_slabs, tiled=...]
where the time goes in v8:
time: 90.4 us; the launch traced here: 90.2 us
  blocking collectives  55.2 us (61%)
  starting transfers between devices  20.4 us (23%)
  Pallas kernels  10.4 us (12%)
  waiting for transfers between devices  2.27 us (3%)
  local copies, waits for them, and re-layouts  1.24 us (1%)
    all_to_all x2, blocking collectives, shards(): lax.all_to_all(to_slab, 'slab', 0, 0, axis_index_groups=all_slabs, tiled=...  31.8 us
    all_to_all x2, blocking collectives, shards(): lax.all_to_all(to_pencil, 'pencil', 0, 0, axis_index_groups=same_core, ti...  23.4 us
    pallas_call x12, Pallas kernels, run(): pl.pallas_call(kernel, out_shape=shapes, in_specs=specs, out_specs=[pl.Bl...  10.4 us
    ppermute x1, starting transfers between devices, shards(): other = lax.ppermute(own, 'pencil', swap)  5.46 us
    ppermute x1, starting transfers between devices, shards(): x_b = lax.ppermute(edge_b, 'slab', swap_odd)  5.39 us
    ppermute x1, starting transfers between devices, shards(): x_a = lax.ppermute(edge_a, 'slab', swap)  3.83 us
    ppermute x1, starting transfers between devices, shards(): got = lax.ppermute(other, 'pencil', swap)  2.61 us
  transfers between devices with their start and end apart: 7, of which 2 were waited for; matrix products, arithmetic and copies ran while one was open for 0% of the time, Pallas kernels for 4%

profile of v8, /device:TPU:1, one launch (start us, length us, event | category | flops | bytes accessed | tf_op | source)
XLA Modules:
  0.0 90.2 jit_solution(15502790278955401962)
XLA Ops:
  0.6 1.6 %field.1 = (f32[4,16,256]{2,1,0:T(8,128)S(1)}, f32[4,16,256]{2,1,0:T(8,128)S(1)}, f32[4,16,256]{2,1,0:T(8,128)S(1)}, bf16[32,4,16,256]{3,2,1,0:T(8,128)(2,1)S(1)...) custom-call(bf16[32,4,16,256]{3,2,1,0:T(8,128)(2,1)} %pre_hbm.1, ...), custom_call_target="tpu_custom_call" | custom-call | bytes 14760000 | tf_op jit(solution)/shard_map/field/pallas_call | solution.py:651
  2.2 3.8 %collective-permute-start = (f32[4,16,256]{2,1,0:T(8,128)S(1)}, f32[4,16,256]{2,1,0:T(8,128)S(1)}, u32[]{:S(2)}, u32[]{:S(2)}) collective-permute-start(f32[4,16,256]{2,1,0:T(8,128)S(1)} %get-tuple-element.36), channel_id=1, source_target_pairs={{0,16},{16,0},{32,48},{48,32},{64,80},{80,64},{96,112},{112,96},{1... | collective-permute-start | bytes 196616 | tf_op jit(solution)/shard_map/ppermute | solution.py:711
  6.1 5.4 %collective-permute-start.1 = (f32[4,16,256]{2,1,0:T(8,128)S(1)}, f32[4,16,256]{2,1,0:T(8,128)S(1)}, u32[]{:S(2)}, u32[]{:S(2)}) collective-permute-start(f32[4,16,256]{2,1,0:T(8,128)S(1)} %get-tuple-element.37), channel_id=1, source_target_pairs={{0,240},{16,32},{32,16},{48,64},{64,48},{80,96},{96,80},{112,128},... | collective-permute-start | bytes 196616 | tf_op jit(solution)/shard_map/ppermute | solution.py:712
  11.5 1.2 %copy-done = bf16[32,4,16,256]{3,2,1,0:T(8,128)(2,1)S(1)} copy-done((bf16[32,4,16,256]{3,2,1,0:T(8,128)(2,1)S(1)}, bf16[32,4,16,256]{3,2,1,0:T(8,128)(2,1)}, u32[]{:S(2)}) %copy-start) | copy-done | bytes 1048600
  12.7 0.9 %input_modes.1 = (f32[8,64,128]{2,1,0:T(8,128)S(1)}, f32[8,64,128]{2,1,0:T(8,128)S(1)}) custom-call(f32[40,128]{1,0:T(8,128)S(1)} %get-tuple-element.35.phase_ref, bf16[32,4,16,256]{3,2,1,0:T(8,128)(2,1)S(1)} %copy-done, bf16[64,256]{1,0:T(8,128)(2,1)S(1)} %get-tuple-element.41.table_ref), custom_call_target="tpu_custom_call" | custom-call | bytes 7380000 | tf_op jit(solution)/shard_map/input_modes/pallas_call | solution.py:651
  13.6 1.1 %slope.1 = (f32[2,2176,128]{2,1,0:T(8,128)S(1)}, f32[128,128]{1,0:T(8,128)S(1)}, f32[128,128]{1,0:T(8,128)S(1)}, f32[512,128]{1,0:T(8,128)S(1)}, bf16[96,256]{1,0:T(8,128)(2,1)S(1)}) custom-call(bf16[32,4,16,256]{3,2,1,0:T(8,128)(2,1)S(1)} %get-tuple-element.38.pre_ref, f32[32,128]{1,0:T(8,128)S(1)} %get-tuple-element.39.proj_ref, ...), custom_call_target="tpu_custom_call" | custom-call | bytes 7380000 | tf_op jit(solution)/shard_map/slope/pallas_call | solution.py:651
  14.8 1.3 %collective-permute-start.4 = (f32[8,64,128]{2,1,0:T(8,128)S(1)}, f32[8,64,128]{2,1,0:T(8,128)S(1)}, u32[]{:S(2)}, u32[]{:S(2)}) collective-permute-start(f32[8,64,128]{2,1,0:T(8,128)S(1)} %get-tuple-element.52), channel_id=1, source_target_pairs={{0,1},{1,0},{2,3},{3,2},{4,5},{5,4},{6,7},{7,6},{8,9},{9,8},{10,11... | collective-permute-start | bytes 786440 | tf_op jit(solution)/shard_map/ppermute | solution.py:749
  16.1 0.1 collective-permute-start.2
  16.2 1.6 %collective-permute-start.3 = (f32[32,256]{1,0:T(8,128)S(1)}, f32[32,256]{1,0:T(8,128)S(1)}, u32[]{:S(2)}, u32[]{:S(2)}) collective-permute-start(f32[32,256]{1,0:T(8,128)S(1)} %get-tuple-element.51), channel_id=1, source_target_pairs={{0,15},{1,2},{2,1},{3,4},{4,3},{5,6},{6,5},{7,8},{8,7},{9,10},{10,... | collective-permute-start | bytes 98312 | tf_op jit(solution)/shard_map/ppermute | solution.py:754
  17.9 1.7 %collective-permute-done.3.y_b_ref = f32[32,256]{1,0:T(8,128)S(1)} collective-permute-done((f32[32,256]{1,0:T(8,128)S(1)}, f32[32,256]{1,0:T(8,128)S(1)}, u32[]{:S(2)}, u32[]{:S(2)}) %collective-permute-start.3) | collective-permute-done | bytes 32800 | tf_op jit(solution)/shard_map/ppermute | solution.py:754
  19.6 1.6 %grad_modes.1 = (f32[8,64,128]{2,1,0:T(8,128)S(1)}, f32[8,64,128]{2,1,0:T(8,128)S(1)}, f32[4,32,256]{2,1,0:T(8,128)S(1)}) custom-call(f32[40,128]{1,0:T(8,128)S(1)} %get-tuple-element.35.phase_ref, f32[4,16,256]{2,1,0:T(8,128)S(1)} %get-tuple-element.45.field_ref, bf16[4,16,256]{2,1,0:T(8,128)(2,1)S(1)} %get-tuple-element.46.coef_ref, ...), custom_call_target="tpu_custom_call" | custom-call | bytes 11070000 | tf_op jit(solution)/shard_map/grad_modes/pallas_call | solution.py:651
  21.3 2.6 %collective-permute-start.5 = (f32[8,64,128]{2,1,0:T(8,128)S(1)}, f32[8,64,128]{2,1,0:T(8,128)S(1)}, u32[]{:S(2)}, u32[]{:S(2)}) collective-permute-start(f32[8,64,128]{2,1,0:T(8,128)S(1)} %get-tuple-element.58), channel_id=1, source_target_pairs={{0,1},{1,0},{2,3},{3,2},{4,5},{5,4},{6,7},{7,6},{8,9},{9,8},{10,11... | collective-permute-start | bytes 786440 | tf_op jit(solution)/shard_map/ppermute | solution.py:779
  23.9 0.6 local.1.local_ref
  24.5 0.5 collective-permute-done.5.got_ref
  25.1 14.3 %all_to_all.20.parts_ref = f32[8,128,128]{2,1,0:T(8,128)S(1)} all-to-all(f32[8,128,128]{2,1,0:T(8,128)S(1)} %combine.1), channel_id=1, replica_groups={{0,2,6,4,12,14,10,8},{1,3,7,5,13,15,11,9},{16,18,22,20,28,30,26,24},{17..., dimensions={0} | all-to-all | bytes 1048576 | tf_op jit(solution)/shard_map/all_to_all | solution.py:785
  39.4 0.2 slab_forward.1
  39.7 15.3 %all_to_all.21.parts_ref = f32[16,40,128]{2,1,0:T(8,128)S(1)} all-to-all(f32[16,40,128]{2,1,0:T(8,128)S(1)} %slab_forward.1), channel_id=1, replica_groups={{0,160,64,224,128,32,192,96,16,112,208,48,144,240,80,176},{1,161,65,225..., dimensions={0} | all-to-all | bytes 655360 | tf_op jit(solution)/shard_map/all_to_all | solution.py:792
  55.0 0.7 back.1
  55.7 16.5 %all_to_all.22.parts_ref = f32[16,40,128]{2,1,0:T(8,128)S(1)} all-to-all(f32[16,40,128]{2,1,0:T(8,128)S(1)} %get-tuple-element.63), channel_id=1, replica_groups={{0,160,64,224,128,32,192,96,16,112,208,48,144,240,80,176},{1,161,65,225..., dimensions={0} | all-to-all | bytes 655360 | tf_op jit(solution)/shard_map/all_to_all | solution.py:796
  72.2 0.2 slab_backward.1
  72.4 9.1 %all_to_all.23.own_ref = f32[8,64,128]{2,1,0:T(8,128)S(1)} all-to-all(f32[8,64,128]{2,1,0:T(8,128)S(1)} %slab_backward.1), channel_id=1, replica_groups={{0,2,6,4,12,14,10,8},{1,3,7,5,13,15,11,9},{16,18,22,20,28,30,26,24},{17..., dimensions={0} | all-to-all | bytes 524288 | tf_op jit(solution)/shard_map/all_to_all | solution.py:801
  81.4 5.5 %collective-permute-start.6 = (f32[8,64,128]{2,1,0:T(8,128)S(1)}, f32[8,64,128]{2,1,0:T(8,128)S(1)}, u32[]{:S(2)}, u32[]{:S(2)}) collective-permute-start(f32[8,64,128]{2,1,0:T(8,128)S(1)} %all_to_all.23.own_ref), channel_id=1, source_target_pairs={{0,1},{1,0},{2,3},{3,2},{4,5},{5,4},{6,7},{7,6},{8,9},{9,8},{10,11... | collective-permute-start | bytes 786440 | tf_op jit(solution)/shard_map/ppermute | solution.py:802
  86.9 1.3 %weight_grad.1 = bf16[2,2,2,32,512]{4,3,2,1,0:T(8,128)(2,1)} custom-call(f32[32,128]{1,0:T(8,128)S(1)} %get-tuple-element.67.modes_ref, f32[640,128]{1,0:T(8,128)S(1)} %bitcast.1), custom_call_target="tpu_custom_call" | custom-call | bytes 3690000 | tf_op jit(solution)/shard_map/weight_grad/pallas_call | solution.py:651
  88.2 1.9 %output.1 = bf16[32,4,16,256]{3,2,1,0:T(8,128)(2,1)} custom-call(f32[40,128]{1,0:T(8,128)S(1)} %get-tuple-element.35.phase_ref, f32[8,64,128]{2,1,0:T(8,128)S(1)} %all_to_all.23.own_ref, f32[8,64,128]{2,1,0:T(8,128)S(1)} %collective-permute-done.6.other_ref, f32[16,128,256]{2,1,0:T(8,128)S(1)} %local.1.local_ref, bf16[96,256]{1,0:T(8,128)(2,1)S(1)} %get-tuple-element.66.table_ref), custom_call_target="tpu_custom_call" | custom-call | bytes 3690000 | tf_op jit(solution)/shard_map/output/pallas_call | solution.py:651
  (12 shorter events, 0.1 us)
Async XLA Ops:
  2.2 12.5 %collective-permute-start = (f32[4,16,256]{2,1,0:T(8,128)S(1)}, f32[4,16,256]{2,1,0:T(8,128)S(1)}, u32[]{:S(2)}, u32[]{:S(2)}) collective-permute-start(f32[4,16,256]{2,1,0:T(8,128)S(1)} %get-tuple-element.36), channel_id=1, source_target_pairs={{0,16},{16,0},{32,48},{48,32},{64,80},{80,64},{96,112},{112,96},{1... | collective-permute-start | bytes 196616 | tf_op jit(solution)/shard_map/ppermute | solution.py:711
  6.1 8.7 %collective-permute-start.1 = (f32[4,16,256]{2,1,0:T(8,128)S(1)}, f32[4,16,256]{2,1,0:T(8,128)S(1)}, u32[]{:S(2)}, u32[]{:S(2)}) collective-permute-start(f32[4,16,256]{2,1,0:T(8,128)S(1)} %get-tuple-element.37), channel_id=1, source_target_pairs={{0,240},{16,32},{32,16},{48,64},{64,48},{80,96},{96,80},{112,128},... | collective-permute-start | bytes 196616 | tf_op jit(solution)/shard_map/ppermute | solution.py:712
  11.5 1.2 %copy-start = (bf16[32,4,16,256]{3,2,1,0:T(8,128)(2,1)S(1)}, bf16[32,4,16,256]{3,2,1,0:T(8,128)(2,1)}, u32[]{:S(2)}) copy-start(bf16[32,4,16,256]{3,2,1,0:T(8,128)(2,1)} %input_ref.1) | copy-start | bytes 3145732
  14.7 9.1 %copy-start.2 = (bf16[32,32]{1,0:T(8,128)(2,1)S(1)}, bf16[32,32]{1,0:T(8,128)(2,1)}, u32[]{:S(2)}) copy-start(bf16[32,32]{1,0:T(8,128)(2,1)} %pointwise_ref.1) | copy-start | bytes 6148
  14.8 4.9 %collective-permute-start.4 = (f32[8,64,128]{2,1,0:T(8,128)S(1)}, f32[8,64,128]{2,1,0:T(8,128)S(1)}, u32[]{:S(2)}, u32[]{:S(2)}) collective-permute-start(f32[8,64,128]{2,1,0:T(8,128)S(1)} %get-tuple-element.52), channel_id=1, source_target_pairs={{0,1},{1,0},{2,3},{3,2},{4,5},{5,4},{6,7},{7,6},{8,9},{9,8},{10,11... | collective-permute-start | bytes 786440 | tf_op jit(solution)/shard_map/ppermute | solution.py:749
  16.1 1.8 %collective-permute-start.2 = (f32[32,256]{1,0:T(8,128)S(1)}, f32[32,256]{1,0:T(8,128)S(1)}, u32[]{:S(2)}, u32[]{:S(2)}) collective-permute-start(f32[32,256]{1,0:T(8,128)S(1)} %get-tuple-element.50), channel_id=1, source_target_pairs={{0,1},{1,0},{2,3},{3,2},{4,5},{5,4},{6,7},{7,6},{8,9},{9,8},{10,11... | collective-permute-start | bytes 98312 | tf_op jit(solution)/shard_map/ppermute | solution.py:753
  16.2 3.4 %collective-permute-start.3 = (f32[32,256]{1,0:T(8,128)S(1)}, f32[32,256]{1,0:T(8,128)S(1)}, u32[]{:S(2)}, u32[]{:S(2)}) collective-permute-start(f32[32,256]{1,0:T(8,128)S(1)} %get-tuple-element.51), channel_id=1, source_target_pairs={{0,15},{1,2},{2,1},{3,4},{4,3},{5,6},{6,5},{7,8},{8,7},{9,10},{10,... | collective-permute-start | bytes 98312 | tf_op jit(solution)/shard_map/ppermute | solution.py:754
  21.3 3.8 %collective-permute-start.5 = (f32[8,64,128]{2,1,0:T(8,128)S(1)}, f32[8,64,128]{2,1,0:T(8,128)S(1)}, u32[]{:S(2)}, u32[]{:S(2)}) collective-permute-start(f32[8,64,128]{2,1,0:T(8,128)S(1)} %get-tuple-element.58), channel_id=1, source_target_pairs={{0,1},{1,0},{2,3},{3,2},{4,5},{5,4},{6,7},{7,6},{8,9},{9,8},{10,11... | collective-permute-start | bytes 786440 | tf_op jit(solution)/shard_map/ppermute | solution.py:779
  24.5 30.5 %copy-start.1 = (bf16[2,2,2,32,512]{4,3,2,1,0:T(8,128)(2,1)S(1)}, bf16[2,2,2,32,512]{4,3,2,1,0:T(8,128)(2,1)}, u32[]{:S(2)}) copy-start(bf16[2,2,2,32,512]{4,3,2,1,0:T(8,128)(2,1)} %weight_ref.1) | copy-start | bytes 786436
  81.4 6.8 %collective-permute-start.6 = (f32[8,64,128]{2,1,0:T(8,128)S(1)}, f32[8,64,128]{2,1,0:T(8,128)S(1)}, u32[]{:S(2)}, u32[]{:S(2)}) collective-permute-start(f32[8,64,128]{2,1,0:T(8,128)S(1)} %all_to_all.23.own_ref), channel_id=1, source_target_pairs={{0,1},{1,0},{2,3},{3,2},{4,5},{5,4},{6,7},{7,6},{8,9},{9,8},{10,11... | collective-permute-start | bytes 786440 | tf_op jit(solution)/shard_map/ppermute | solution.py:802

commit v9 on v7

--- a/solution.py
+++ b/solution.py
@@ -749,16 +749,13 @@
         ],
         us=2,
     )(phases, layer_input, depth_forward)
-    x_a, x_b, slope, own_in, other_in = lax.optimization_barrier(
-        (x_a, x_b, slope, own_in, other_in)
-    )
     got_in = lax.ppermute(other_in, "pencil", swap)
+    x_a, x_b, slope, own_in, got_in = lax.optimization_barrier((x_a, x_b, slope, own_in, got_in))
     side_a, side_b = call(pack_kernel, "pack", [((32, NZ), F32), ((32, NZ), F32)])(
         field, coefficient, source, x_a, x_b
     )
     y_a = lax.ppermute(side_a, "pencil", swap)
     y_b = lax.ppermute(side_b, "pencil", swap_odd)
-    y_a, y_b, got_in = lax.optimization_barrier((y_a, y_b, got_in))
     own, other, grad = call(
         grad_kernel,
         "grad_modes",

time: 90.5 us -> 91.4 us (level)
  waiting for transfers between devices: 2.28 us -> 3.63 us
    ppermute x1, starting transfers between devices: 3.83 us -> 1.2 us  [shards(): x_a = lax.ppermute(edge_a, 'slab', swap)]
    ppermute x1, starting transfers between devices: 1.37 us -> 3.33 us  [shards(): got_in = lax.ppermute(other_in, 'pencil', swap)]
    ppermute x1, waiting for transfers between devices: 0.01 us -> 1.04 us  [shards(): x_b = lax.ppermute(edge_b, 'slab', swap_odd)]
  transfers between devices with their start and end apart: 7 -> 7, of which waited for: 2 -> 3; matrix products, arithmetic and copies ran while one was open for 0% -> 0% of each run, Pallas kernels for 4% -> 3%
where the time goes in v9:
time: 91.4 us; the launch traced here: 91.1 us
  blocking collectives  56.5 us (62%)
  starting transfers between devices  19.9 us (22%)
  Pallas kernels  10.4 us (11%)
  waiting for transfers between devices  3.63 us (4%)
    all_to_all x2, blocking collectives, shards(): lax.all_to_all(to_slab, 'slab', 0, 0, axis_index_groups=all_slabs, tiled=...  32.8 us
    all_to_all x2, blocking collectives, shards(): lax.all_to_all(to_pencil, 'pencil', 0, 0, axis_index_groups=same_core, ti...  23.7 us
    pallas_call x12, Pallas kernels, run(): pl.pallas_call(kernel, out_shape=shapes, in_specs=specs, out_specs=[pl.Bl...  10.4 us
    ppermute x1, starting transfers between devices, shards(): other = lax.ppermute(own, 'pencil', swap)  5.46 us
    ppermute x1, starting transfers between devices, shards(): x_b = lax.ppermute(edge_b, 'slab', swap_odd)  5.35 us
    ppermute x1, starting transfers between devices, shards(): got_in = lax.ppermute(other_in, 'pencil', swap)  3.33 us
    ppermute x1, starting transfers between devices, shards(): got = lax.ppermute(other, 'pencil', swap)  2.3 us
    ppermute x1, waiting for transfers between devices, shards(): y_b = lax.ppermute(side_b, 'pencil', swap_odd)  2.06 us
  transfers between devices with their start and end apart: 7, of which 3 were waited for; matrix products, arithmetic and copies ran while one was open for 0% of the time, Pallas kernels for 3%

profile of v9, /device:TPU:1, one launch (start us, length us, event | category | flops | bytes accessed | tf_op | source)
XLA Modules:
  0.0 91.1 jit_solution(3850079492225735167)
XLA Ops:
  0.6 1.7 %field.1 = (f32[4,16,256]{2,1,0:T(8,128)S(1)}, f32[4,16,256]{2,1,0:T(8,128)S(1)}, f32[4,16,256]{2,1,0:T(8,128)S(1)}, bf16[32,4,16,256]{3,2,1,0:T(8,128)(2,1)S(1)...) custom-call(bf16[32,4,16,256]{3,2,1,0:T(8,128)(2,1)} %pre_hbm.1, ...), custom_call_target="tpu_custom_call" | custom-call | bytes 14760000 | tf_op jit(solution)/shard_map/field/pallas_call | solution.py:654
  2.3 0.9 %input_modes.1 = (f32[8,64,128]{2,1,0:T(8,128)S(1)}, f32[8,64,128]{2,1,0:T(8,128)S(1)}) custom-call(f32[40,128]{1,0:T(8,128)S(1)} %get-tuple-element.33.phase_ref, bf16[32,4,16,256]{3,2,1,0:T(8,128)(2,1)S(1)} %get-tuple-element.39.input_ref, bf16[64,256]{1,0:T(8,128)(2,1)S(1)} %get-tuple-element.40.table_ref), custom_call_target="tpu_custom_call" | custom-call | bytes 7380000 | tf_op jit(solution)/shard_map/input_modes/pallas_call | solution.py:654
  3.3 3.3 %collective-permute-start.2 = (f32[8,64,128]{2,1,0:T(8,128)S(1)}, f32[8,64,128]{2,1,0:T(8,128)S(1)}, u32[]{:S(2)}, u32[]{:S(2)}) collective-permute-start(f32[8,64,128]{2,1,0:T(8,128)S(1)} %get-tuple-element.42), channel_id=1, source_target_pairs={{0,1},{1,0},{2,3},{3,2},{4,5},{5,4},{6,7},{7,6},{8,9},{9,8},{10,11... | collective-permute-start | bytes 786440 | tf_op jit(solution)/shard_map/ppermute | solution.py:752
  6.6 1.2 %collective-permute-start = (f32[4,16,256]{2,1,0:T(8,128)S(1)}, f32[4,16,256]{2,1,0:T(8,128)S(1)}, u32[]{:S(2)}, u32[]{:S(2)}) collective-permute-start(f32[4,16,256]{2,1,0:T(8,128)S(1)} %get-tuple-element.34), channel_id=1, source_target_pairs={{0,16},{16,0},{32,48},{48,32},{64,80},{80,64},{96,112},{112,96},{1... | collective-permute-start | bytes 196616 | tf_op jit(solution)/shard_map/ppermute | solution.py:717
  7.8 5.3 %collective-permute-start.1 = (f32[4,16,256]{2,1,0:T(8,128)S(1)}, f32[4,16,256]{2,1,0:T(8,128)S(1)}, u32[]{:S(2)}, u32[]{:S(2)}) collective-permute-start(f32[4,16,256]{2,1,0:T(8,128)S(1)} %get-tuple-element.35), channel_id=1, source_target_pairs={{0,240},{16,32},{32,16},{48,64},{64,48},{80,96},{96,80},{112,128},... | collective-permute-start | bytes 196616 | tf_op jit(solution)/shard_map/ppermute | solution.py:718
  13.1 1.1 %slope.1 = (f32[2,2176,128]{2,1,0:T(8,128)S(1)}, f32[128,128]{1,0:T(8,128)S(1)}, f32[128,128]{1,0:T(8,128)S(1)}, f32[512,128]{1,0:T(8,128)S(1)}, bf16[96,256]{1,0:T(8,128)(2,1)S(1)}) custom-call(bf16[32,4,16,256]{3,2,1,0:T(8,128)(2,1)S(1)} %get-tuple-element.36.pre_ref, f32[32,128]{1,0:T(8,128)S(1)} %get-tuple-element.37.proj_ref, ...), custom_call_target="tpu_custom_call" | custom-call | bytes 7380000 | tf_op jit(solution)/shard_map/slope/pallas_call | solution.py:654
  14.3 1.0 %collective-permute-done.1.got_b_ref.x_b_ref = f32[4,16,256]{2,1,0:T(8,128)S(1)} collective-permute-done((f32[4,16,256]{2,1,0:T(8,128)S(1)}, f32[4,16,256]{2,1,0:T(8,128)S(1)}, u32[]{:S(2)}, u32[]{:S(2)}) %collective-permute-start.1) | collective-permute-done | bytes 65568 | tf_op jit(solution)/shard_map/ppermute | solution.py:718
  15.3 1.0 %collective-permute-start.3 = (f32[32,256]{1,0:T(8,128)S(1)}, f32[32,256]{1,0:T(8,128)S(1)}, u32[]{:S(2)}, u32[]{:S(2)}) collective-permute-start(f32[32,256]{1,0:T(8,128)S(1)} %get-tuple-element.50), channel_id=1, source_target_pairs={{0,1},{1,0},{2,3},{3,2},{4,5},{5,4},{6,7},{7,6},{8,9},{9,8},{10,11... | collective-permute-start | bytes 98312 | tf_op jit(solution)/shard_map/ppermute | solution.py:757
  16.3 1.3 %collective-permute-start.4 = (f32[32,256]{1,0:T(8,128)S(1)}, f32[32,256]{1,0:T(8,128)S(1)}, u32[]{:S(2)}, u32[]{:S(2)}) collective-permute-start(f32[32,256]{1,0:T(8,128)S(1)} %get-tuple-element.51), channel_id=1, source_target_pairs={{0,15},{1,2},{2,1},{3,4},{4,3},{5,6},{6,5},{7,8},{8,7},{9,10},{10,... | collective-permute-start | bytes 98312 | tf_op jit(solution)/shard_map/ppermute | solution.py:758
  17.6 2.1 %collective-permute-done.4.y_b_ref = f32[32,256]{1,0:T(8,128)S(1)} collective-permute-done((f32[32,256]{1,0:T(8,128)S(1)}, f32[32,256]{1,0:T(8,128)S(1)}, u32[]{:S(2)}, u32[]{:S(2)}) %collective-permute-start.4) | collective-permute-done | bytes 32800 | tf_op jit(solution)/shard_map/ppermute | solution.py:758
  19.7 1.6 %grad_modes.1 = (f32[8,64,128]{2,1,0:T(8,128)S(1)}, f32[8,64,128]{2,1,0:T(8,128)S(1)}, f32[4,32,256]{2,1,0:T(8,128)S(1)}) custom-call(f32[40,128]{1,0:T(8,128)S(1)} %get-tuple-element.33.phase_ref, f32[4,16,256]{2,1,0:T(8,128)S(1)} %get-tuple-element.45.field_ref, bf16[4,16,256]{2,1,0:T(8,128)(2,1)S(1)} %get-tuple-element.46.coef_ref, ...), custom_call_target="tpu_custom_call" | custom-call | bytes 11070000 | tf_op jit(solution)/shard_map/grad_modes/pallas_call | solution.py:654
  21.3 2.3 %collective-permute-start.5 = (f32[8,64,128]{2,1,0:T(8,128)S(1)}, f32[8,64,128]{2,1,0:T(8,128)S(1)}, u32[]{:S(2)}, u32[]{:S(2)}) collective-permute-start(f32[8,64,128]{2,1,0:T(8,128)S(1)} %get-tuple-element.54), channel_id=1, source_target_pairs={{0,1},{1,0},{2,3},{3,2},{4,5},{5,4},{6,7},{7,6},{8,9},{9,8},{10,11... | collective-permute-start | bytes 786440 | tf_op jit(solution)/shard_map/ppermute | solution.py:782
  23.6 0.6 local.1.local_ref
  24.2 0.5 collective-permute-done.5.got_ref
  24.8 14.6 %all_to_all.20.parts_ref = f32[8,128,128]{2,1,0:T(8,128)S(1)} all-to-all(f32[8,128,128]{2,1,0:T(8,128)S(1)} %combine.1), channel_id=1, replica_groups={{0,2,6,4,12,14,10,8},{1,3,7,5,13,15,11,9},{16,18,22,20,28,30,26,24},{17..., dimensions={0} | all-to-all | bytes 1048576 | tf_op jit(solution)/shard_map/all_to_all | solution.py:788
  39.4 0.2 slab_forward.1
  39.7 16.3 %all_to_all.21.parts_ref = f32[16,40,128]{2,1,0:T(8,128)S(1)} all-to-all(f32[16,40,128]{2,1,0:T(8,128)S(1)} %slab_forward.1), channel_id=1, replica_groups={{0,160,64,224,128,32,192,96,16,112,208,48,144,240,80,176},{1,161,65,225..., dimensions={0} | all-to-all | bytes 655360 | tf_op jit(solution)/shard_map/all_to_all | solution.py:795
  56.0 0.7 back.1
  56.7 16.5 %all_to_all.22.parts_ref = f32[16,40,128]{2,1,0:T(8,128)S(1)} all-to-all(f32[16,40,128]{2,1,0:T(8,128)S(1)} %get-tuple-element.59), channel_id=1, replica_groups={{0,160,64,224,128,32,192,96,16,112,208,48,144,240,80,176},{1,161,65,225..., dimensions={0} | all-to-all | bytes 655360 | tf_op jit(solution)/shard_map/all_to_all | solution.py:799
  73.2 0.2 slab_backward.1
  73.4 9.1 %all_to_all.23.own_ref = f32[8,64,128]{2,1,0:T(8,128)S(1)} all-to-all(f32[8,64,128]{2,1,0:T(8,128)S(1)} %slab_backward.1), channel_id=1, replica_groups={{0,2,6,4,12,14,10,8},{1,3,7,5,13,15,11,9},{16,18,22,20,28,30,26,24},{17..., dimensions={0} | all-to-all | bytes 524288 | tf_op jit(solution)/shard_map/all_to_all | solution.py:804
  82.4 5.5 %collective-permute-start.6 = (f32[8,64,128]{2,1,0:T(8,128)S(1)}, f32[8,64,128]{2,1,0:T(8,128)S(1)}, u32[]{:S(2)}, u32[]{:S(2)}) collective-permute-start(f32[8,64,128]{2,1,0:T(8,128)S(1)} %all_to_all.23.own_ref), channel_id=1, source_target_pairs={{0,1},{1,0},{2,3},{3,2},{4,5},{5,4},{6,7},{7,6},{8,9},{9,8},{10,11... | collective-permute-start | bytes 786440 | tf_op jit(solution)/shard_map/ppermute | solution.py:805
  87.9 1.3 %weight_grad.1 = bf16[2,2,2,32,512]{4,3,2,1,0:T(8,128)(2,1)} custom-call(f32[32,128]{1,0:T(8,128)S(1)} %get-tuple-element.63.modes_ref, f32[640,128]{1,0:T(8,128)S(1)} %bitcast.1), custom_call_target="tpu_custom_call" | custom-call | bytes 3690000 | tf_op jit(solution)/shard_map/weight_grad/pallas_call | solution.py:654
  89.2 1.9 %output.1 = bf16[32,4,16,256]{3,2,1,0:T(8,128)(2,1)} custom-call(f32[40,128]{1,0:T(8,128)S(1)} %get-tuple-element.33.phase_ref, f32[8,64,128]{2,1,0:T(8,128)S(1)} %all_to_all.23.own_ref, f32[8,64,128]{2,1,0:T(8,128)S(1)} %collective-permute-done.6.other_ref, f32[16,128,256]{2,1,0:T(8,128)S(1)} %local.1.local_ref, bf16[96,256]{1,0:T(8,128)(2,1)S(1)} %get-tuple-element.62.table_ref), custom_call_target="tpu_custom_call" | custom-call | bytes 3690000 | tf_op jit(solution)/shard_map/output/pallas_call | solution.py:654
  (10 shorter events, 0.1 us)
Async XLA Ops:
  3.3 12.0 %collective-permute-start.2 = (f32[8,64,128]{2,1,0:T(8,128)S(1)}, f32[8,64,128]{2,1,0:T(8,128)S(1)}, u32[]{:S(2)}, u32[]{:S(2)}) collective-permute-start(f32[8,64,128]{2,1,0:T(8,128)S(1)} %get-tuple-element.42), channel_id=1, source_target_pairs={{0,1},{1,0},{2,3},{3,2},{4,5},{5,4},{6,7},{7,6},{8,9},{9,8},{10,11... | collective-permute-start | bytes 786440 | tf_op jit(solution)/shard_map/ppermute | solution.py:752
  6.6 7.7 %collective-permute-start = (f32[4,16,256]{2,1,0:T(8,128)S(1)}, f32[4,16,256]{2,1,0:T(8,128)S(1)}, u32[]{:S(2)}, u32[]{:S(2)}) collective-permute-start(f32[4,16,256]{2,1,0:T(8,128)S(1)} %get-tuple-element.34), channel_id=1, source_target_pairs={{0,16},{16,0},{32,48},{48,32},{64,80},{80,64},{96,112},{112,96},{1... | collective-permute-start | bytes 196616 | tf_op jit(solution)/shard_map/ppermute | solution.py:717
  7.8 7.5 %collective-permute-start.1 = (f32[4,16,256]{2,1,0:T(8,128)S(1)}, f32[4,16,256]{2,1,0:T(8,128)S(1)}, u32[]{:S(2)}, u32[]{:S(2)}) collective-permute-start(f32[4,16,256]{2,1,0:T(8,128)S(1)} %get-tuple-element.35), channel_id=1, source_target_pairs={{0,240},{16,32},{32,16},{48,64},{64,48},{80,96},{96,80},{112,128},... | collective-permute-start | bytes 196616 | tf_op jit(solution)/shard_map/ppermute | solution.py:718
  14.2 9.3 %copy-start.1 = (bf16[32,32]{1,0:T(8,128)(2,1)S(1)}, bf16[32,32]{1,0:T(8,128)(2,1)}, u32[]{:S(2)}) copy-start(bf16[32,32]{1,0:T(8,128)(2,1)} %pointwise_ref.1) | copy-start | bytes 6148
  15.3 2.3 %collective-permute-start.3 = (f32[32,256]{1,0:T(8,128)S(1)}, f32[32,256]{1,0:T(8,128)S(1)}, u32[]{:S(2)}, u32[]{:S(2)}) collective-permute-start(f32[32,256]{1,0:T(8,128)S(1)} %get-tuple-element.50), channel_id=1, source_target_pairs={{0,1},{1,0},{2,3},{3,2},{4,5},{5,4},{6,7},{7,6},{8,9},{9,8},{10,11... | collective-permute-start | bytes 98312 | tf_op jit(solution)/shard_map/ppermute | solution.py:757
  16.3 3.3 %collective-permute-start.4 = (f32[32,256]{1,0:T(8,128)S(1)}, f32[32,256]{1,0:T(8,128)S(1)}, u32[]{:S(2)}, u32[]{:S(2)}) collective-permute-start(f32[32,256]{1,0:T(8,128)S(1)} %get-tuple-element.51), channel_id=1, source_target_pairs={{0,15},{1,2},{2,1},{3,4},{4,3},{5,6},{6,5},{7,8},{8,7},{9,10},{10,... | collective-permute-start | bytes 98312 | tf_op jit(solution)/shard_map/ppermute | solution.py:758
  21.3 3.5 %collective-permute-start.5 = (f32[8,64,128]{2,1,0:T(8,128)S(1)}, f32[8,64,128]{2,1,0:T(8,128)S(1)}, u32[]{:S(2)}, u32[]{:S(2)}) collective-permute-start(f32[8,64,128]{2,1,0:T(8,128)S(1)} %get-tuple-element.54), channel_id=1, source_target_pairs={{0,1},{1,0},{2,3},{3,2},{4,5},{5,4},{6,7},{7,6},{8,9},{9,8},{10,11... | collective-permute-start | bytes 786440 | tf_op jit(solution)/shard_map/ppermute | solution.py:782
  24.2 31.8 %copy-start = (bf16[2,2,2,32,512]{4,3,2,1,0:T(8,128)(2,1)S(1)}, bf16[2,2,2,32,512]{4,3,2,1,0:T(8,128)(2,1)}, u32[]{:S(2)}) copy-start(bf16[2,2,2,32,512]{4,3,2,1,0:T(8,128)(2,1)} %weight_ref.1) | copy-start | bytes 786436
  82.4 6.8 %collective-permute-start.6 = (f32[8,64,128]{2,1,0:T(8,128)S(1)}, f32[8,64,128]{2,1,0:T(8,128)S(1)}, u32[]{:S(2)}, u32[]{:S(2)}) collective-permute-start(f32[8,64,128]{2,1,0:T(8,128)S(1)} %all_to_all.23.own_ref), channel_id=1, source_target_pairs={{0,1},{1,0},{2,3},{3,2},{4,5},{5,4},{6,7},{7,6},{8,9},{9,8},{10,11... | collective-permute-start | bytes 786440 | tf_op jit(solution)/shard_map/ppermute | solution.py:805
